TPU v7x, 256 devices: a whole 4x4x8 slice. The times are simulated.
256 devices in a mesh: ctx: 64 (over z, x, core), seq: 4 (over y).
Axes of the slice: x: 4, y: 4, z: 8, core: 2. Of those that a mesh axis runs over, the one named last changes fastest.
Arguments:
- x_loader: bfloat16 [32768, 4096], P(('seq', 'ctx')), parts along dimension 0, may hold values from -6 to 6
- b_loader: bfloat16 [32768, 512], P(('seq', 'ctx')), parts along dimension 0, may hold values from -0.75 to 0.75
- c_loader: bfloat16 [32768, 512], P(('seq', 'ctx')), parts along dimension 0, may hold values from -0.75 to 0.75
- dt_loader: bfloat16 [32768, 64], P(('seq', 'ctx')), parts along dimension 0, may hold values from -5 to 5
- local_order: int32 [256, 128], P(('seq', 'ctx')), parts along dimension 0, may hold values from 0 to 127, each once within a row
- resets: int32 [32768], P(('seq', 'ctx')), parts along dimension 0, may hold values 0 or 1
- decay_rate: float32 [64], replicated, may hold values from 0 to 1, as said below
- skip_gain: float32 [64], replicated, may hold values from 0.5 to 1.5
Outputs:
- layer_out: bfloat16 [32768, 4096], P(('seq', 'ctx')), parts along dimension 0
There are 4 independent parts, one for each index of `seq`. A program takes and returns all parts, laid end to end along the dimension named above; an argument that names none is the same for every part. Nothing has to cross between parts.
Inputs may be any that keep to these rules, and one draw needn't show every extreme that they name: Each row of local_order is a permutation of 0 to 127. `decay_rate`: positive rates.
All inputs are finite; a program needn't handle non-finite values. No bound on the sum of `resets` on one device may be relied on, other than what follows from the above.
Results may differ from a plain program's by a relative error of at most 0.0056.
Values may be sent and summed in bfloat16 or wider, within the bound.
No kernel may reach another device: no remote copies, remote signals or barrier semaphores. Data moves between devices by JAX's collectives and lax.ppermute only.
A program may use at most 192 MiB of HBM per device.

v0:
```python
import jax
import jax.numpy as jnp
from jax import lax
from jax.sharding import PartitionSpec as P

H = 64
P_SIZE = 64
N = 64
G = 8
SPAN = 128


def prefix(part, axis, combine, identity):
    place = lax.axis_index(axis)
    gathered = jax.tree.map(lambda a: lax.all_gather(a, axis), part)
    state = jax.tree.map(lambda a, e: jnp.zeros_like(a) + jnp.asarray(e, a.dtype), part, identity)

    def one(lap, state):
        return combine(
            state, jax.tree.map(lambda a: lax.dynamic_index_in_dim(a, lap, 0, False), gathered)
        )

    return lax.fori_loop(0, place, one, state)


def combine(earlier, following):
    first_decay, first_state = earlier
    second_decay, second_state = following
    spread = second_decay.reshape(
        second_decay.shape + (1,) * (first_state.ndim - second_decay.ndim)
    )
    return (first_decay * second_decay, spread * first_state + second_state)


def per_device(x_loader, b_loader, c_loader, dt_loader, local_order, resets, decay_rate, skip_gain):
    n_ctx = lax.axis_size("ctx")
    dev_rows = x_loader.shape[0]
    slab_rows = dev_rows // n_ctx
    per_group = H // G
    spans = dev_rows // SPAN

    def to_owner(source_block):
        return source_block.reshape((n_ctx, slab_rows) + source_block.shape[1:])

    arrived = (
        lax.all_to_all(to_owner(x_loader), "ctx", split_axis=0, concat_axis=0, tiled=True),
        lax.all_to_all(to_owner(b_loader), "ctx", split_axis=0, concat_axis=0, tiled=True),
        lax.all_to_all(to_owner(c_loader), "ctx", split_axis=0, concat_axis=0, tiled=True),
        lax.all_to_all(to_owner(dt_loader), "ctx", split_axis=0, concat_axis=0, tiled=True),
    )
    ordering = local_order[0]
    x_rows, b_rows, c_rows, dt_rows = [
        jnp.take(portion.reshape((dev_rows,) + portion.shape[2:]), ordering, axis=0)
        for portion in arrived
    ]
    x_span = x_rows.reshape(spans, SPAN, H, P_SIZE)
    b_span = b_rows.reshape(spans, SPAN, G, N)
    c_span = c_rows.reshape(spans, SPAN, G, N)
    step_size = jax.nn.softplus(dt_rows.astype(jnp.float32)).reshape(spans, SPAN, H)
    cumulate = jnp.cumsum(-step_size * decay_rate, axis=1)
    boundary = jnp.cumsum(resets.reshape(spans, SPAN), axis=1)
    position = jnp.arange(SPAN)
    causal = position[:, None] >= position[None, :]
    keep_mask = causal[None] & (boundary[:, :, None] == boundary[:, None, :])
    x_group = x_span.reshape(spans, SPAN, G, per_group, P_SIZE)

    def group_work(group_index):
        x_here = lax.dynamic_index_in_dim(x_group, group_index, 2, keepdims=False)
        b_here = lax.dynamic_index_in_dim(b_span, group_index, 2, keepdims=False)
        c_here = lax.dynamic_index_in_dim(c_span, group_index, 2, keepdims=False)
        cum_here = lax.dynamic_slice_in_dim(cumulate, group_index * per_group, per_group, 2)
        step_here = lax.dynamic_slice_in_dim(step_size, group_index * per_group, per_group, 2)
        scores = jnp.einsum("ctn,csn->cts", c_here, b_here, preferred_element_type=jnp.float32)
        cum_heads = jnp.swapaxes(cum_here, 1, 2)
        gap = cum_heads[:, :, :, None] - cum_heads[:, :, None, :]
        decay = jnp.exp(jnp.where(keep_mask[:, None], gap, -jnp.inf))
        weights = (scores[:, None] * decay * jnp.swapaxes(step_here, 1, 2)[:, :, None, :]).astype(
            jnp.bfloat16
        )
        return jnp.einsum("cjts,csjp->ctjp", weights, x_here, preferred_element_type=jnp.float32)

    local_out = lax.map(group_work, jnp.arange(G))
    local_out = jnp.moveaxis(local_out, 0, 2).reshape(spans, SPAN, H, P_SIZE)
    tail = cumulate[:, -1:, :] - cumulate
    weight_in = (
        jnp.exp(tail) * step_size * (boundary[:, -1:] == boundary).astype(jnp.float32)[:, :, None]
    )
    x_weighted = (x_span * weight_in[..., None]).astype(jnp.bfloat16)
    span_state = jnp.einsum(
        "csgjp,csgn->cgjpn",
        x_weighted.reshape(spans, SPAN, G, per_group, P_SIZE),
        b_span,
        preferred_element_type=jnp.float32,
    ).reshape(spans, H, P_SIZE, N)
    span_decay = jnp.exp(cumulate[:, -1, :]) * (boundary[:, -1] == 0).astype(jnp.float32)[:, None]
    block_decay = jnp.ones((H,), jnp.float32)
    block_state = jnp.zeros((H, P_SIZE, N), jnp.float32)
    number = 0
    block_decay, block_state = combine(
        (block_decay, block_state), (span_decay[number], span_state[number])
    )
    identity = (jnp.ones((H,), jnp.float32), jnp.zeros((H, P_SIZE * N), jnp.float32))
    flat_state = block_state.reshape(H, P_SIZE * N)
    incoming = prefix((block_decay, flat_state), "ctx", combine, identity)[1].reshape(H, P_SIZE, N)
    entry_decay = jnp.exp(cumulate) * (boundary == 0).astype(jnp.float32)[:, :, None]
    number = 0
    rounded = incoming.astype(jnp.bfloat16).reshape(G, per_group, P_SIZE, N)
    inter = jnp.einsum(
        "tgn,gjpn->tgjp", c_span[number], rounded, preferred_element_type=jnp.float32
    ).reshape(SPAN, H, P_SIZE)
    total = (
        local_out[number]
        + inter * entry_decay[number][:, :, None]
        + skip_gain[None, :, None] * x_span[number].astype(jnp.float32)
    )
    outputs = total.astype(jnp.bfloat16).reshape(SPAN, H * P_SIZE)
    return outputs


def solution(mesh):
    in_specs = (
        P(("seq", "ctx"), None),
        P(("seq", "ctx"), None),
        P(("seq", "ctx"), None),
        P(("seq", "ctx"), None),
        P(("seq", "ctx"), None),
        P(("seq", "ctx")),
        P(),
        P(),
    )
    out_specs = P(("seq", "ctx"), None)
    return jax.shard_map(
        per_device, mesh=mesh, in_specs=in_specs, out_specs=out_specs, check_vma=False
    )
```

profile of v0, /device:TPU:231, one launch (start us, length us, event | category | flops | bytes accessed | tf_op | source)
XLA Modules:
  0.0 486.4 jit_solution(2003862161757766460)
XLA Ops:
  8.0 9.4 %all-to-all-start.3 = ((bf16[64,2,64]{2,1,0:T(2,128)(2,1)}), bf16[64,2,64]{2,1,0:T(2,128)(2,1)S(1)}, u32[]{:S(2)}, u32[]{:S(2)}) async-start(bf16[64,2,64]{2,1,0:T(2,128)(2,1)} %bitcast.8), calls=%async_computation.3 | async-start | bytes 65536 | tf_op jit(solution)/shard_map/all_to_all | solution.py:49
  17.4 1.6 reshape.545
  19.0 3.7 all-to-all-done.3
  22.6 8.9 %all-to-all-start.2 = ((bf16[64,2,512]{2,1,0:T(2,128)(2,1)}), bf16[64,2,512]{2,1,0:T(2,128)(2,1)S(1)}, u32[]{:S(2)}, u32[]{:S(2)}) async-start(bf16[64,2,512]{2,1,0:T(2,128)(2,1)} %reshape.545), calls=%async_computation.2 | async-start | bytes 262144 | tf_op jit(solution)/shard_map/all_to_all | solution.py:47
  31.6 1.6 reshape.542
  33.2 5.6 %all-to-all-done.2 = bf16[64,2,512]{2,1,0:T(2,128)(2,1)S(1)} async-done(((bf16[64,2,512]{2,1,0:T(2,128)(2,1)}), bf16[64,2,512]{2,1,0:T(2,128)(2,1)S(1)}, u32[]{:S(2)}, u32[]{:S(2)}) %all-to-all-start.2) | async-done | bytes 131104 | tf_op jit(solution)/shard_map/all_to_all | solution.py:47
  38.8 8.6 %all-to-all-start.1 = ((bf16[64,2,512]{2,1,0:T(2,128)(2,1)}), bf16[64,2,512]{2,1,0:T(2,128)(2,1)S(1)}, u32[]{:S(2)}, u32[]{:S(2)}) async-start(bf16[64,2,512]{2,1,0:T(2,128)(2,1)} %reshape.542), calls=%async_computation.1 | async-start | bytes 262144 | tf_op jit(solution)/shard_map/all_to_all | solution.py:48
  47.4 2.5 reshape.540
  49.9 4.6 all-to-all-done.1
  54.5 8.6 %all-to-all-start = ((bf16[64,2,4096]{2,1,0:T(2,128)(2,1)}), bf16[64,2,4096]{2,1,0:T(2,128)(2,1)S(1)}, u32[]{:S(2)}, u32[]{:S(2)}) async-start(bf16[64,2,4096]{2,1,0:T(2,128)(2,1)} %reshape.540), calls=%async_computation | async-start | bytes 2097152 | tf_op jit(solution)/shard_map/all_to_all | solution.py:46
  70.8 17.5 %all-to-all-done = bf16[64,2,4096]{2,1,0:T(2,128)(2,1)S(1)} async-done(((bf16[64,2,4096]{2,1,0:T(2,128)(2,1)}), bf16[64,2,4096]{2,1,0:T(2,128)(2,1)S(1)}, u32[]{:S(2)}, u32[]{:S(2)}) %all-to-all-start) | async-done | bytes 1048608 | tf_op jit(solution)/shard_map/all_to_all | solution.py:46
  90.7 1.8 fusion.21
  92.5 2.1 squeeze_reshape.11
  97.3 1.5 mul.189
  98.9 2.9 copy.49
  101.8 41.8 %all-gather = f32[64,1,64]{2,1,0:T(1,128)} all-gather(f32[1,1,64]{2,1,0:T(1,128)S(1)} %copy-done.5), channel_id=2, replica_groups=mesh['ctx'=64,'seq'=4] {'ctx'}, dimensions={0}, use_global_device_ids=true | all-gather | bytes 16640 | tf_op jit(solution)/shard_map/all_gather | solution.py:15
  144.4 45.6 %while.24 = (s32[]{:T(128)}, f32[8,1,128,8,64]{2,4,3,1,0:T(8,128)}, s32[8]{0:T(128)S(1)}, bf16[1,128,8,8,64]{1,4,3,2,0:T(8,128)(2,1)S(1)}, bf16[1,128,8,64]{1,3,...) while((s32[]{:T(128)}, f32[8,1,128,8,64]{2,4,3,1,0:T(8,128)}, ...), condition=%wide.region_3.5_spmd.clone, body=%wide.region_2.4_spmd.clone.sunk | while | flops 19578888 | bytes 620269 | solution.py:82
  190.0 3.0 copy.50
  193.0 136.2 %all-gather.3.cloned.1.call-done = f32[64,64,4096]{2,1,0:T(8,128)} async-done(((f32[1,64,4096]{2,1,0:T(8,128)}), f32[64,64,4096]{2,1,0:T(8,128)}) %all-gather.3.cloned.1.call-update) | async-done | bytes 67108880 | tf_op jit(solution)/shard_map/all_gather | solution.py:15
  329.2 140.1 %while.23 = (s32[]{:T(128)}, f32[64,4096]{1,0:T(8,128)S(1)}, s32[]{:T(128)}, f32[64,64]{1,0:T(8,128)}, f32[64,64,4096]{2,1,0:T(8,128)}, /*index=5*/s32[]{:T(128)}, s32[]{:T(128)}, s32[]{:T(128)}) while((s32[]{:T(128)}, f32[64,4096]{1,0:T(8,128)S(1)}, s32[]{:T(128)}, f32[64,64]{1,0:T(8,128)}, f32[64,64,4096]{2,1,0:T(8,128)}, ...), condition=%wide.region_5.7_spmd, body=%wide.region_4.6_spmd.sunk | while | flops 524293 | bytes 3146631 | solution.py:23
  329.9 1.5 bitcast_add_fusion.2
  332.1 1.5 bitcast_add_fusion.2
  334.4 1.5 bitcast_add_fusion.2
  336.6 1.5 bitcast_add_fusion.2
  338.8 1.5 bitcast_add_fusion.2
  341.0 1.5 bitcast_add_fusion.2
  343.2 1.5 bitcast_add_fusion.2
  345.5 1.5 bitcast_add_fusion.2
  347.7 1.5 bitcast_add_fusion.2
  349.9 1.5 bitcast_add_fusion.2
  352.1 1.5 bitcast_add_fusion.2
  354.4 1.5 bitcast_add_fusion.2
  356.6 1.5 bitcast_add_fusion.2
  358.8 1.5 bitcast_add_fusion.2
  361.1 1.5 bitcast_add_fusion.2
  374.4 1.5 bitcast_add_fusion.2
  376.6 1.5 bitcast_add_fusion.2
  378.8 1.5 bitcast_add_fusion.2
  381.0 1.5 bitcast_add_fusion.2
  383.3 1.5 bitcast_add_fusion.2
  385.5 1.5 bitcast_add_fusion.2
  387.7 1.5 bitcast_add_fusion.2
  398.8 1.5 bitcast_add_fusion.2
  401.0 1.5 bitcast_add_fusion.2
  405.4 1.5 bitcast_add_fusion.2
  407.7 1.5 bitcast_add_fusion.2
  412.1 1.5 bitcast_add_fusion.2
  421.0 1.5 bitcast_add_fusion.2
  423.2 1.5 bitcast_add_fusion.2
  429.8 1.5 bitcast_add_fusion.2
  432.1 1.5 bitcast_add_fusion.2
  436.5 1.5 bitcast_add_fusion.2
  441.0 1.5 bitcast_add_fusion.2
  443.2 1.5 bitcast_add_fusion.2
  447.6 1.5 bitcast_add_fusion.2
  452.1 1.5 bitcast_add_fusion.2
  454.3 1.5 bitcast_add_fusion.2
  461.0 1.5 bitcast_add_fusion.2
  463.2 1.5 bitcast_add_fusion.2
  465.4 1.5 bitcast_add_fusion.2
  469.4 2.1 convert_element_type.82
  471.5 1.6 fusion.39
  473.2 1.8 copy.48
  475.0 4.5 add_convert_fusion
  (186 shorter events, 119.2 us)
Async XLA Ops:
  8.0 14.7 %all-to-all-start.3 = ((bf16[64,2,64]{2,1,0:T(2,128)(2,1)}), bf16[64,2,64]{2,1,0:T(2,128)(2,1)S(1)}, u32[]{:S(2)}, u32[]{:S(2)}) async-start(bf16[64,2,64]{2,1,0:T(2,128)(2,1)} %bitcast.8), calls=%async_computation.3 | async-start | bytes 65536 | tf_op jit(solution)/shard_map/all_to_all | solution.py:49
  22.6 16.1 %all-to-all-start.2 = ((bf16[64,2,512]{2,1,0:T(2,128)(2,1)}), bf16[64,2,512]{2,1,0:T(2,128)(2,1)S(1)}, u32[]{:S(2)}, u32[]{:S(2)}) async-start(bf16[64,2,512]{2,1,0:T(2,128)(2,1)} %reshape.545), calls=%async_computation.2 | async-start | bytes 262144 | tf_op jit(solution)/shard_map/all_to_all | solution.py:47
  38.8 15.8 %all-to-all-start.1 = ((bf16[64,2,512]{2,1,0:T(2,128)(2,1)}), bf16[64,2,512]{2,1,0:T(2,128)(2,1)S(1)}, u32[]{:S(2)}, u32[]{:S(2)}) async-start(bf16[64,2,512]{2,1,0:T(2,128)(2,1)} %reshape.542), calls=%async_computation.1 | async-start | bytes 262144 | tf_op jit(solution)/shard_map/all_to_all | solution.py:48
  47.4 15.9 %copy-start.8 = (s32[128]{0:T(128)S(1)}, s32[128]{0:T(128)}, u32[]{:S(2)}) copy-start(s32[128]{0:T(128)} %param.19) | copy-start | bytes 1540
  47.4 17.6 %copy-start.9 = (s32[1,128]{1,0:T(1,128)S(1)}, s32[1,128]{1,0:T(1,128)}, u32[]{:S(2)}) copy-start(s32[1,128]{1,0:T(1,128)} %param.18) | copy-start | bytes 1540
  47.4 19.6 %copy-start.6 = (f32[64]{0:T(128)S(1)}, f32[64]{0:T(128)}, u32[]{:S(2)}) copy-start(f32[64]{0:T(128)} %param.20) | copy-start | bytes 772
  54.5 33.8 %all-to-all-start = ((bf16[64,2,4096]{2,1,0:T(2,128)(2,1)}), bf16[64,2,4096]{2,1,0:T(2,128)(2,1)S(1)}, u32[]{:S(2)}, u32[]{:S(2)}) async-start(bf16[64,2,4096]{2,1,0:T(2,128)(2,1)} %reshape.540), calls=%async_computation | async-start | bytes 2097152 | tf_op jit(solution)/shard_map/all_to_all | solution.py:46
  63.2 265.9 %all-gather.3.cloned.1.call-start = ((), (), s32[]{:S(2)}) async-start(), calls=%async_computation.4 | async-start | bytes 68157440 | tf_op jit(solution)/shard_map/all_gather | solution.py:15
  63.6 2.7 copy-start.2
  65.0 25.6 %copy-start.3 = (pred[128]{0:T(512)(128)(4,1)}, pred[128]{0:T(512)(128)(4,1)S(1)}, u32[]{:S(2)}) copy-start(pred[128]{0:T(512)(128)(4,1)S(1)} %compare_and_fusion) | copy-start | bytes 388
  67.4 0.7 copy-start
  89.9 0.8 copy-start.1
  94.6 1.2 copy-start.7
  98.9 2.9 copy-start.5
  473.1 1.9 copy-start.4
Sparse Core Ops, SparseCore 0:
  95.9 233.2 all-gather.2
where the time goes:
time: 492 us; the launch traced here: 486 us
  waiting for transfers between devices  167 us (34%)
  other arithmetic  112 us (23%)
  local copies, waits for them, and re-layouts  81.1 us (16%)
  blocking collectives  41.8 us (8%)
  starting transfers between devices  35.6 us (7%)
  loops' own time  20.2 us (4%)
  between operations  14.4 us (3%)
  matrix products  13.6 us (3%)
    all_gather x1, waiting for transfers between devices, prefix(): gathered = jax.tree.map(lambda a: lax.all_gather(a, axis), part)  136 us
    add x64, other arithmetic, combine(): return (first_decay * second_decay, spread * first_state + second_state)  96.4 us
    mul x63, local copies, waits for them, and re-layouts, combine(): return (first_decay * second_decay, spread * first_state + second_state)  43.2 us
    all_gather x1, blocking collectives, prefix(): gathered = jax.tree.map(lambda a: lax.all_gather(a, axis), part)  41.8 us
    another operation x1, loops' own time, per_device(): local_out = lax.map(group_work, jnp.arange(G))  18.6 us
    all_to_all x1, waiting for transfers between devices, per_device(): lax.all_to_all(to_owner(x_loader), 'ctx', split_axis=0, concat_axis=0, ti...  17.5 us
  transfers between devices with their start and end apart: 5, of which 5 were waited for; matrix products, arithmetic and copies ran while one was open for 10% of the time, Pallas kernels for 0%

commit v1 on v0

v1 whole, which is shorter than its diff:
```python
import jax
import jax.numpy as jnp
from jax import lax
from jax.experimental import pallas as pl
from jax.experimental.pallas import tpu as pltpu
from jax.sharding import Mesh, PartitionSpec as P

F32 = jnp.float32
BF16 = jnp.bfloat16
I32 = jnp.int32
T = 128
NZ = 8
NW = 8
HG = 8
HP = 64
N = 64
GW = HG * HP
MSG = 88
VMEM = 48 * 1024 * 1024


def iota(shape, dim):
    return lax.broadcasted_iota(I32, shape, dim)


def dot(a, b):
    return jnp.dot(a, b, preferred_element_type=F32)


def params():
    return pltpu.CompilerParams(vmem_limit_bytes=VMEM)


def pack_kernel(x_ref, b_ref, c_ref, dt_ref, order_ref, reset_ref, out_ref):
    head, lane = iota((64, 1024), 0), iota((64, 1024), 1)
    spread = (lane % 128 < 64) & (head == (lane // 128) * 8 + lane % 8)
    wide = dot(dt_ref[...], spread.astype(BF16))
    row, lane = iota((T, 1024), 0), iota((T, 1024), 1)
    wide = jnp.where((row // 2) % 8 == (lane % 128) // 8, wide, 0.0).astype(BF16)
    to, row = iota((64, T), 0), iota((64, T), 1)
    pick = (row // 16 == to // 8) & (row % 2 == to % 8)
    steps = dot(pick.astype(BF16), wide)
    upto = (iota((T, T), 0) <= iota((T, T), 1)).astype(BF16)
    resets = jnp.broadcast_to(reset_ref[...].astype(F32), (8, T)).astype(BF16)
    count = dot(resets, upto)
    order = jnp.broadcast_to(order_ref[...].astype(F32), (8, T))
    own = iota((8, T), 1) % 8 == iota((8, T), 0)
    place = iota((T, T), 1) - iota((T, T), 0) // 8
    extra = dot(jnp.where(own, order, 0.0).astype(BF16), (place == 64).astype(BF16))
    extra += dot(jnp.where(own, count, 0.0).astype(BF16), (place == 80).astype(BF16))
    for z in range(NZ):
        rows = pl.ds(16 * z, 16)
        for g in range(NW):
            m = z * NW + g
            for j in range(4):
                out_ref[m, pl.ds(16 * j, 16), :] = x_ref[rows, pl.ds(GW * g + 128 * j, 128)]
            b = b_ref[rows, pl.ds(128 * (g // 2), 128)]
            c = c_ref[rows, pl.ds(128 * (g // 2), 128)]
            lo = N * (g % 2)
            out_ref[m, pl.ds(64, 16), :] = jnp.concatenate(
                [b[:, lo : lo + N], c[:, lo : lo + N]], axis=1
            )
            tail = steps[8 * z : 8 * z + 8, 128 * g : 128 * g + 128] + extra
            out_ref[m, pl.ds(80, 8), :] = tail.astype(BF16)


def expander():
    return (iota((T, GW), 0) % 8 == iota((T, GW), 1) // HP).astype(BF16)


def two_parts(v):
    high = v.astype(BF16).astype(F32)
    low = v - high
    return jnp.where(iota(v.shape, 1) < 64, high, pltpu.roll(low, 64, 1))


def expand(parts, i, e):
    mine = (iota(parts.shape, 1) % 64) // 8 == i
    return dot(jnp.where(mine, parts, 0.0).astype(BF16), e)


def state_kernel(
    arrived_ref, rate_ref, x_ref, bc_ref, cum_ref, key_ref, entry_ref, carry_ref, count_ref, hin_ref, msg_ref, perm_ref
):
    z = lax.axis_index("z")
    tails = jnp.concatenate(
        [arrived_ref[z * 8 + i, pl.ds(80, 8), :].astype(F32) for i in range(8)], axis=0
    ).astype(BF16)
    row, col = iota((1024, 64), 0), iota((1024, 64), 1)
    sel = (col == (row // T) * 8 + row % 8).astype(BF16)
    spread = dot(sel, tails)
    lane = iota((1024, T), 1)
    block = (iota((1024, T), 0) % T) // 8
    spread = jnp.where((lane == 64 + block) | (lane == 80 + block), spread, 0.0).astype(BF16)
    src, dst = iota((T, 256), 0), iota((T, 256), 1)
    gather = ((src >= 64) & (src < 80) & (dst < T)) | ((src >= 80) & (src < 96) & (dst >= T))
    both = dot(spread, gather.astype(BF16))
    order = both[:, :T].astype(I32)
    count = both[:, T:]
    count_ref[...] = count
    span = iota((1024, T), 0) // T
    target = (order // 2) * 16 + 2 * span + order % 2
    for m in range(8):
        perm_ref[:, pl.ds(128 * m, 128)] = jnp.where(lane + 128 * m == target, 1.0, 0.0).astype(BF16)
    rows = jnp.concatenate(
        [arrived_ref[:, pl.ds(16 * j, 16), :].reshape(1024, 128) for j in range(5)], axis=1
    )
    rows = dot(perm_ref[...], rows).astype(BF16)
    x_ref[...] = rows[:, :GW]
    bc_ref[...] = rows[:, GW:]
    steps_in = arrived_ref[:, pl.ds(80, 8), :].astype(F32).reshape(512, 128).astype(BF16)
    target = (order // 2) * 8 + order % 2
    small = jnp.concatenate(
        [jnp.where(lane + 128 * m == target, 1.0, 0.0).astype(BF16) for m in range(4)], axis=1
    )
    raw_all = dot(small, steps_in)
    lane = iota((T, T), 1)
    raw = jnp.zeros((T, T), F32)
    cnt = jnp.zeros((T, T), F32)
    for i in range(8):
        raw = jnp.where(lane // 8 == i, raw_all[T * i : T * i + T], raw)
        cnt = jnp.where(lane // 8 == i, count[T * i : T * i + T], cnt)
    step = jnp.maximum(raw, 0.0) + jnp.log1p(jnp.exp(-jnp.abs(raw)))
    logd = -step * rate_ref[...]
    lower = (iota((T, T), 0) >= iota((T, T), 1)).astype(F32)
    cum = jnp.dot(lower, logd, preferred_element_type=F32, precision=lax.Precision.HIGHEST)
    cum_ref[...] = cum
    key_ref[...] = (cum - jnp.log(step)).T
    last = cum[T - 1 : T]
    last_cnt = cnt[T - 1 : T]
    entry = jnp.where(cnt == 0.0, jnp.exp(cum), 0.0)
    entry_ref[...] = entry
    decay = jnp.where(last_cnt == 0.0, jnp.exp(last), 0.0)
    decay = jnp.broadcast_to(decay, (8, T))
    lane8 = iota((8, T), 1)
    before = jnp.where(lane8 < 8, 1.0, pltpu.roll(decay, 8, 1))
    for shift in (8, 16, 32):
        before = before * jnp.where(lane8 < shift, 1.0, pltpu.roll(before, shift, 1))
    carry_ref[...] = entry * before[:1]
    coef = jnp.where(cnt == last_cnt, jnp.exp(last - cum) * step, 0.0)
    e = expander()
    coef = two_parts(coef)
    mine = (lane8 % 64) // 8 == iota((8, T), 0)
    decay = dot(jnp.where(mine, two_parts(decay), 0.0).astype(BF16), e)
    h = jnp.zeros((N, GW), F32)
    total = jnp.ones((1, GW), F32)
    for i in range(8):
        here = pl.ds(T * i, T)
        hin_ref[i] = h.astype(BF16)
        xw = (x_ref[here, :].astype(F32) * expand(coef, i, e)).astype(BF16)
        b = bc_ref[here, :].astype(F32).T[:N].astype(BF16)
        h = decay[i : i + 1] * h + dot(b, xw)
        total = total * decay[i : i + 1]
    high = total.astype(BF16).astype(F32)
    mid = (total - high).astype(BF16).astype(F32)
    low = total - high - mid
    row = iota((16, GW), 0)
    parts = jnp.where(row == 0, high, jnp.where(row == 1, mid, jnp.where(row == 2, low, 0.0)))
    for m in range(8):
        lanes = slice(128 * (m // 2), 128 * (m // 2) + 128)
        msg_ref[m, pl.ds(0, 32), :] = h[32 * (m % 2) : 32 * (m % 2) + 32, lanes].astype(BF16)
        msg_ref[m, pl.ds(32, 16), :] = parts[:, lanes].astype(BF16)


def local_kernel(x_ref, bc_ref, cum_ref, key_ref, entry_ref, count_ref, hin_ref, skip_ref, out_ref):
    e = expander()
    entry = two_parts(entry_ref[...])
    causal = iota((T, T), 0) >= iota((T, T), 1)
    left = iota((T, T), 1) < HP
    for i in range(8):
        here = pl.ds(T * i, T)
        count = count_ref[here, :]
        keep = causal & (count == count.T)
        bc = bc_ref[here, :]
        b = bc.astype(F32).T[:N].astype(BF16)
        scores = dot(bc[:, N:], b)
        carried = dot(bc[:, N:], hin_ref[i]) * expand(entry, i, e)
        for pair in range(4):
            weights = []
            for h in (2 * pair, 2 * pair + 1):
                c = 8 * i + h
                gap = cum_ref[:, c : c + 1] - key_ref[c : c + 1, :]
                weights.append((jnp.exp(jnp.where(keep, gap, -jnp.inf)) * scores).astype(BF16))
            lanes = pl.ds(128 * pair, 128)
            x = x_ref[here, lanes]
            zero = jnp.zeros_like(x)
            both = jnp.concatenate([jnp.where(left, x, zero), jnp.where(left, zero, x)], axis=0)
            local = dot(jnp.concatenate(weights, axis=1), both)
            out_ref[here, lanes] = (
                local + carried[:, 128 * pair : 128 * pair + 128] + skip_ref[:, lanes] * x.astype(F32)
            )


def scan_kernel(in_ref, out_ref):
    h = jnp.zeros((32, 128), F32)
    for z in range(NZ):
        out_ref[z] = h.astype(BF16)
        parts = in_ref[z, pl.ds(32, 16), :].astype(F32)
        decay = parts[0:1] + parts[1:2] + parts[2:3]
        h = decay * h + in_ref[z, pl.ds(0, 32), :].astype(F32)


def final_kernel(partial_ref, bc_ref, carry_ref, h_ref, out_ref):
    e = expander()
    carry = two_parts(carry_ref[...])
    state = jnp.concatenate(
        [jnp.concatenate([h_ref[2 * p], h_ref[2 * p + 1]], axis=0) for p in range(4)], axis=1
    )
    for i in range(8):
        here = pl.ds(T * i, T)
        inter = dot(bc_ref[here, :][:, N:], state) * expand(carry, i, e)
        out_ref[i] = (partial_ref[here, :] + inter).astype(BF16)


def join_kernel(in_ref, out_ref):
    for g in range(NW):
        out_ref[:, pl.ds(GW * g, GW)] = in_ref[g]


def per_device(x, b, c, dt, order, resets, rate, skip):
    w = lax.axis_index("w")
    sds = jax.ShapeDtypeStruct
    packed = pl.pallas_call(
        pack_kernel, out_shape=sds((NZ * NW, MSG, 128), BF16), compiler_params=params(), name="pack"
    )(x, b, c, dt, order, resets.reshape(1, T))
    arrived = lax.all_to_all(packed, ("z", "w"), split_axis=0, concat_axis=0, tiled=True)
    mine = lax.dynamic_slice_in_dim(rate, w * HG, HG)
    rate_row = jnp.concatenate([jnp.tile(mine, 8), jnp.zeros((64,), F32)]).reshape(1, T)
    skip_row = jnp.repeat(lax.dynamic_slice_in_dim(skip, w * HG, HG), HP).reshape(1, GW)
    xs, bc, cum, key, entry, carry, count, hin, msg = pl.pallas_call(
        state_kernel,
        out_shape=(
            sds((NZ * T, GW), BF16),
            sds((NZ * T, 128), BF16),
            sds((T, T), F32),
            sds((T, T), F32),
            sds((T, T), F32),
            sds((T, T), F32),
            sds((NZ * T, T), F32),
            sds((8, N, GW), BF16),
            sds((NZ, 48, 128), BF16),
        ),
        scratch_shapes=[pltpu.VMEM((1024, 1024), BF16)],
        compiler_params=params(),
        name="state",
    )(arrived, rate_row)
    totals = lax.all_to_all(msg, "z", split_axis=0, concat_axis=0, tiled=True)
    partial = pl.pallas_call(
        local_kernel,
        out_shape=sds((NZ * T, GW), F32),
        compiler_params=params(),
        cost_estimate=pl.CostEstimate(flops=600_000_000, bytes_accessed=6_000_000, transcendentals=1_100_000),
        name="local",
    )(xs, bc, cum, key, entry, count, hin, skip_row)
    entering = pl.pallas_call(
        scan_kernel, out_shape=sds((NZ, 32, 128), BF16), compiler_params=params(), name="planes"
    )(totals)
    states = lax.all_to_all(entering, "z", split_axis=0, concat_axis=0, tiled=True)
    out = pl.pallas_call(
        final_kernel,
        out_shape=sds((8, T, GW), BF16),
        compiler_params=params(),
        name="final",
    )(partial, bc, carry, states)
    owned = lax.all_to_all(out, "w", split_axis=0, concat_axis=0, tiled=True)
    return pl.pallas_call(
        join_kernel, out_shape=sds((T, NW * GW), BF16), compiler_params=params(), name="join"
    )(owned)


def solution(mesh):
    fine = Mesh(mesh.devices.reshape(NZ, NW, mesh.shape["seq"]), ("z", "w", "seq"))
    rows = ("seq", "z", "w")
    in_specs = (P(rows, None),) * 5 + (P(rows), P(), P())
    return jax.shard_map(
        per_device, mesh=fine, in_specs=in_specs, out_specs=P(rows, None), check_vma=False
    )
```

time: 492 us -> 109 us (0.22)
  the two profiles are of different devices: /device:TPU:231 before, /device:TPU:1 now
where the time goes in v1:
time: 109 us; the launch traced here: 108 us
  waiting for transfers between devices  36.3 us (33%)
  blocking collectives  32.7 us (30%)
  starting transfers between devices  16.5 us (15%)
  local copies, waits for them, and re-layouts  11.8 us (11%)
  Pallas kernels  11.1 us (10%)
    all_to_all x1, waiting for transfers between devices, per_device(): lax.all_to_all(packed, ('z', 'w'), split_axis=0, concat_axis=0, tiled=True)  36.2 us
    all_to_all x1, blocking collectives, per_device(): owned = lax.all_to_all(out, 'w', split_axis=0, concat_axis=0, tiled=True)  21 us
    all_to_all x1, starting transfers between devices, per_device(): lax.all_to_all(packed, ('z', 'w'), split_axis=0, concat_axis=0, tiled=True)  13.1 us
    all_to_all x1, blocking collectives, per_device(): totals = lax.all_to_all(msg, 'z', split_axis=0, concat_axis=0, tiled=True)  11.7 us
    unnamed x35, local copies, waits for them, and re-layouts  11.4 us
    pallas_call x1, Pallas kernels, per_device(): pl.pallas_call(state_kernel, out_shape=(sds((NZ * T, GW), BF16), sds((NZ...  4.67 us
    all_to_all x1, starting transfers between devices, per_device(): lax.all_to_all(entering, 'z', split_axis=0, concat_axis=0, tiled=True)  3.35 us
    pallas_call x1, Pallas kernels, per_device(): pl.pallas_call(local_kernel, out_shape=sds((NZ * T, GW), F32), compiler_p...  2.28 us
  transfers between devices with their start and end apart: 2, of which 2 were waited for; matrix products, arithmetic and copies ran while one was open for 0% of the time, Pallas kernels for 2%

profile of v1, /device:TPU:1, one launch (start us, length us, event | category | flops | bytes accessed | tf_op | source)
XLA Modules:
  0.0 108.4 jit_solution(2833846229661712480)
XLA Ops:
  0.0 0.8 copy.9.dt_ref
  0.8 0.0 copy-start
  0.8 1.2 %copy-done = bf16[128,4096]{1,0:T(8,128)(2,1)S(1)} copy-done((bf16[128,4096]{1,0:T(8,128)(2,1)S(1)}, bf16[128,4096]{1,0:T(8,128)(2,1)}, u32[]{:S(2)}) %copy-start) | copy-done | bytes 1048600
  2.1 0.0 copy-start.5
  2.1 0.9 copy-done.5
  3.0 0.0 copy-start.6
  3.0 0.9 copy-done.6
  3.9 0.0 copy-start.13
  3.9 0.7 copy-done.13
  4.5 0.0 copy-start.14
  4.5 0.7 copy-done.14
  5.2 1.7 %pack.1 = bf16[64,88,128]{2,1,0:T(8,128)(2,1)} custom-call(bf16[128,4096]{1,0:T(8,128)(2,1)S(1)} %copy-done, bf16[128,512]{1,0:T(8,128)(2,1)S(1)} %copy-done.5, bf16[128,512]{1,0:T(8,128)(2,1)S(1)} %copy-done.6, bf16[128,64]{1,0:T(8,128)(2,1)S(1)} %copy.9.dt_ref, s32[1,128]{1,0:T(1,128)S(1)} %copy-done.13, s32[1,128]{1,0:T(1,128)S(1)} %bitcast.3), custom_call_target="tpu_custom_call" | custom-call | tf_op jit(solution)/shard_map/pack/pallas_call | solution.py:223
  6.9 0.0 copy-start.15
  6.9 13.1 %all-to-all-start = ((bf16[64,88,128]{2,1,0:T(8,128)(2,1)}), bf16[64,88,128]{2,1,0:T(8,128)(2,1)S(1)}, u32[]{:S(2)}, u32[]{:S(2)}) async-start(bf16[64,88,128]{2,1,0:T(8,128)(2,1)} %pack.1), calls=%async_computation | async-start | bytes 2883584 | tf_op jit(solution)/shard_map/all_to_all | solution.py:226
  20.0 0.0 copy-start.16
  20.1 0.0 copy-done.15
  20.1 0.1 dynamic_slice.6
  20.1 0.1 tile.10
  20.2 36.2 %all-to-all-done.arrived_ref = bf16[64,88,128]{2,1,0:T(8,128)(2,1)S(1)} async-done(((bf16[64,88,128]{2,1,0:T(8,128)(2,1)}), bf16[64,88,128]{2,1,0:T(8,128)(2,1)S(1)}, u32[]{:S(2)}, u32[]{:S(2)}) %all-to-all-start) | async-done | bytes 1441824 | tf_op jit(solution)/shard_map/all_to_all | solution.py:226
  56.4 4.7 %state.1 = (bf16[1024,512]{1,0:T(8,128)(2,1)S(1)}, bf16[1024,128]{1,0:T(8,128)(2,1)S(1)}, f32[128,128]{1,0:T(8,128)S(1)}, f32[128,128]{1,0:T(8,128)S(1)}, f32[12...) custom-call(bf16[64,88,128]{2,1,0:T(8,128)(2,1)S(1)} %all-to-all-don, ...), custom_call_target="tpu_custom_call" | custom-call | tf_op jit(solution)/shard_map/state/pallas_call | solution.py:230
  61.1 0.0 copy-start.1
  61.1 0.8 copy-done.1
  61.9 0.0 copy-start.3
  61.9 0.8 copy-done.3
  62.7 0.0 copy-start.7
  62.7 0.0 copy-start.9
  62.7 0.0 copy-start.11
  62.7 11.7 %all_to_all.20.in_ref = bf16[8,48,128]{2,1,0:T(8,128)(2,1)S(1)} all-to-all(bf16[8,48,128]{2,1,0:T(8,128)(2,1)S(1)} %get-tuple-element.22), channel_id=1, replica_groups=mesh['z'=8,'w'=8,'seq'=4] {'z'}, dimensions={0} | all-to-all | bytes 196608 | tf_op jit(solution)/shard_map/all_to_all | solution.py:247
  74.4 0.0 copy-done.7
  74.4 0.7 planes.1
  75.0 0.0 copy-done.9
  75.0 3.3 %all-to-all-start.2 = ((bf16[8,32,128]{2,1,0:T(8,128)(2,1)}), bf16[8,32,128]{2,1,0:T(8,128)(2,1)S(1)}, u32[]{:S(2)}, u32[]{:S(2)}) async-start(bf16[8,32,128]{2,1,0:T(8,128)(2,1)} %planes.1), calls=%async_computation.2 | async-start | bytes 131072 | tf_op jit(solution)/shard_map/all_to_all | solution.py:258
  78.4 0.0 copy-done.16
  78.4 0.1 dynamic_slice.7
  78.5 0.1 broadcast_in_dim.4
  78.6 0.1 reshape_reshape.3.skip_ref
  78.6 0.0 copy-done.11
  78.6 0.0 copy-start.2
  78.6 1.0 copy-done.2
  79.7 0.0 copy-start.4
  79.7 1.0 copy-done.4
  80.7 0.0 copy-start.8
  80.7 0.8 copy-done.8
  81.6 0.0 copy-start.10
  81.6 0.8 copy-done.10
  82.4 0.0 copy-start.12
  82.4 0.8 copy-done.12
  83.2 2.3 %local.1.partial_ref = f32[1024,512]{1,0:T(8,128)S(1)} custom-call(bf16[1024,512]{1,0:T(8,128)(2,1)S(1)} %get-tuple-element.14.x_ref, bf16[1024,128]{1,0:T(8,128)(2,1)S(1)} %get-tuple-element.15.bc_ref, f32[128,128]{1,0:T(8,128)S(1)} %copy-done.8, f32[128,128]{1,0:T(8,128)S(1)} %copy-done.10, f32[128,128]{1,0:T(8,128)S(1)} %copy-done.12, ...), custom_call_target="tpu_custom_call" | custom-call | flops 600000000 | bytes 6000000 | tf_op jit(solution)/shard_map/local/pallas_call | solution.py:248
  85.5 0.1 all-to-all-done.2.h_ref
  85.7 0.7 final.1
  86.4 21.0 %all_to_all.21.in_ref = bf16[8,128,512]{2,1,0:T(8,128)(2,1)S(1)} all-to-all(bf16[8,128,512]{2,1,0:T(8,128)(2,1)S(1)} %final.1), channel_id=1, replica_groups=mesh['z'=8,'w'=8,'seq'=4] {'w'}, dimensions={0} | all-to-all | bytes 2097152 | tf_op jit(solution)/shard_map/all_to_all | solution.py:265
  107.4 1.0 join.1
  (2 shorter events, 0.0 us)
Async XLA Ops:
  0.8 1.2 %copy-start = (bf16[128,4096]{1,0:T(8,128)(2,1)S(1)}, bf16[128,4096]{1,0:T(8,128)(2,1)}, u32[]{:S(2)}) copy-start(bf16[128,4096]{1,0:T(8,128)(2,1)} %x_ref.1) | copy-start | bytes 3145732
  2.1 0.9 copy-start.5
  3.0 0.9 copy-start.6
  3.9 0.7 copy-start.13
  4.5 0.7 copy-start.14
  6.9 13.1 %copy-start.15 = (f32[64]{0:T(128)S(1)}, f32[64]{0:T(128)}, u32[]{:S(2)}) copy-start(f32[64]{0:T(128)} %param.14) | copy-start | bytes 772
  6.9 49.5 %all-to-all-start = ((bf16[64,88,128]{2,1,0:T(8,128)(2,1)}), bf16[64,88,128]{2,1,0:T(8,128)(2,1)S(1)}, u32[]{:S(2)}, u32[]{:S(2)}) async-start(bf16[64,88,128]{2,1,0:T(8,128)(2,1)} %pack.1), calls=%async_computation | async-start | bytes 2883584 | tf_op jit(solution)/shard_map/all_to_all | solution.py:226
  20.0 58.4 %copy-start.16 = (f32[64]{0:T(128)S(1)}, f32[64]{0:T(128)}, u32[]{:S(2)}) copy-start(f32[64]{0:T(128)} %param.15) | copy-start | bytes 772
  61.1 0.8 copy-start.1
  61.9 0.8 copy-start.3
  62.7 11.7 %copy-start.7 = (f32[128,128]{1,0:T(8,128)}, f32[128,128]{1,0:T(8,128)S(1)}, u32[]{:S(2)}) copy-start(f32[128,128]{1,0:T(8,128)S(1)} %get-tuple-element.16.cum_ref) | copy-start | bytes 196612
  62.7 12.4 %copy-start.9 = (f32[128,128]{1,0:T(8,128)}, f32[128,128]{1,0:T(8,128)S(1)}, u32[]{:S(2)}) copy-start(f32[128,128]{1,0:T(8,128)S(1)} %get-tuple-element.17.key_ref) | copy-start | bytes 196612
  62.7 16.0 %copy-start.11 = (f32[128,128]{1,0:T(8,128)}, f32[128,128]{1,0:T(8,128)S(1)}, u32[]{:S(2)}) copy-start(f32[128,128]{1,0:T(8,128)S(1)} %get-tuple-element.18.entry_ref) | copy-start | bytes 196612
  75.0 10.6 %all-to-all-start.2 = ((bf16[8,32,128]{2,1,0:T(8,128)(2,1)}), bf16[8,32,128]{2,1,0:T(8,128)(2,1)S(1)}, u32[]{:S(2)}, u32[]{:S(2)}) async-start(bf16[8,32,128]{2,1,0:T(8,128)(2,1)} %planes.1), calls=%async_computation.2 | async-start | bytes 131072 | tf_op jit(solution)/shard_map/all_to_all | solution.py:258
  78.6 1.0 copy-start.2
  79.7 1.0 copy-start.4
  80.7 0.8 copy-start.8
  81.6 0.8 copy-start.10
  82.4 0.8 copy-start.12

commit v2 on v1

v2 whole, which is shorter than its diff:
```python
import jax
import jax.numpy as jnp
from jax import lax
from jax.experimental import pallas as pl
from jax.experimental.pallas import tpu as pltpu
from jax.sharding import Mesh, PartitionSpec as P

F32 = jnp.float32
BF16 = jnp.bfloat16
I32 = jnp.int32
T = 128
NP = 32
HG = 8
HP = 64
N = 64
GW = HG * HP
HH = 32
HW = HH * HP
MSG = 88


def iota(shape, dim):
    return lax.broadcasted_iota(I32, shape, dim)


def dot(a, b):
    return jnp.dot(a, b, preferred_element_type=F32)


def dot_nt(a, b):
    return lax.dot_general(a, b, (((1,), (1,)), ((), ())), preferred_element_type=F32)


def params(mib):
    return pltpu.CompilerParams(vmem_limit_bytes=mib * 1024 * 1024)


def pack_kernel(x_hbm, b_hbm, c_hbm, dt_hbm, order_hbm, reset_hbm, out_ref, x_ref, b_ref, c_ref, dt_ref, order_ref, reset_ref, sems):
    pairs = (
        (order_hbm, order_ref), (reset_hbm, reset_ref), (dt_hbm, dt_ref),
        (b_hbm, b_ref), (c_hbm, c_ref), (x_hbm, x_ref),
    )
    copies = [pltpu.make_async_copy(s, d, sems.at[n]) for n, (s, d) in enumerate(pairs)]
    for copy in copies:
        copy.start()
    row, col = iota((256, 256), 0), iota((256, 256), 1)
    pick = (col // 64 == (row % 16) // 4) & (col % 64 == (row // 16) * 4 + row % 4)
    pick = pick.astype(BF16)
    lane, head = iota((256, 64), 0), iota((256, 64), 1)
    spread = (lane % T < 64) & (head == (lane // T) * HH + lane % HH)
    to, row = iota((256, T), 0), iota((256, T), 1)
    own_row = ((row // 4 == to // 8) & (row % 2 == to % 8)).astype(BF16)
    own_span = (row // 2) % 2 == (to % T) // HH
    upto = (iota((T, T), 0) <= iota((T, T), 1)).astype(BF16)
    own = iota((8, T), 1) % 8 == iota((8, T), 0)
    place = iota((T, T), 1) - iota((T, T), 0) // 8
    for copy in copies[:3]:
        copy.wait()
    wide = jnp.where(own_span, dot(spread.astype(BF16), dt_ref[...]), 0.0).astype(BF16)
    steps = dot_nt(own_row, wide)
    resets = jnp.broadcast_to(reset_ref[...].astype(F32), (8, T)).astype(BF16)
    count = dot(resets, upto)
    order = jnp.broadcast_to(order_ref[...].astype(F32), (8, T))
    extra = dot(jnp.where(own, order, 0.0).astype(BF16), (place == 64).astype(BF16))
    extra += dot(jnp.where(own, count, 0.0).astype(BF16), (place == 80).astype(BF16))
    for p in range(NP):
        for c in range(2):
            tail = steps[8 * p : 8 * p + 8, T * c : T * c + T] + extra
            out_ref[2 * p + c, pl.ds(80, 8), :] = tail.astype(BF16)
    for copy in copies[3:]:
        copy.wait()
    for part in range(2):
        rows = pl.ds(64 * part, 64)
        tiles = []
        for c in range(2):
            for q in range(4):
                tiles.append([x_ref[rows, pl.ds(HW * c + 512 * q + T * j, T)] for j in range(4)])
            tiles.append(
                [b_ref[rows, pl.ds(256 * c, T)], b_ref[rows, pl.ds(256 * c + T, T)],
                 c_ref[rows, pl.ds(256 * c, T)], c_ref[rows, pl.ds(256 * c + T, T)]]
            )
        right = jnp.concatenate([jnp.concatenate(t, axis=0) for t in tiles], axis=1)
        got = dot(pick, right).astype(BF16)
        for p in range(16):
            for c in range(2):
                for q in range(5):
                    lanes = slice(T * (5 * c + q), T * (5 * c + q) + T)
                    out_ref[2 * (16 * part + p) + c, pl.ds(16 * q, 16), :] = got[16 * p : 16 * p + 16, lanes]


def expander():
    return (iota((T, HW), 0) % HH == iota((T, HW), 1) // HP).astype(BF16)


def two_parts(v):
    high = v.astype(BF16).astype(F32)
    low = v - high
    return jnp.where(iota(v.shape, 1) < 64, high, pltpu.roll(low, 64, 1))


def of_span(parts, i):
    return jnp.where((iota(parts.shape, 1) % 64) // HH == i, parts, 0.0).astype(BF16)


def state_kernel(
    arrived_ref, rate_ref, x_ref, bc_ref, cum_ref, key_ref, entry_ref, carry_ref, count_ref, hin_ref, msg_ref, perm_ref
):
    chip = lax.axis_index("p")
    tails = jnp.concatenate(
        [arrived_ref[chip * 2 + i, pl.ds(80, 8), :].astype(F32) for i in range(2)], axis=0
    ).astype(BF16)
    row, col = iota((256, 16), 0), iota((256, 16), 1)
    sel = (col == (row // T) * 8 + row % 8).astype(BF16)
    spread = dot(sel, tails)
    lane = iota((256, T), 1)
    block = (iota((256, T), 0) % T) // 8
    spread = jnp.where((lane == 64 + block) | (lane == 80 + block), spread, 0.0).astype(BF16)
    src, dst = iota((T, 256), 0), iota((T, 256), 1)
    gather = ((src >= 64) & (src < 80) & (dst < T)) | ((src >= 80) & (src < 96) & (dst >= T))
    both = dot(spread, gather.astype(BF16))
    order = both[:, :T].astype(I32)
    count = both[:, T:]
    count_ref[...] = count
    target = (order // 2) * 16 + 2 * (iota((256, T), 0) // T) + order % 2
    for j in range(4):
        for m in range(8):
            hit = lane + (T * m - 4 * j) == target
            perm_ref[pl.ds(256 * j, 256), pl.ds(T * m, T)] = jnp.where(hit, 1.0, 0.0).astype(BF16)
    rows = jnp.concatenate(
        [arrived_ref[:, pl.ds(16 * q, 16), :].reshape(1024, T) for q in range(5)], axis=1
    )
    rows = dot(perm_ref[...], rows).astype(BF16)
    for j in range(4):
        for q in range(4):
            x_ref[:, pl.ds(T * (4 * q + j), T)] = rows[256 * j : 256 * j + 256, T * q : T * q + T]
        bc_ref[:, pl.ds(T * j, T)] = rows[256 * j : 256 * j + 256, T * 4 :]
    steps_in = arrived_ref[:, pl.ds(80, 8), :].astype(F32).reshape(512, T).astype(BF16)
    target = (order // 2) * 8 + order % 2
    small = jnp.concatenate(
        [jnp.where(lane + T * m == target, 1.0, 0.0).astype(BF16) for m in range(4)], axis=1
    )
    raw = dot(small, steps_in)
    first = iota((T, T), 1) < HH
    raw = jnp.where(first, raw[:T], raw[T:])
    cnt = jnp.where(first, count[:T], count[T:])
    step = jnp.maximum(raw, 0.0) + jnp.log1p(jnp.exp(-jnp.abs(raw)))
    logd = -step * rate_ref[...]
    lower = (iota((T, T), 0) >= iota((T, T), 1)).astype(F32)
    cum = jnp.dot(lower, logd, preferred_element_type=F32, precision=lax.Precision.HIGHEST)
    cum_ref[...] = cum
    key_ref[...] = (cum - jnp.log(step)).T
    last = cum[T - 1 : T]
    last_cnt = cnt[T - 1 : T]
    entry = jnp.where(cnt == 0.0, jnp.exp(cum), 0.0)
    entry_ref[...] = entry
    decay = jnp.where(last_cnt == 0.0, jnp.exp(last), 0.0)
    decay = jnp.broadcast_to(decay, (8, T))
    before = jnp.where(iota((8, T), 1) < HH, 1.0, pltpu.roll(decay, HH, 1))
    carry_ref[...] = entry * before[:1]
    coef = two_parts(jnp.where(cnt == last_cnt, jnp.exp(last - cum) * step, 0.0))
    e = expander()
    decay = two_parts(decay)
    decay = [dot(of_span(decay, i), e)[:1] for i in range(2)]
    total = decay[0] * decay[1]
    weighted = []
    for i in range(2):
        here = pl.ds(T * i, T)
        weighted.append((x_ref[here, :].astype(F32) * dot(of_span(coef, i), e)).astype(BF16))
    high = total.astype(BF16).astype(F32)
    mid = (total - high).astype(BF16).astype(F32)
    low = total - high - mid
    row = iota((8, HW), 0)
    parts = jnp.where(row == 0, high, jnp.where(row == 1, mid, jnp.where(row == 2, low, 0.0))).astype(BF16)
    for tile in range(2):
        b = [bc_ref[pl.ds(T * i, T), pl.ds(T * tile, T)].astype(F32).T.astype(BF16) for i in range(2)]
        for half in range(2):
            g = 2 * tile + half
            lanes = slice(GW * g, GW * g + GW)
            states = [dot(b[i][N * half : N * half + N], weighted[i][:, lanes]) for i in range(2)]
            hin_ref[:, lanes] = states[0].astype(BF16)
            h = (decay[1][:, lanes] * states[0] + states[1]).astype(BF16)
            for pair in range(4):
                for k in range(2):
                    m = (4 * g + pair) * 2 + k
                    msg_ref[m, pl.ds(0, 32), :] = h[32 * k : 32 * k + 32, T * pair : T * pair + T]
    for m in range(NP):
        msg_ref[m, pl.ds(32, 8), :] = parts[:, T * (m // 2) : T * (m // 2) + T]


def local_kernel(x_ref, bc_ref, cum_ref, key_ref, entry_ref, count_ref, hin_ref, skip_ref, out_ref):
    e = expander()
    entry = dot(of_span(two_parts(entry_ref[...]), 1), e)
    causal = iota((T, T), 0) >= iota((T, T), 1)
    left = iota((T, T), 1) < HP
    for i in range(2):
        here = pl.ds(T * i, T)
        count = count_ref[here, :]
        keep = causal & (count == count.T)
        for g in range(4):
            tile, half = g // 2, g % 2
            b = bc_ref[here, pl.ds(T * tile, T)][:, N * half : N * half + N]
            c = bc_ref[here, pl.ds(2 * T + T * tile, T)][:, N * half : N * half + N]
            scores = dot_nt(c, b)
            if i == 1:
                lanes = pl.ds(GW * g, GW)
                carried = dot(c, hin_ref[:, lanes]) * entry[:, GW * g : GW * g + GW]
            for pair in range(4):
                weights = []
                for h in (2 * pair, 2 * pair + 1):
                    col = HH * i + HG * g + h
                    gap = cum_ref[:, col : col + 1] - key_ref[col : col + 1, :]
                    weights.append((jnp.exp(jnp.where(keep, gap, -jnp.inf)) * scores).astype(BF16))
                lanes = pl.ds(GW * g + T * pair, T)
                x = x_ref[here, lanes]
                zero = jnp.zeros_like(x)
                both = jnp.concatenate([jnp.where(left, x, zero), jnp.where(left, zero, x)], axis=0)
                out = dot(jnp.concatenate(weights, axis=1), both) + skip_ref[:, lanes] * x.astype(F32)
                if i == 1:
                    out += carried[:, T * pair : T * pair + T]
                out_ref[here, lanes] = out


def scan_kernel(in_ref, out_ref):
    h = jnp.zeros((32, T), F32)
    for p in range(NP):
        out_ref[p] = h.astype(BF16)
        parts = in_ref[p, pl.ds(32, 8), :].astype(F32)
        decay = parts[0:1] + parts[1:2] + parts[2:3]
        h = decay * h + in_ref[p, pl.ds(0, 32), :].astype(F32)


def final_kernel(partial_ref, bc_ref, carry_ref, h_ref, mine_ref, other_ref):
    core = lax.axis_index("c")
    e = expander()
    carry = two_parts(carry_ref[...])
    for ref, i in ((other_ref, 1 - core), (mine_ref, core)):
        here = pl.ds(pl.multiple_of(T * i, T), T)
        scale = dot(of_span(carry, i), e)
        for g in range(4):
            c = bc_ref[here, pl.ds(2 * T + T * (g // 2), T)][:, N * (g % 2) : N * (g % 2) + N]
            state = jnp.concatenate(
                [jnp.concatenate([h_ref[8 * g + 2 * p], h_ref[8 * g + 2 * p + 1]], axis=0) for p in range(4)], axis=1
            )
            lanes = slice(GW * g, GW * g + GW)
            inter = dot(c, state) * scale[:, lanes]
            ref[:, lanes] = (partial_ref[here, lanes] + inter).astype(BF16)


def join_kernel(mine_ref, other_ref, out_ref):
    core = lax.axis_index("c")
    for k in range(2):

        @pl.when(core == k)
        def _():
            out_ref[:, pl.ds(HW * k, HW)] = mine_ref[...]
            out_ref[:, pl.ds(HW * (1 - k), HW)] = other_ref[...]


def per_device(x, b, c, dt, order, resets, rate, skip):
    core = lax.axis_index("c")
    sds = jax.ShapeDtypeStruct
    packed = pl.pallas_call(
        pack_kernel,
        out_shape=sds((2 * NP, MSG, T), BF16),
        in_specs=[pl.BlockSpec(memory_space=pltpu.HBM)] * 6,
        scratch_shapes=[
            pltpu.VMEM(x.shape, BF16),
            pltpu.VMEM(b.shape, BF16),
            pltpu.VMEM(c.shape, BF16),
            pltpu.VMEM(dt.shape[::-1], BF16),
            pltpu.VMEM((1, T), I32),
            pltpu.VMEM((1, T), I32),
            pltpu.SemaphoreType.DMA((6,)),
        ],
        compiler_params=params(20),
        name="pack",
    )(x, b, c, dt.T, order, resets.reshape(1, T))
    arrived = lax.all_to_all(packed, ("p", "c"), split_axis=0, concat_axis=0, tiled=True)
    mine = lax.dynamic_slice_in_dim(rate, core * HH, HH)
    rate_row = jnp.concatenate([mine, mine, jnp.zeros((64,), F32)]).reshape(1, T)
    skip_row = jnp.repeat(lax.dynamic_slice_in_dim(skip, core * HH, HH), HP).reshape(1, HW)
    xs, bc, cum, key, entry, carry, count, hin, msg = pl.pallas_call(
        state_kernel,
        out_shape=(
            sds((2 * T, HW), BF16),
            sds((2 * T, 4 * T), BF16),
            sds((T, T), F32),
            sds((T, T), F32),
            sds((T, T), F32),
            sds((T, T), F32),
            sds((2 * T, T), F32),
            sds((N, HW), BF16),
            sds((NP, 40, T), BF16),
        ),
        scratch_shapes=[pltpu.VMEM((1024, 1024), BF16)],
        compiler_params=params(24),
        name="state",
    )(arrived, rate_row)
    totals = lax.all_to_all(msg, "p", split_axis=0, concat_axis=0, tiled=True)
    partial = pl.pallas_call(
        local_kernel,
        out_shape=sds((2 * T, HW), F32),
        compiler_params=params(20),
        cost_estimate=pl.CostEstimate(flops=2_000_000_000, bytes_accessed=6_000_000, transcendentals=1_100_000),
        name="local",
    )(xs, bc, cum, key, entry, count, hin, skip_row)
    entering = pl.pallas_call(
        scan_kernel, out_shape=sds((NP, 32, T), BF16), compiler_params=params(16), name="chips"
    )(totals)
    states = lax.all_to_all(entering, "p", split_axis=0, concat_axis=0, tiled=True)
    own, other = pl.pallas_call(
        final_kernel,
        out_shape=(sds((T, HW), BF16), sds((T, HW), BF16)),
        compiler_params=params(20),
        name="final",
    )(partial, bc, carry, states)
    other = lax.ppermute(other, "c", [(0, 1), (1, 0)])
    return pl.pallas_call(
        join_kernel, out_shape=sds((T, 2 * HW), BF16), compiler_params=params(16), name="join"
    )(own, other)


def solution(mesh):
    fine = Mesh(mesh.devices.reshape(NP, 2, mesh.shape["seq"]), ("p", "c", "seq"))
    rows = ("seq", "p", "c")
    in_specs = (P(rows, None),) * 5 + (P(rows), P(), P())
    return jax.shard_map(
        per_device, mesh=fine, in_specs=in_specs, out_specs=P(rows, None), check_vma=False
    )
```

time: 109 us -> 102 us (0.936)
  blocking collectives: 32.7 us -> 17.4 us
  waiting for transfers between devices: 36.3 us -> 44.4 us
  starting transfers between devices: 16.5 us -> 21.6 us
  local copies, waits for them, and re-layouts: 11.8 us -> 7.57 us
    all_to_all x2 -> x1, blocking collectives: 32.7 us -> 17.4 us  [per_device(): totals = lax.all_to_all(msg, 'p', split_axis=0, concat_axis=0, tiled=True)]
    all_to_all x2, waiting for transfers between devices: 36.3 us -> 42.9 us  [the longest x1 36.2 us: per_device(): lax.all_to_all(packed, ('p', 'c'), split_axis=0, concat_axis=0, tiled=True)]
    unnamed x35 -> x20, local copies, waits for them, and re-layouts: 11.4 us -> 7.26 us
    ppermute x0 -> x1, starting transfers between devices: none -> 3.85 us  [per_device(): other = lax.ppermute(other, 'c', [(0, 1), (1, 0)])]
    ppermute x0 -> x1, waiting for transfers between devices: none -> 1.54 us  [per_device(): other = lax.ppermute(other, 'c', [(0, 1), (1, 0)])]
    all_to_all x2, starting transfers between devices: 16.5 us -> 17.8 us  [the longest x1 13 us: per_device(): lax.all_to_all(packed, ('p', 'c'), split_axis=0, concat_axis=0, tiled=True)]
  transfers between devices with their start and end apart: 2 -> 3, of which waited for: 2 -> 3; matrix products, arithmetic and copies ran while one was open for 0% -> 0% of each run, Pallas kernels for 2% -> 2%
where the time goes in v2:
time: 102 us
  waiting for transfers between devices  44.4 us (44%)
  starting transfers between devices  21.6 us (21%)
  blocking collectives  17.4 us (17%)
  Pallas kernels  10.8 us (11%)
  local copies, waits for them, and re-layouts  7.57 us (7%)
    all_to_all x1, waiting for transfers between devices, per_device(): lax.all_to_all(packed, ('p', 'c'), split_axis=0, concat_axis=0, tiled=True)  36.2 us
    all_to_all x1, blocking collectives, per_device(): totals = lax.all_to_all(msg, 'p', split_axis=0, concat_axis=0, tiled=True)  17.4 us
    all_to_all x1, starting transfers between devices, per_device(): lax.all_to_all(packed, ('p', 'c'), split_axis=0, concat_axis=0, tiled=True)  13 us
    unnamed x20, local copies, waits for them, and re-layouts  7.26 us
    all_to_all x1, waiting for transfers between devices, per_device(): lax.all_to_all(entering, 'p', split_axis=0, concat_axis=0, tiled=True)  6.69 us
    all_to_all x1, starting transfers between devices, per_device(): lax.all_to_all(entering, 'p', split_axis=0, concat_axis=0, tiled=True)  4.76 us
    ppermute x1, starting transfers between devices, per_device(): other = lax.ppermute(other, 'c', [(0, 1), (1, 0)])  3.85 us
    pallas_call x1, Pallas kernels, per_device(): pl.pallas_call(state_kernel, out_shape=(sds((2 * T, HW), BF16), sds((2 *...  3.34 us
  transfers between devices with their start and end apart: 3, of which 3 were waited for; matrix products, arithmetic and copies ran while one was open for 0% of the time, Pallas kernels for 2%

profile of v2, /device:TPU:1, one launch (start us, length us, event | category | flops | bytes accessed | tf_op | source)
XLA Modules:
  0.0 101.9 jit_solution(17396344097651530292)
XLA Ops:
  0.0 0.0 copy-start
  0.0 1.2 %copy-done = bf16[128,4096]{1,0:T(8,128)(2,1)S(1)} copy-done((bf16[128,4096]{1,0:T(8,128)(2,1)S(1)}, bf16[128,4096]{1,0:T(8,128)(2,1)}, u32[]{:S(2)}) %copy-start) | copy-done | bytes 1048600
  1.2 0.0 copy-start.1
  1.2 0.9 copy-done.1
  2.1 0.0 copy-start.2
  2.1 0.9 copy-done.2
  3.0 0.0 copy-start.3
  3.0 0.7 copy-done.3
  3.8 0.0 copy-start.4
  3.8 0.7 copy-done.4
  4.4 0.0 copy-start.5
  4.4 0.7 copy-done.5
  5.1 2.6 %pack.1 = bf16[64,88,128]{2,1,0:T(8,128)(2,1)} custom-call(bf16[128,4096]{1,0:T(8,128)(2,1)S(1)} %copy-done, bf16[128,512]{1,0:T(8,128)(2,1)S(1)} %copy-done.1, bf16[128,512]{1,0:T(8,128)(2,1)S(1)} %copy-done.2, bf16[64,128]{1,0:T(8,128)(2,1)S(1)} %bitcast.4, s32[1,128]{1,0:T(1,128)S(1)} %copy-done.4, s32[1,128]{1,0:T(1,128)S(1)} %bitcast.5), custom_call_target="tpu_custom_call" | custom-call | tf_op jit(solution)/shard_map/pack/pallas_call | solution.py:262
  7.7 0.0 copy-start.8
  7.7 13.0 %all-to-all-start = ((bf16[64,88,128]{2,1,0:T(8,128)(2,1)}), bf16[64,88,128]{2,1,0:T(8,128)(2,1)S(1)}, u32[]{:S(2)}, u32[]{:S(2)}) async-start(bf16[64,88,128]{2,1,0:T(8,128)(2,1)} %pack.1), calls=%async_computation | async-start | bytes 2883584 | tf_op jit(solution)/shard_map/all_to_all | solution.py:278
  20.7 0.0 copy-done.8
  20.7 0.1 dynamic_slice.6
  20.8 0.1 maximum_bitcast_fusion.rate_ref
  20.9 0.0 copy-start.9
  20.9 36.2 %all-to-all-done.arrived_ref = bf16[64,88,128]{2,1,0:T(8,128)(2,1)S(1)} async-done(((bf16[64,88,128]{2,1,0:T(8,128)(2,1)}), bf16[64,88,128]{2,1,0:T(8,128)(2,1)S(1)}, u32[]{:S(2)}, u32[]{:S(2)}) %all-to-all-start) | async-done | bytes 1441824 | tf_op jit(solution)/shard_map/all_to_all | solution.py:278
  57.1 3.3 %state.1 = (bf16[256,2048]{1,0:T(8,128)(2,1)S(1)}, bf16[256,512]{1,0:T(8,128)(2,1)S(1)}, f32[128,128]{1,0:T(8,128)S(1)}, f32[128,128]{1,0:T(8,128)S(1)}, f32[128...) custom-call(bf16[64,88,128]{2,1,0:T(8,128)(2,1)S(1)} %all-to-all-don, ...), custom_call_target="tpu_custom_call" | custom-call | tf_op jit(solution)/shard_map/state/pallas_call | solution.py:282
  60.4 0.0 copy-start.6
  60.4 1.0 copy-done.6
  61.4 17.4 %all_to_all.15.in_ref = bf16[32,40,128]{2,1,0:T(8,128)(2,1)S(1)} all-to-all(bf16[32,40,128]{2,1,0:T(8,128)(2,1)S(1)} %get-tuple-element.24), channel_id=1, replica_groups=mesh['p'=32,'c'=2,'seq'=4] {'p'}, dimensions={0} | all-to-all | bytes 655360 | tf_op jit(solution)/shard_map/all_to_all | solution.py:299
  78.8 0.8 chips.1
  79.6 4.8 %all-to-all-start.2 = ((bf16[32,32,128]{2,1,0:T(8,128)(2,1)}), bf16[32,32,128]{2,1,0:T(8,128)(2,1)S(1)}, u32[]{:S(2)}, u32[]{:S(2)}) async-start(bf16[32,32,128]{2,1,0:T(8,128)(2,1)} %chips.1), calls=%async_computation.2 | async-start | bytes 524288 | tf_op jit(solution)/shard_map/all_to_all | solution.py:310
  84.3 0.0 copy-done.9
  84.4 0.1 dynamic_slice.7
  84.4 0.1 broadcast_in_dim.7
  84.5 0.1 reshape_reshape.3.skip_ref
  84.6 0.0 copy-start.7
  84.6 1.2 %copy-done.7 = bf16[256,2048]{1,0:T(8,128)(2,1)S(1)} copy-done((bf16[256,2048]{1,0:T(8,128)(2,1)S(1)}, bf16[256,2048]{1,0:T(8,128)(2,1)}, u32[]{:S(2)}) %copy-start.7) | copy-done | bytes 1048600
  85.8 2.2 %local.1.partial_ref = f32[256,2048]{1,0:T(8,128)S(1)} custom-call(bf16[256,2048]{1,0:T(8,128)(2,1)S(1)} %copy-done.7, bf16[256,512]{1,0:T(8,128)(2,1)S(1)} %get-tuple-element.17.bc_ref, f32[128,128]{1,0:T(8,128)S(1)} %get-tuple-element.18.cum_ref, f32[128,128]{1,0:T(8,128)S(1)} %get-tuple-element.19.key_ref, f32[128,128]{1,0:T(8,128)S(1)} %get-tuple-element.20.entry_ref, ...), custom_call_target="tpu_custom_call" | custom-call | flops 2000000000 | bytes 6000000 | tf_op jit(solution)/shard_map/local/pallas_call | solution.py:300
  88.1 6.7 %all-to-all-done.2.h_ref = bf16[32,32,128]{2,1,0:T(8,128)(2,1)S(1)} async-done(((bf16[32,32,128]{2,1,0:T(8,128)(2,1)}), bf16[32,32,128]{2,1,0:T(8,128)(2,1)S(1)}, u32[]{:S(2)}, u32[]{:S(2)}) %all-to-all-start.2) | async-done | bytes 262176 | tf_op jit(solution)/shard_map/all_to_all | solution.py:310
  94.7 0.8 final.1
  95.5 3.8 %collective-permute-start = (bf16[128,2048]{1,0:T(8,128)(2,1)S(1)}, bf16[128,2048]{1,0:T(8,128)(2,1)S(1)}, u32[]{:S(2)}, u32[]{:S(2)}) collective-permute-start(bf16[128,2048]{1,0:T(8,128)(2,1)S(1)} %get-tuple-element.26), channel_id=1, source_target_pairs={{0,4},{4,0},{1,5},{5,1},{2,6},{6,2},{3,7},{7,3},{8,12},{12,8},{9,1... | collective-permute-start | bytes 1572872 | tf_op jit(solution)/shard_map/ppermute | solution.py:317
  99.4 1.5 %collective-permute-done.other_ref = bf16[128,2048]{1,0:T(8,128)(2,1)S(1)} collective-permute-done((bf16[128,2048]{1,0:T(8,128)(2,1)S(1)}, bf16[128,2048]{1,0:T(8,128)(2,1)S(1)}, u32[]{:S(2)}, u32[]{:S(2)}) %collective-permute-start) | collective-permute-done | bytes 524320 | tf_op jit(solution)/shard_map/ppermute | solution.py:317
  100.9 1.0 %join.1 = bf16[128,4096]{1,0:T(8,128)(2,1)} custom-call(bf16[128,2048]{1,0:T(8,128)(2,1)S(1)} %get-tuple-element.25.mine_ref, bf16[128,2048]{1,0:T(8,128)(2,1)S(1)} %collective-permute-done.other_ref), custom_call_target="tpu_custom_call" | custom-call | tf_op jit(solution)/shard_map/join/pallas_call | solution.py:318
  (1 shorter events, 0.0 us)
Async XLA Ops:
  0.0 1.2 %copy-start = (bf16[128,4096]{1,0:T(8,128)(2,1)S(1)}, bf16[128,4096]{1,0:T(8,128)(2,1)}, u32[]{:S(2)}) copy-start(bf16[128,4096]{1,0:T(8,128)(2,1)} %x_hbm.1) | copy-start | bytes 3145732
  1.2 0.9 copy-start.1
  2.1 0.9 copy-start.2
  3.0 0.7 copy-start.3
  3.8 0.7 copy-start.4
  4.4 0.7 copy-start.5
  7.7 13.0 %copy-start.8 = (f32[64]{0:T(128)S(1)}, f32[64]{0:T(128)}, u32[]{:S(2)}) copy-start(f32[64]{0:T(128)} %param.14) | copy-start | bytes 772
  7.7 49.4 %all-to-all-start = ((bf16[64,88,128]{2,1,0:T(8,128)(2,1)}), bf16[64,88,128]{2,1,0:T(8,128)(2,1)S(1)}, u32[]{:S(2)}, u32[]{:S(2)}) async-start(bf16[64,88,128]{2,1,0:T(8,128)(2,1)} %pack.1), calls=%async_computation | async-start | bytes 2883584 | tf_op jit(solution)/shard_map/all_to_all | solution.py:278
  20.9 63.5 %copy-start.9 = (f32[64]{0:T(128)S(1)}, f32[64]{0:T(128)}, u32[]{:S(2)}) copy-start(f32[64]{0:T(128)} %param.15) | copy-start | bytes 772
  60.4 1.0 copy-start.6
  79.6 15.2 %all-to-all-start.2 = ((bf16[32,32,128]{2,1,0:T(8,128)(2,1)}), bf16[32,32,128]{2,1,0:T(8,128)(2,1)S(1)}, u32[]{:S(2)}, u32[]{:S(2)}) async-start(bf16[32,32,128]{2,1,0:T(8,128)(2,1)} %chips.1), calls=%async_computation.2 | async-start | bytes 524288 | tf_op jit(solution)/shard_map/all_to_all | solution.py:310
  84.6 1.2 %copy-start.7 = (bf16[256,2048]{1,0:T(8,128)(2,1)S(1)}, bf16[256,2048]{1,0:T(8,128)(2,1)}, u32[]{:S(2)}) copy-start(bf16[256,2048]{1,0:T(8,128)(2,1)} %copy-done.6) | copy-start | bytes 3145732
  95.5 5.4 %collective-permute-start = (bf16[128,2048]{1,0:T(8,128)(2,1)S(1)}, bf16[128,2048]{1,0:T(8,128)(2,1)S(1)}, u32[]{:S(2)}, u32[]{:S(2)}) collective-permute-start(bf16[128,2048]{1,0:T(8,128)(2,1)S(1)} %get-tuple-element.26), channel_id=1, source_target_pairs={{0,4},{4,0},{1,5},{5,1},{2,6},{6,2},{3,7},{7,3},{8,12},{12,8},{9,1... | collective-permute-start | bytes 1572872 | tf_op jit(solution)/shard_map/ppermute | solution.py:317

commit v3 on v2

v3 whole, which is shorter than its diff:
```python
import jax
import jax.numpy as jnp
from jax import lax
from jax.experimental import pallas as pl
from jax.experimental.pallas import tpu as pltpu
from jax.sharding import Mesh, PartitionSpec as P

F32 = jnp.float32
BF16 = jnp.bfloat16
I32 = jnp.int32
T = 128
NX, NZ = 4, 8
NP = NX * NZ
HG = 8
HP = 64
N = 64
GW = HG * HP
HH = 32
HW = HH * HP
MSG = 88
PARTS = 4


def iota(shape, dim):
    return lax.broadcasted_iota(I32, shape, dim)


def dot(a, b):
    return jnp.dot(a, b, preferred_element_type=F32)


def dot_nt(a, b):
    return lax.dot_general(a, b, (((1,), (1,)), ((), ())), preferred_element_type=F32)


def params(mib):
    return pltpu.CompilerParams(vmem_limit_bytes=mib * 1024 * 1024)


def softplus(v):
    return jnp.maximum(v, 0.0) + jnp.log1p(jnp.exp(-jnp.abs(v)))


def pack_kernel(
    x_hbm, b_hbm, c_hbm, dt_hbm, order_hbm, reset_hbm, out_hbm,
    x_ref, b_ref, c_ref, dt_ref, order_ref, reset_ref, out_ref, sems, out_sems,
):
    pairs = [(order_hbm, order_ref), (reset_hbm, reset_ref), (dt_hbm, dt_ref)]
    span = T // PARTS
    for part in range(PARTS):
        rows = pl.ds(span * part, span)
        pairs += [(src.at[rows], dst.at[rows]) for src, dst in ((b_hbm, b_ref), (c_hbm, c_ref), (x_hbm, x_ref))]
    copies = [pltpu.make_async_copy(s, d, sems.at[n]) for n, (s, d) in enumerate(pairs)]
    for copy in copies:
        copy.start()
    row, col = iota((4 * span, 4 * span), 0), iota((4 * span, 4 * span), 1)
    pick = (col // span == (row % 16) // 4) & (col % span == (row // 16) * 4 + row % 4)
    pick = pick.astype(BF16)
    lane, head = iota((256, 64), 0), iota((256, 64), 1)
    spread = (lane % T < 64) & (head == (lane // T) * HH + lane % HH)
    to, row = iota((256, T), 0), iota((256, T), 1)
    own_row = ((row // 4 == to // 8) & (row % 2 == to % 8)).astype(BF16)
    own_span = (row // 2) % 2 == (to % T) // HH
    upto = (iota((T, T), 0) <= iota((T, T), 1)).astype(BF16)
    own = iota((8, T), 1) % 8 == iota((8, T), 0)
    place = iota((T, T), 1) - iota((T, T), 0) // 8
    to_part, part = iota((256, 192), 0), iota((256, 192), 1)
    rr = to_part % 8 - 2
    chosen = (rr >= 0) & (part // 64 == rr // 2) & (part % 64 == 2 * (to_part // 8) + rr % 2)
    chosen = chosen.astype(BF16)
    of_chip = (iota((T, T), 0) // 4 == iota((T, T), 1)).astype(F32)
    for copy in copies[:6]:
        copy.wait()
    sums = jnp.dot(
        softplus(dt_ref[...].astype(F32)), of_chip, preferred_element_type=F32, precision=lax.Precision.HIGHEST
    )
    high = sums.astype(BF16)
    mid = (sums - high.astype(F32)).astype(BF16)
    low = (sums - high.astype(F32) - mid.astype(F32)).astype(BF16)
    sums = dot(chosen, jnp.concatenate([high, mid, low], axis=0))
    wide = jnp.where(own_span, dot(spread.astype(BF16), dt_ref[...]), 0.0).astype(BF16)
    steps = dot_nt(own_row, wide)
    resets = jnp.broadcast_to(reset_ref[...].astype(F32), (8, T)).astype(BF16)
    count = dot(resets, upto)
    order = jnp.broadcast_to(order_ref[...].astype(F32), (8, T))
    extra = dot(jnp.where(own, order, 0.0).astype(BF16), (place == 64).astype(BF16))
    extra += dot(jnp.where(own, count, 0.0).astype(BF16), (place == 80).astype(BF16))
    sent = []
    for part in range(PARTS):
        if part > 0:
            for copy in copies[3 + 3 * part : 6 + 3 * part]:
                copy.wait()
        rows = pl.ds(span * part, span)
        tiles = []
        for c in range(2):
            for q in range(4):
                tiles.append([x_ref[rows, pl.ds(HW * c + 512 * q + T * j, T)] for j in range(4)])
            tiles.append(
                [b_ref[rows, pl.ds(256 * c, T)], b_ref[rows, pl.ds(256 * c + T, T)],
                 c_ref[rows, pl.ds(256 * c, T)], c_ref[rows, pl.ds(256 * c + T, T)]]
            )
        right = jnp.concatenate([jnp.concatenate(t, axis=0) for t in tiles], axis=1)
        got = dot(pick, right).astype(BF16)
        for p in range(NP // PARTS):
            z, x = NZ // PARTS * part + p // NX, p % NX
            at = 8 * (NP // PARTS * part + p)
            for c in range(2):
                to = 2 * x + c
                for q in range(5):
                    lanes = slice(T * (5 * c + q), T * (5 * c + q) + T)
                    out_ref[to, z, pl.ds(16 * q, 16), :] = got[16 * p : 16 * p + 16, lanes]
                m = 8 * (16 * c + (NZ * x + z) // 2)
                tail = steps[at : at + 8, T * c : T * c + T] + sums[m : m + 8] + extra
                out_ref[to, z, pl.ds(80, 8), :] = tail.astype(BF16)
        here = pl.ds(NZ // PARTS * part, NZ // PARTS)
        sent.append(pltpu.make_async_copy(out_ref.at[:, here], out_hbm.at[:, here], out_sems.at[part]))
        sent[-1].start()
    for copy in sent:
        copy.wait()


def expander():
    return (iota((T, HW), 0) % HH == iota((T, HW), 1) // HP).astype(BF16)


def two_parts(v):
    high = v.astype(BF16).astype(F32)
    low = v - high
    return jnp.where(iota(v.shape, 1) < 64, high, pltpu.roll(low, 64, 1))


def of_span(parts, i):
    return jnp.where((iota(parts.shape, 1) % 64) // HH == i, parts, 0.0).astype(BF16)


def state_kernel(
    arrived_hbm, rate_ref, x_ref, bc_ref, cum_ref, key_ref, entry_ref, carry_ref, count_ref, hin_ref, msg_ref,
    sums_ref, resets_ref, arrived_ref, sems,
):
    copies = []
    for n, rows in enumerate((pl.ds(80, 8), pl.ds(0, 80))):
        copies.append(pltpu.make_async_copy(arrived_hbm.at[:, rows], arrived_ref.at[:, rows], sems.at[n]))
        copies[-1].start()
    plane, column = lax.axis_index("z"), lax.axis_index("x")
    copies[0].wait()
    tails = jnp.concatenate(
        [arrived_ref[(column * 2 + i) * NZ + plane, pl.ds(80, 8), :].astype(F32) for i in range(2)], axis=0
    ).astype(BF16)
    row, col = iota((256, 16), 0), iota((256, 16), 1)
    sel = (col == (row // T) * 8 + row % 8).astype(BF16)
    spread = dot(sel, tails)
    lane = iota((256, T), 1)
    block = (iota((256, T), 0) % T) // 8
    spread = jnp.where((lane == 64 + block) | (lane == 80 + block), spread, 0.0).astype(BF16)
    src, dst = iota((T, 256), 0), iota((T, 256), 1)
    gather = ((src >= 64) & (src < 80) & (dst < T)) | ((src >= 80) & (src < 96) & (dst >= T))
    both = dot(spread, gather.astype(BF16))
    order = both[:, :T].astype(I32)
    count = both[:, T:]
    count_ref[...] = count
    source = order >> 1
    source = ((source & (NZ - 1)) << 3) + (source >> 3)
    target = (source << 2) + ((iota((256, T), 0) >> 7) << 1) + (order & 1)
    perm = jnp.concatenate(
        [jnp.where(lane + T * m == target, 1.0, 0.0).astype(BF16) for m in range(2)], axis=1
    )
    top = iota((NP, 8, T), 1) < 4
    for copy in copies[1:]:
        copy.wait()
    tiles = [[] for _ in range(4)]
    for q in range(5):
        here = arrived_ref[:, pl.ds(16 * q, 16), :].astype(F32).reshape(NP, 2, 2, 8, T)
        for half in range(2):
            even, odd = here[:, 0, half], here[:, 1, half]
            low = jnp.where(top, even, pltpu.roll(odd, 4, 1))
            high = jnp.where(top, pltpu.roll(even, 4, 1), odd)
            tiles[2 * half].append(low.reshape(256, T))
            tiles[2 * half + 1].append(high.reshape(256, T))
    for j in range(4):
        rows = dot(perm, jnp.concatenate(tiles[j], axis=1).astype(BF16)).astype(BF16)
        for q in range(4):
            x_ref[:, pl.ds(T * (4 * q + j), T)] = rows[:, T * q : T * q + T]
        bc_ref[:, pl.ds(T * j, T)] = rows[:, T * 4 :]
    steps_in = arrived_ref[:, pl.ds(80, 8), :].astype(F32).reshape(512, T).astype(BF16)
    target = (source << 3) + (order & 1)
    small = jnp.concatenate(
        [jnp.where(lane + T * m == target, 1.0, 0.0).astype(BF16) for m in range(4)], axis=1
    )
    raw = dot(small, steps_in)
    first = iota((T, T), 1) < HH
    raw = jnp.where(first, raw[:T], raw[T:])
    cnt = jnp.where(first, count[:T], count[T:])
    step = softplus(raw)
    logd = -step * rate_ref[...]
    lower = (iota((T, T), 0) >= iota((T, T), 1)).astype(F32)
    cum = jnp.dot(lower, logd, preferred_element_type=F32, precision=lax.Precision.HIGHEST)
    cum_ref[...] = cum
    key_ref[...] = (cum - jnp.log(step)).T
    last = cum[T - 1 : T]
    last_cnt = cnt[T - 1 : T]
    entry = jnp.where(cnt == 0.0, jnp.exp(cum), 0.0)
    entry_ref[...] = entry
    decay = jnp.where(last_cnt == 0.0, jnp.exp(last), 0.0)
    decay = jnp.broadcast_to(decay, (8, T))
    before = jnp.where(iota((8, T), 1) < HH, 1.0, pltpu.roll(decay, HH, 1))
    carry_ref[...] = entry * before[:1]
    coef = two_parts(jnp.where(cnt == last_cnt, jnp.exp(last - cum) * step, 0.0))
    e = expander()
    decay = two_parts(decay)
    decay = dot(of_span(decay, 1), e)[:1]
    weighted = []
    for i in range(2):
        here = pl.ds(T * i, T)
        weighted.append((x_ref[here, :].astype(F32) * dot(of_span(coef, i), e)).astype(BF16))
    for tile in range(2):
        b = [bc_ref[pl.ds(T * i, T), pl.ds(T * tile, T)].astype(F32).T.astype(BF16) for i in range(2)]
        for half in range(2):
            g = 2 * tile + half
            lanes = slice(GW * g, GW * g + GW)
            states = [dot(b[i][N * half : N * half + N], weighted[i][:, lanes]) for i in range(2)]
            hin_ref[:, lanes] = states[0].astype(BF16)
            h = (decay[:, lanes] * states[0] + states[1]).astype(BF16)
            for pair in range(4):
                for k in range(2):
                    m = (4 * g + pair) * 2 + k
                    msg_ref[m, pl.ds(0, 32), :] = h[32 * k : 32 * k + 32, T * pair : T * pair + T]
    tails = arrived_ref[:, pl.ds(80, 8), :].astype(F32)
    sums_ref[...] = jnp.sum(tails, axis=0)
    chip, source = iota((NP, 512), 0), iota((NP, 512), 1) >> 3
    ends = ((source & (NZ - 1)) * NX + (source >> 4) == chip) & ((iota((NP, 512), 1) & 7) == 7)
    resets_ref[...] = dot(ends.astype(BF16), steps_in)


def local_kernel(
    x_ref, bc_ref, cum_ref, key_ref, entry_ref, carry_ref, count_ref, hin_ref, skip_ref,
    sums_ref, resets_ref, pair_ref, mine_ref, swap_ref, decay_ref, out_ref,
):
    core = lax.axis_index("c")
    there = pl.ds(pl.multiple_of(T * (1 - core), T), T)
    e = expander()
    entry = dot(of_span(two_parts(entry_ref[...]), 1), e)
    causal = iota((T, T), 0) >= iota((T, T), 1)
    left = iota((T, T), 1) < HP
    for i in range(2):
        here = pl.ds(T * i, T)
        count = count_ref[here, :]
        keep = causal & (count == count.T)
        for g in range(4):
            tile, half = g // 2, g % 2
            b = bc_ref[here, pl.ds(T * tile, T)][:, N * half : N * half + N]
            c = bc_ref[here, pl.ds(2 * T + T * tile, T)][:, N * half : N * half + N]
            scores = dot_nt(c, b)
            if i == 1:
                lanes = pl.ds(GW * g, GW)
                carried = dot(c, hin_ref[:, lanes]) * entry[:, GW * g : GW * g + GW]
            for pair in range(4):
                weights = []
                for h in (2 * pair, 2 * pair + 1):
                    col = HH * i + HG * g + h
                    gap = cum_ref[:, col : col + 1] - key_ref[col : col + 1, :]
                    weights.append((jnp.exp(jnp.where(keep, gap, -jnp.inf)) * scores).astype(BF16))
                lanes = pl.ds(GW * g + T * pair, T)
                x = x_ref[here, lanes]
                zero = jnp.zeros_like(x)
                both = jnp.concatenate([jnp.where(left, x, zero), jnp.where(left, zero, x)], axis=0)
                out = dot(jnp.concatenate(weights, axis=1), both) + skip_ref[:, lanes] * x.astype(F32)
                if i == 1:
                    out += carried[:, T * pair : T * pair + T]
                out_ref[here, lanes] = out
    mine_ref[...] = out_ref[pl.ds(pl.multiple_of(T * core, T), T), :]
    other = out_ref[there, :]
    high = other.astype(BF16)
    swap_ref[:, pl.ds(0, HW)] = high
    swap_ref[:, pl.ds(HW, HW)] = (other - high.astype(F32)).astype(BF16)
    swap_ref[:, pl.ds(2 * HW, 2 * T)] = bc_ref[there, pl.ds(2 * T, 2 * T)]
    swap_ref[:, pl.ds(2 * HW + 2 * T, T)] = of_span(two_parts(carry_ref[...]), 1 - core)
    sums = sums_ref[pl.ds(2, 2), :] + sums_ref[pl.ds(4, 2), :] + sums_ref[pl.ds(6, 2), :]
    sums = jnp.concatenate([sums, jnp.zeros((T - 2, T), F32)], axis=0).T[:NP]
    sums = jnp.where(iota((NP, T), 1) < HP, sums[:, 0:1], sums[:, 1:2])
    decay_ref[...] = jnp.where(resets_ref[:, 95:96] == 0.0, jnp.exp(-sums * pair_ref[...]), 0.0)


def scan_kernel(in_ref, decay_ref, out_ref):
    h = jnp.zeros((32, T), F32)
    for p in range(NP):
        at = (p % NX) * NZ + p // NX
        out_ref[at] = h.astype(BF16)
        h = decay_ref[pl.ds(p, 1), :] * h + in_ref[at].astype(F32)


def carried(c, h_ref, g, scale):
    state = jnp.concatenate(
        [jnp.concatenate([h_ref[8 * g + 2 * p], h_ref[8 * g + 2 * p + 1]], axis=0) for p in range(4)], axis=1
    )
    return dot(c, state) * scale[:, GW * g : GW * g + GW]


def mine_kernel(partial_ref, bc_ref, carry_ref, h_ref, out_ref):
    core = lax.axis_index("c")
    scale = dot(of_span(two_parts(carry_ref[...]), core), expander())
    cs = bc_ref[pl.ds(pl.multiple_of(T * core, T), T), pl.ds(2 * T, 2 * T)]
    for g in range(4):
        lanes = pl.ds(GW * g, GW)
        inter = carried(cs[:, N * g : N * g + N], h_ref, g, scale)
        out_ref[:, lanes] = (partial_ref[:, lanes] + inter).astype(BF16)


def final_kernel(mine_ref, swap_ref, h_ref, out_hbm, other_ref, sems):
    core = lax.axis_index("c")

    def copy(src, n, half):
        return pltpu.make_async_copy(src, out_hbm.at[:, pl.ds(HW * half, HW)], sems.at[n])

    for k in range(2):

        @pl.when(core == k)
        def _():
            copy(mine_ref, 0, k).start()

    scale = dot(swap_ref[:, pl.ds(2 * HW + 2 * T, T)], expander())
    cs = swap_ref[:, pl.ds(2 * HW, 2 * T)]
    for g in range(4):
        lanes = pl.ds(GW * g, GW)
        partial = swap_ref[:, lanes].astype(F32) + swap_ref[:, pl.ds(HW + GW * g, GW)].astype(F32)
        inter = carried(cs[:, N * g : N * g + N], h_ref, g, scale)
        other_ref[:, lanes] = (partial + inter).astype(BF16)
    for k in range(2):

        @pl.when(core == k)
        def _():
            copy(other_ref, 1, 1 - k).start()
            copy(mine_ref, 0, k).wait()
            copy(other_ref, 1, 1 - k).wait()


def per_device(x, b, c, dt, order, resets, rate, skip):
    core = lax.axis_index("c")
    sds = jax.ShapeDtypeStruct
    hbm = pl.BlockSpec(memory_space=pltpu.HBM)
    packed = pl.pallas_call(
        pack_kernel,
        out_shape=sds((2 * NX, NZ, MSG, T), BF16),
        in_specs=[hbm] * 6,
        out_specs=hbm,
        scratch_shapes=[
            pltpu.VMEM(x.shape, BF16),
            pltpu.VMEM(b.shape, BF16),
            pltpu.VMEM(c.shape, BF16),
            pltpu.VMEM(dt.shape[::-1], BF16),
            pltpu.VMEM((1, T), I32),
            pltpu.VMEM((1, T), I32),
            pltpu.VMEM((2 * NX, NZ, MSG, T), BF16),
            pltpu.SemaphoreType.DMA((3 + 3 * PARTS,)),
            pltpu.SemaphoreType.DMA((PARTS,)),
        ],
        compiler_params=params(56),
        name="pack",
    )(x, b, c, dt.T, order, resets.reshape(1, T))
    packed = packed.reshape(2 * NP, MSG, T)
    arrived = lax.all_to_all(packed, ("x", "c", "z"), split_axis=0, concat_axis=0, tiled=True)
    mine = lax.dynamic_slice_in_dim(rate, core * HH, HH)
    rate_row = jnp.concatenate([mine, mine, jnp.zeros((64,), F32)]).reshape(1, T)
    pair = (lax.axis_index("x") * NZ + lax.axis_index("z")) // 2 * 2
    pair_row = jnp.repeat(lax.dynamic_slice_in_dim(rate, core * HH + pair, 2), HP).reshape(1, T)
    skip_row = jnp.repeat(lax.dynamic_slice_in_dim(skip, core * HH, HH), HP).reshape(1, HW)
    xs, bc, cum, key, entry, carry, count, hin, msg, sums, ends = pl.pallas_call(
        state_kernel,
        out_shape=(
            sds((2 * T, HW), BF16),
            sds((2 * T, 4 * T), BF16),
            sds((T, T), F32),
            sds((T, T), F32),
            sds((T, T), F32),
            sds((T, T), F32),
            sds((2 * T, T), F32),
            sds((N, HW), BF16),
            sds((NP, 32, T), BF16),
            sds((8, T), F32),
            sds((NP, T), F32),
        ),
        in_specs=[hbm, pl.BlockSpec(memory_space=pltpu.VMEM)],
        scratch_shapes=[pltpu.VMEM((2 * NP, MSG, T), BF16), pltpu.SemaphoreType.DMA((2,))],
        compiler_params=params(51),
        name="state",
    )(arrived, rate_row)
    totals = lax.all_to_all(msg, ("x", "z"), split_axis=0, concat_axis=0, tiled=True)
    partial, swap, decays = pl.pallas_call(
        local_kernel,
        out_shape=(sds((T, HW), F32), sds((T, 2 * HW + 3 * T), BF16), sds((NP, T), F32)),
        scratch_shapes=[pltpu.VMEM((2 * T, HW), F32)],
        compiler_params=params(20),
        cost_estimate=pl.CostEstimate(flops=2_000_000_000, bytes_accessed=6_000_000, transcendentals=1_100_000),
        name="local",
    )(xs, bc, cum, key, entry, carry, count, hin, skip_row, sums, ends, pair_row)
    swap = lax.ppermute(swap, "c", [(0, 1), (1, 0)])
    entering = pl.pallas_call(
        scan_kernel, out_shape=sds((NP, 32, T), BF16), compiler_params=params(16), name="chips"
    )(totals, decays)
    states = lax.all_to_all(entering, ("x", "z"), split_axis=0, concat_axis=0, tiled=True)
    other = lax.ppermute(states, "c", [(0, 1), (1, 0)])
    own = pl.pallas_call(
        mine_kernel, out_shape=sds((T, HW), BF16), compiler_params=params(20), name="mine"
    )(partial, bc, carry, states)
    return pl.pallas_call(
        final_kernel,
        out_shape=sds((T, 2 * HW), BF16),
        in_specs=[pl.BlockSpec(memory_space=pltpu.VMEM)] * 3,
        out_specs=hbm,
        scratch_shapes=[pltpu.VMEM((T, HW), BF16), pltpu.SemaphoreType.DMA((2,))],
        compiler_params=params(20),
        name="final",
    )(own, swap, other)


def solution(mesh):
    fine = Mesh(mesh.devices.reshape(NZ, NX, 2, mesh.shape["seq"]), ("z", "x", "c", "seq"))
    rows = ("seq", "z", "x", "c")
    in_specs = (P(rows, None),) * 5 + (P(rows), P(), P())
    return jax.shard_map(
        per_device, mesh=fine, in_specs=in_specs, out_specs=P(rows, None), check_vma=False
    )
```

time: 102 us -> 94.6 us (0.927)
  local copies, waits for them, and re-layouts: 7.57 us -> 0.54 us
  waiting for transfers between devices: 44.4 us -> 41.6 us
  Pallas kernels: 10.8 us -> 12.9 us
  starting transfers between devices: 21.6 us -> 23.3 us
  blocking collectives: 17.4 us -> 15.8 us
    unnamed x20 -> x4, local copies, waits for them, and re-layouts: 7.26 us -> 0.01 us
    pallas_call x4, Pallas kernels: 6.64 us -> 8.97 us  [the longest x1 3.77 us: per_device(): pl.pallas_call(local_kernel, out_shape=(sds((T, HW), F32), sds((T, 2 * HW...]
    all_to_all x2, waiting for transfers between devices: 42.9 us -> 40.9 us  [the longest x1 35.9 us: per_device(): lax.all_to_all(packed, ('x', 'c', 'z'), split_axis=0, concat_axis=0, tile...]
    all_to_all x1, blocking collectives: 17.4 us -> 15.8 us  [per_device(): lax.all_to_all(entering, ('x', 'z'), split_axis=0, concat_axis=0, tiled=T...]
    ppermute x1 -> x2, starting transfers between devices: 3.85 us -> 4.55 us  [the longest x1 3.6 us: per_device(): other = lax.ppermute(states, 'c', [(0, 1), (1, 0)])]
  transfers between devices with their start and end apart: 3 -> 4, of which waited for: 3 -> 3; matrix products, arithmetic and copies ran while one was open for 0% -> 1% of each run, Pallas kernels for 2% -> 5%
where the time goes in v3:
time: 94.6 us; the launch traced here: 94.3 us
  waiting for transfers between devices  41.6 us (44%)
  starting transfers between devices  23.3 us (25%)
  blocking collectives  15.8 us (17%)
  Pallas kernels  12.9 us (14%)
    all_to_all x1, waiting for transfers between devices, per_device(): lax.all_to_all(packed, ('x', 'c', 'z'), split_axis=0, concat_axis=0, tile...  35.9 us
    all_to_all x1, blocking collectives, per_device(): lax.all_to_all(entering, ('x', 'z'), split_axis=0, concat_axis=0, tiled=T...  15.8 us
    all_to_all x1, starting transfers between devices, per_device(): lax.all_to_all(packed, ('x', 'c', 'z'), split_axis=0, concat_axis=0, tile...  13.2 us
    all_to_all x1, starting transfers between devices, per_device(): lax.all_to_all(msg, ('x', 'z'), split_axis=0, concat_axis=0, tiled=True)  5.59 us
    all_to_all x1, waiting for transfers between devices, per_device(): lax.all_to_all(msg, ('x', 'z'), split_axis=0, concat_axis=0, tiled=True)  4.96 us
    pallas_call x1, Pallas kernels, per_device(): pl.pallas_call(state_kernel, out_shape=(sds((2 * T, HW), BF16), sds((2 *...  3.89 us
    pallas_call x1, Pallas kernels, per_device(): pl.pallas_call(local_kernel, out_shape=(sds((T, HW), F32), sds((T, 2 * HW...  3.77 us
    ppermute x1, starting transfers between devices, per_device(): other = lax.ppermute(states, 'c', [(0, 1), (1, 0)])  3.6 us
  transfers between devices with their start and end apart: 4, of which 3 were waited for; matrix products, arithmetic and copies ran while one was open for 1% of the time, Pallas kernels for 5%

profile of v3, /device:TPU:1, one launch (start us, length us, event | category | flops | bytes accessed | tf_op | source)
XLA Modules:
  0.0 94.3 jit_solution(5950312781148027805)
XLA Ops:
  0.0 3.5 %pack.1 = bf16[8,8,88,128]{3,2,1,0:T(8,128)(2,1)} custom-call(bf16[128,4096]{1,0:T(8,128)(2,1)} %x_hbm.1, bf16[128,512]{1,0:T(8,128)(2,1)} %b_hbm.1, bf16[128,512]{1,0:T(8,128)(2,1)} %c_hbm.1, bf16[64,128]{1,0:T(8,128)(2,1)} %bitcast.6, s32[1,128]{1,0:T(1,128)} %order_hbm.1, s32[1,128]{1,0:T(1,128)} %bitcast.7), custom_call_target="tpu_custom_call" | custom-call | tf_op jit(solution)/shard_map/pack/pallas_call | solution.py:340
  3.5 0.0 copy-start
  3.5 0.0 copy-start.1
  3.5 13.2 %all-to-all-start = ((bf16[64,88,128]{2,1,0:T(8,128)(2,1)}), bf16[64,88,128]{2,1,0:T(8,128)(2,1)}, u32[]{:S(2)}, u32[]{:S(2)}) async-start(bf16[64,88,128]{2,1,0:T(8,128)(2,1)} %bitcast.5), calls=%async_computation | async-start | bytes 2883584 | tf_op jit(solution)/shard_map/all_to_all | solution.py:360
  16.7 0.0 copy-done
  16.7 0.1 dynamic_slice.11
  16.8 0.1 dynamic_slice.9
  16.8 0.0 copy-done.1
  16.8 0.1 dynamic_slice.10
  16.9 0.1 broadcast_in_dim.11
  17.0 0.1 reshape_reshape.7.pair_ref
  17.1 0.1 broadcast_in_dim.10
  17.1 0.1 reshape_reshape.6.skip_ref
  17.2 0.1 maximum_bitcast_fusion.rate_ref
  17.3 35.9 %all-to-all-done.arrived_hbm = bf16[64,88,128]{2,1,0:T(8,128)(2,1)} async-done(((bf16[64,88,128]{2,1,0:T(8,128)(2,1)}), bf16[64,88,128]{2,1,0:T(8,128)(2,1)}, u32[]{:S(2)}, u32[]{:S(2)}) %all-to-all-start) | async-done | bytes 1441824 | tf_op jit(solution)/shard_map/all_to_all | solution.py:360
  53.2 3.9 %state.1 = (bf16[256,2048]{1,0:T(8,128)(2,1)S(1)}, bf16[256,512]{1,0:T(8,128)(2,1)S(1)}, f32[128,128]{1,0:T(8,128)S(1)}, f32[128,128]{1,0:T(8,128)S(1)}, f32[128...) custom-call(bf16[64,88,128]{2,1,0:T(8,128)(2,1)} %all-to-all-done.ar, ...), custom_call_target="tpu_custom_call" | custom-call | tf_op jit(solution)/shard_map/state/pallas_call | solution.py:366
  57.1 5.6 %all-to-all-start.1 = ((bf16[32,32,128]{2,1,0:T(8,128)(2,1)}), bf16[32,32,128]{2,1,0:T(8,128)(2,1)S(1)}, u32[]{:S(2)}, u32[]{:S(2)}) async-start(bf16[32,32,128]{2,1,0:T(8,128)(2,1)} %get-tuple-element.30), calls=%async_computation.1 | async-start | bytes 524288 | tf_op jit(solution)/shard_map/all_to_all | solution.py:386
  62.7 3.8 %local.1 = (f32[128,2048]{1,0:T(8,128)S(1)}, bf16[128,4480]{1,0:T(8,128)(2,1)}, f32[32,128]{1,0:T(8,128)S(1)}) custom-call(bf16[256,2048]{1,0:T(8,128)(2,1)S(1)} %get-tuple-element.19.x_ref, bf16[256,512]{1,0:T(8,128)(2,1)S(1)} %get-tuple-element.20.bc_ref, f32[128,128]{1,0:T(8,128)S(1)} %get-tuple-element.21.cum_ref, ...), custom_call_target="tpu_custom_call" | custom-call | flops 2000000000 | bytes 6000000 | tf_op jit(solution)/shard_map/local/pallas_call | solution.py:387
  66.5 1.0 %collective-permute-start = (bf16[128,4480]{1,0:T(8,128)(2,1)}, bf16[128,4480]{1,0:T(8,128)(2,1)S(1)}, u32[]{:S(2)}, u32[]{:S(2)}) collective-permute-start(bf16[128,4480]{1,0:T(8,128)(2,1)} %get-tuple-element.32), channel_id=1, source_target_pairs={{0,4},{4,0},{1,5},{5,1},{2,6},{6,2},{3,7},{7,3},{8,12},{12,8},{9,1... | collective-permute-start | bytes 3440648 | tf_op jit(solution)/shard_map/ppermute | solution.py:395
  67.5 5.0 %all-to-all-done.1.in_ref = bf16[32,32,128]{2,1,0:T(8,128)(2,1)S(1)} async-done(((bf16[32,32,128]{2,1,0:T(8,128)(2,1)}), bf16[32,32,128]{2,1,0:T(8,128)(2,1)S(1)}, u32[]{:S(2)}, u32[]{:S(2)}) %all-to-all-start.1) | async-done | bytes 262176 | tf_op jit(solution)/shard_map/all_to_all | solution.py:386
  72.4 0.1 chips.1
  72.5 15.8 %all_to_all.15.h_ref = bf16[32,32,128]{2,1,0:T(8,128)(2,1)S(1)} all-to-all(bf16[32,32,128]{2,1,0:T(8,128)(2,1)S(1)} %chips.1), channel_id=1, replica_groups=mesh['z'=8,'x'=4,'c'=2,'seq'=4] {'x','z'}, dimensions={0} | all-to-all | bytes 524288 | tf_op jit(solution)/shard_map/all_to_all | solution.py:399
  88.2 3.6 %collective-permute-start.1 = (bf16[32,32,128]{2,1,0:T(8,128)(2,1)S(1)}, bf16[32,32,128]{2,1,0:T(8,128)(2,1)S(1)}, u32[]{:S(2)}, u32[]{:S(2)}) collective-permute-start(bf16[32,32,128]{2,1,0:T(8,128)(2,1)S(1)} %all_to_all.15.h_ref), channel_id=1, source_target_pairs={{0,4},{4,0},{1,5},{5,1},{2,6},{6,2},{3,7},{7,3},{8,12},{12,8},{9,1... | collective-permute-start | bytes 786440 | tf_op jit(solution)/shard_map/ppermute | solution.py:400
  91.8 0.5 mine.1.mine_ref
  92.3 0.0 collective-permute-done.swap_ref
  92.3 0.7 collective-permute-done.1.h_ref
  93.0 1.3 %final.1 = bf16[128,4096]{1,0:T(8,128)(2,1)} custom-call(bf16[128,2048]{1,0:T(8,128)(2,1)S(1)} %mine.1.mine_ref, bf16[128,4480]{1,0:T(8,128)(2,1)S(1)} %collective-permute-done.swap_ref, bf16[32,32,128]{2,1,0:T(8,128)(2,1)S(1)} %collective-permute-done.1.h_ref), custom_call_target="tpu_custom_call" | custom-call | tf_op jit(solution)/shard_map/final/pallas_call | solution.py:404
  (1 shorter events, 0.0 us)
Async XLA Ops:
  3.5 13.2 %copy-start = (f32[64]{0:T(128)S(1)}, f32[64]{0:T(128)}, u32[]{:S(2)}) copy-start(f32[64]{0:T(128)} %param.14) | copy-start | bytes 772
  3.5 13.4 %copy-start.1 = (f32[64]{0:T(128)S(1)}, f32[64]{0:T(128)}, u32[]{:S(2)}) copy-start(f32[64]{0:T(128)} %param.15) | copy-start | bytes 772
  3.5 49.8 %all-to-all-start = ((bf16[64,88,128]{2,1,0:T(8,128)(2,1)}), bf16[64,88,128]{2,1,0:T(8,128)(2,1)}, u32[]{:S(2)}, u32[]{:S(2)}) async-start(bf16[64,88,128]{2,1,0:T(8,128)(2,1)} %bitcast.5), calls=%async_computation | async-start | bytes 2883584 | tf_op jit(solution)/shard_map/all_to_all | solution.py:360
  57.1 15.3 %all-to-all-start.1 = ((bf16[32,32,128]{2,1,0:T(8,128)(2,1)}), bf16[32,32,128]{2,1,0:T(8,128)(2,1)S(1)}, u32[]{:S(2)}, u32[]{:S(2)}) async-start(bf16[32,32,128]{2,1,0:T(8,128)(2,1)} %get-tuple-element.30), calls=%async_computation.1 | async-start | bytes 524288 | tf_op jit(solution)/shard_map/all_to_all | solution.py:386
  66.5 25.8 %collective-permute-start = (bf16[128,4480]{1,0:T(8,128)(2,1)}, bf16[128,4480]{1,0:T(8,128)(2,1)S(1)}, u32[]{:S(2)}, u32[]{:S(2)}) collective-permute-start(bf16[128,4480]{1,0:T(8,128)(2,1)} %get-tuple-element.32), channel_id=1, source_target_pairs={{0,4},{4,0},{1,5},{5,1},{2,6},{6,2},{3,7},{7,3},{8,12},{12,8},{9,1... | collective-permute-start | bytes 3440648 | tf_op jit(solution)/shard_map/ppermute | solution.py:395
  88.2 4.8 %collective-permute-start.1 = (bf16[32,32,128]{2,1,0:T(8,128)(2,1)S(1)}, bf16[32,32,128]{2,1,0:T(8,128)(2,1)S(1)}, u32[]{:S(2)}, u32[]{:S(2)}) collective-permute-start(bf16[32,32,128]{2,1,0:T(8,128)(2,1)S(1)} %all_to_all.15.h_ref), channel_id=1, source_target_pairs={{0,4},{4,0},{1,5},{5,1},{2,6},{6,2},{3,7},{7,3},{8,12},{12,8},{9,1... | collective-permute-start | bytes 786440 | tf_op jit(solution)/shard_map/ppermute | solution.py:400

commit v4 on v3

v4 whole, which is shorter than its diff:
```python
import jax
import jax.numpy as jnp
from jax import lax
from jax.experimental import pallas as pl
from jax.experimental.pallas import tpu as pltpu
from jax.sharding import Mesh, PartitionSpec as P

F32 = jnp.float32
BF16 = jnp.bfloat16
I32 = jnp.int32
T = 128
NX, NZ = 4, 8
NP = NX * NZ
HG = 8
HP = 64
N = 64
GW = HG * HP
HH = 32
HW = HH * HP
MSG = 88
PARTS = 2
AWAY = 12288


def iota(shape, dim):
    return lax.broadcasted_iota(I32, shape, dim)


def dot(a, b):
    return jnp.dot(a, b, preferred_element_type=F32)


def dot_nt(a, b):
    return lax.dot_general(a, b, (((1,), (1,)), ((), ())), preferred_element_type=F32)


def params(mib):
    return pltpu.CompilerParams(vmem_limit_bytes=mib * 1024 * 1024)


def softplus(v):
    return jnp.maximum(v, 0.0) + jnp.log1p(jnp.exp(-jnp.abs(v)))


def three_parts(v):
    high = v.astype(BF16)
    rest = v - high.astype(F32)
    mid = rest.astype(BF16)
    return high, mid, (rest - mid.astype(F32)).astype(BF16)


def pack_kernel(
    x_hbm, b_hbm, c_hbm, dt_hbm, reset_hbm, out_hbm,
    x_ref, b_ref, c_ref, dt_ref, reset_ref, out_ref, sems, out_sems,
):
    pairs = [(reset_hbm, reset_ref), (dt_hbm, dt_ref)]
    span = T // PARTS
    for part in range(PARTS):
        rows = pl.ds(span * part, span)
        pairs += [(src.at[rows], dst.at[rows]) for src, dst in ((b_hbm, b_ref), (c_hbm, c_ref), (x_hbm, x_ref))]
    copies = [pltpu.make_async_copy(s, d, sems.at[n]) for n, (s, d) in enumerate(pairs)]
    for copy in copies:
        copy.start()
    row, col = iota((4 * span, 4 * span), 0), iota((4 * span, 4 * span), 1)
    pick = (col // span == (row % 16) // 4) & (col % span == (row // 16) * 4 + row % 4)
    pick = pick.astype(BF16)
    lane, head = iota((256, 64), 0), iota((256, 64), 1)
    spread = (lane % T < HH) & (head == (lane // T) * HH + lane % T)
    to, row = iota((256, T), 0), iota((256, T), 1)
    own_row = ((to % 8 < 4) & (row == (to // 8) * 4 + to % 8)).astype(BF16)
    to, head = iota((256, 64), 0), iota((256, 64), 1)
    chosen = ((to % 8 // 2 == 2) & (head == 2 * (to // 8) + to % 2)).astype(BF16)
    of_chip = (iota((T, T), 0) // 4 == iota((T, T), 1)).astype(BF16)
    chip = lax.axis_index("z") * NX + lax.axis_index("x")
    flag = (iota((8, T), 0) == 6) & (iota((8, T), 1) == chip)
    for copy in copies[:2]:
        copy.wait()
    dt = dt_ref[...]
    wide = dot(spread.astype(BF16), dt).astype(BF16)
    steps = dot_nt(own_row, wide)
    sums = dot(jnp.concatenate(three_parts(softplus(dt.astype(F32))), axis=0), of_chip)
    high, mid, low = three_parts(sums[:64] + sums[64:128] + sums[128:])
    sums = high.astype(F32) + pltpu.roll(mid.astype(F32), HH, 1) + pltpu.roll(low.astype(F32), 2 * HH, 1)
    sums = dot(chosen, sums.astype(BF16))
    resets = jnp.sum(reset_ref[...].astype(F32), axis=1, keepdims=True)
    flag = jnp.where(flag, jnp.broadcast_to(resets, (8, T)), 0.0)
    sent = []
    for part in range(PARTS):
        for copy in copies[2 + 3 * part : 5 + 3 * part]:
            copy.wait()
        rows = pl.ds(span * part, span)
        tiles = []
        for c in range(2):
            for q in range(4):
                tiles.append([x_ref[rows, pl.ds(HW * c + 512 * q + T * j, T)] for j in range(4)])
            tiles.append(
                [b_ref[rows, pl.ds(256 * c, T)], b_ref[rows, pl.ds(256 * c + T, T)],
                 c_ref[rows, pl.ds(256 * c, T)], c_ref[rows, pl.ds(256 * c + T, T)]]
            )
        right = jnp.concatenate([jnp.concatenate(t, axis=0) for t in tiles], axis=1)
        got = dot(pick, right).astype(BF16)
        for p in range(NP // PARTS):
            z, x = NZ // PARTS * part + p // NX, p % NX
            at = 8 * (NP // PARTS * part + p)
            for c in range(2):
                to = 2 * x + c
                for q in range(5):
                    lanes = slice(T * (5 * c + q), T * (5 * c + q) + T)
                    out_ref[to, z, pl.ds(16 * q, 16), :] = got[16 * p : 16 * p + 16, lanes]
                m = 8 * (16 * c + (NZ * x + z) // 2)
                tail = steps[at : at + 8, T * c : T * c + T] + sums[m : m + 8] + flag
                out_ref[to, z, pl.ds(80, 8), :] = tail.astype(BF16)
        here = pl.ds(NZ // PARTS * part, NZ // PARTS)
        sent.append(pltpu.make_async_copy(out_ref.at[:, here], out_hbm.at[:, here], out_sems.at[part]))
        sent[-1].start()
    for copy in sent:
        copy.wait()


def columns(row):
    return jnp.broadcast_to(row, (T, T)).T


def plan_kernel(order_ref, order2_ref, reset_ref, reset2_ref, perm_ref, cnt_ref):
    core = lax.axis_index("c")
    orders = [order_ref[...].astype(F32), order2_ref[...].astype(F32)]
    resets = [reset_ref[...].astype(F32), reset2_ref[...].astype(F32)]
    orders = [columns(jnp.where(core == i, orders[0], orders[1])) for i in range(2)]
    upto = (iota((T, T), 0) <= iota((T, T), 1)).astype(BF16)
    counts = []
    for i in range(2):
        row = jnp.broadcast_to(jnp.where(core == i, resets[0], resets[1]), (8, T))
        counts.append(columns(dot(row.astype(BF16), upto)[:1]))
    cnt_ref[...] = jnp.where(iota((T, T), 1) < HH, counts[0], counts[1])
    order = jnp.concatenate(orders, axis=0).astype(I32)
    source = order >> 1
    source = ((source & (NZ - 1)) << 3) + (source >> 3)
    target = (source << 2) + ((iota((256, T), 0) >> 7) << 1) + (order & 1)
    for m in range(2):
        perm_ref[:, pl.ds(T * m, T)] = jnp.where(iota((256, T), 1) + T * m == target, 1.0, 0.0).astype(BF16)


def expander():
    gap = iota((T, T), 0) % HH - iota((T, T), 1) // HP
    return jnp.concatenate([jnp.where(gap == 2 * t, 1.0, 0.0).astype(BF16) for t in range(HW // T)], axis=1)


def two_parts(v):
    high = v.astype(BF16).astype(F32)
    low = v - high
    return jnp.where(iota(v.shape, 1) < 64, high, pltpu.roll(low, 64, 1))


def of_span(parts, i):
    return jnp.where((iota(parts.shape, 1) % 64) // HH == i, parts, 0.0).astype(BF16)


def inner_weights(cum, step, cnt):
    last, last_cnt = cum[T - 1 : T], cnt[T - 1 : T]
    return two_parts(jnp.where(cnt == last_cnt, jnp.exp(last - cum) * step, 0.0))


def span_decay(cum, cnt):
    return jnp.where(cnt[T - 1 : T] == 0.0, jnp.exp(cum[T - 1 : T]), 0.0)


def x_tile(x_ref, rows, t):
    return x_ref[rows, pl.ds(T * (4 * (t % 4) + t // 4), T)]


def state_kernel(
    arrived_ref, rate_ref, perm_ref, cnt_ref, x_hbm, bc_ref, cum_ref, step_ref, msg_ref, sums_ref, x_ref, x_sems
):
    top = iota((NP, 8, T), 1) < 4

    def halves(here):
        even, odd = here[:, 0], here[:, 1]
        low = jnp.where(top, even, pltpu.roll(odd, 4, 1)).reshape(256, T).astype(BF16)
        high = jnp.where(top, pltpu.roll(even, 4, 1), odd).reshape(256, T).astype(BF16)
        return low, high

    perm = perm_ref[...]
    cnt = cnt_ref[...]
    tails = arrived_ref[:, pl.ds(80, 8), :].astype(F32)
    sums_ref[...] = jnp.sum(tails, axis=0)
    raw = dot(perm, halves(tails.reshape(NP, 2, 8, T))[0])
    raw = jnp.where(iota((T, T), 1) < HH, raw[:T], pltpu.roll(raw[T:], HH, 1))
    step = softplus(raw)
    lower = (iota((T, T), 0) >= iota((T, T), 1)).astype(BF16)
    cum = dot(lower, jnp.concatenate(three_parts(-step * rate_ref[...]), axis=1))
    cum = cum[:, :T] + cum[:, T : 2 * T] + cum[:, 2 * T :]
    cum_ref[...] = cum
    step_ref[...] = step
    tiles = [[] for _ in range(4)]
    for q in range(5):
        here = arrived_ref[:, pl.ds(16 * q, 16), :].astype(F32).reshape(NP, 2, 2, 8, T)
        for half in range(2):
            low, high = halves(here[:, :, half])
            tiles[2 * half].append(low)
            tiles[2 * half + 1].append(high)
    x_copies = []
    for j in range(4):
        rows = dot(perm, jnp.concatenate(tiles[j], axis=1)).astype(BF16)
        here = pl.ds(GW * j, GW)
        x_ref[:, here] = rows[:, :GW]
        bc_ref[:, pl.ds(T * j, T)] = rows[:, GW:]
        x_copies.append(pltpu.make_async_copy(x_ref.at[:, here], x_hbm.at[pl.ds(0, 2 * T), here], x_sems.at[j]))
        x_copies[-1].start()
    e = expander()
    coef = inner_weights(cum, step, cnt)
    decay = two_parts(jnp.broadcast_to(span_decay(cum, cnt), (8, T)))
    decay = dot(of_span(decay, 1), e)[:1]
    weighted = []
    for i in range(2):
        here = pl.ds(T * i, T)
        scale = dot(of_span(coef, i), e)
        weighted.append([(x_tile(x_ref, here, t).astype(F32) * scale[:, T * t : T * t + T]).astype(BF16) for t in range(16)])
    for tile in range(2):
        b = [bc_ref[pl.ds(T * i, T), pl.ds(T * tile, T)].astype(F32).T.astype(BF16) for i in range(2)]
        for half in range(2):
            g = 2 * tile + half
            lanes = slice(GW * g, GW * g + GW)
            states = [dot(b[i][N * half : N * half + N], jnp.concatenate(weighted[i][4 * g : 4 * g + 4], axis=1)) for i in range(2)]
            h = (decay[:, lanes] * states[0] + states[1]).astype(BF16)
            for pair in range(4):
                for k in range(2):
                    m = (4 * g + pair) * 2 + k
                    msg_ref[m] = h[32 * k : 32 * k + 32, T * pair : T * pair + T]
    for copy in x_copies:
        copy.wait()


def local_kernel(
    x_hbm, bc_ref, cum_ref, step_ref, cnt_ref, skip_ref, sums_ref, pair_ref,
    mine_ref, factor_ref, swap_ref, decay_ref, out_ref, key_ref, x_ref, x_sem,
):
    x_copy = pltpu.make_async_copy(x_hbm.at[pl.ds(0, 2 * T)], x_ref, x_sem)
    x_copy.start()
    core = lax.axis_index("c")
    there = pl.ds(pl.multiple_of(T * (1 - core), T), T)
    cum, step, cnt = cum_ref[...], step_ref[...], cnt_ref[...]
    key_ref[...] = (cum - jnp.log(step)).T
    entry = jnp.where(cnt == 0.0, jnp.exp(cum), 0.0)
    decay = jnp.broadcast_to(span_decay(cum, cnt), (8, T))
    before = jnp.where(iota((8, T), 1) < HH, 1.0, pltpu.roll(decay, HH, 1))
    carry = two_parts(entry * before[:1])
    factor_ref[...] = of_span(carry, core)
    e = expander()
    entry = dot(of_span(two_parts(entry), 1), e)
    x_copy.wait()
    inner = dot(of_span(inner_weights(cum, step, cnt), 0), e)
    weighted = [
        (x_tile(x_ref, pl.ds(0, T), t).astype(F32) * inner[:, T * t : T * t + T]).astype(BF16) for t in range(16)
    ]
    causal = iota((T, T), 0) >= iota((T, T), 1)
    left = iota((T, T), 1) < HP
    for i in range(2):
        here = pl.ds(T * i, T)
        count = jnp.broadcast_to(cnt[:, HH * i : HH * i + 1], (T, T))
        keep = causal & (count == count.T)
        for g in range(4):
            tile, half = g // 2, g % 2
            b = bc_ref[here, pl.ds(T * tile, T)][:, N * half : N * half + N]
            c = bc_ref[here, pl.ds(2 * T + T * tile, T)][:, N * half : N * half + N]
            scores = dot_nt(c, b)
            if i == 1:
                lanes = slice(GW * g, GW * g + GW)
                first = bc_ref[pl.ds(0, T), pl.ds(T * tile, T)].astype(F32).T[N * half : N * half + N].astype(BF16)
                state = dot(first, jnp.concatenate(weighted[4 * g : 4 * g + 4], axis=1)).astype(BF16)
                carried = dot(c, state) * entry[:, lanes]
            for pair in range(4):
                weights = []
                for h in (2 * pair, 2 * pair + 1):
                    col = HH * i + HG * g + h
                    gap = cum_ref[:, col : col + 1] - key_ref[col : col + 1, :]
                    weights.append((jnp.exp(jnp.where(keep, gap, -jnp.inf)) * scores).astype(BF16))
                lanes = pl.ds(GW * g + T * pair, T)
                x = x_tile(x_ref, here, 4 * g + pair)
                zero = jnp.zeros_like(x)
                both = jnp.concatenate([jnp.where(left, x, zero), jnp.where(left, zero, x)], axis=0)
                out = dot(jnp.concatenate(weights, axis=1), both) + skip_ref[:, lanes] * x.astype(F32)
                if i == 1:
                    out += carried[:, T * pair : T * pair + T]
                out_ref[here, lanes] = out
    mine_ref[...] = out_ref[pl.ds(pl.multiple_of(T * core, T), T), :]
    other = out_ref[there, :]
    high = other.astype(BF16)
    swap_ref[:, pl.ds(0, HW)] = high
    swap_ref[:, pl.ds(HW, HW)] = (other - high.astype(F32)).astype(BF16)
    swap_ref[:, pl.ds(2 * HW, 2 * T)] = bc_ref[there, pl.ds(2 * T, 2 * T)]
    swap_ref[:, pl.ds(2 * HW + 2 * T, T)] = of_span(carry, 1 - core)
    tails = sums_ref[...]
    sums = tails + pltpu.roll(tails, T - HH, 1) + pltpu.roll(tails, T - 2 * HH, 1)
    rows = iota((8, T), 0)
    sums = jnp.where(rows == 6, tails, sums)
    sums = jnp.concatenate([sums, jnp.zeros((T - 8, T), F32)], axis=0).T[:NP]
    resets = sums[:, 6:7]
    sums = jnp.where(iota((NP, T), 1) < HP, sums[:, 4:5], sums[:, 5:6])
    decay_ref[...] = jnp.where(resets == 0.0, jnp.exp(-sums * pair_ref[...]), 0.0)


def scan_kernel(in_ref, decay_ref, out_ref):
    h = jnp.zeros((32, T), F32)
    for p in range(NP):
        at = (p % NX) * NZ + p // NX
        out_ref[at] = h.astype(BF16)
        h = decay_ref[pl.ds(p, 1), :] * h + in_ref[at].astype(F32)


def carried(c, h_ref, g, scale):
    state = jnp.concatenate(
        [jnp.concatenate([h_ref[8 * g + 2 * p], h_ref[8 * g + 2 * p + 1]], axis=0) for p in range(4)], axis=1
    )
    return dot(c, state) * scale[:, GW * g : GW * g + GW]


def mine_kernel(partial_ref, bc_ref, factor_ref, h_ref, out_ref):
    core = lax.axis_index("c")
    scale = dot(factor_ref[...], expander())
    cs = bc_ref[pl.ds(pl.multiple_of(T * core, T), T), pl.ds(2 * T, 2 * T)]
    for g in range(4):
        lanes = pl.ds(GW * g, GW)
        inter = carried(cs[:, N * g : N * g + N], h_ref, g, scale)
        out_ref[:, lanes] = (partial_ref[:, lanes] + inter).astype(BF16)


def final_kernel(mine_ref, swap_ref, h_ref, out_hbm, other_ref, sems):
    core = lax.axis_index("c")

    def copy(src, n, half):
        return pltpu.make_async_copy(src, out_hbm.at[:, pl.ds(HW * half, HW)], sems.at[n])

    for k in range(2):

        @pl.when(core == k)
        def _():
            copy(mine_ref, 0, k).start()

    scale = dot(swap_ref[:, pl.ds(2 * HW + 2 * T, T)], expander())
    cs = swap_ref[:, pl.ds(2 * HW, 2 * T)]
    for g in range(4):
        lanes = pl.ds(GW * g, GW)
        partial = swap_ref[:, lanes].astype(F32) + swap_ref[:, pl.ds(HW + GW * g, GW)].astype(F32)
        inter = carried(cs[:, N * g : N * g + N], h_ref, g, scale)
        other_ref[:, lanes] = (partial + inter).astype(BF16)
    for k in range(2):

        @pl.when(core == k)
        def _():
            copy(other_ref, 1, 1 - k).start()
            copy(mine_ref, 0, k).wait()
            copy(other_ref, 1, 1 - k).wait()


def per_device(x, b, c, dt, order, resets, rate, skip):
    core = lax.axis_index("c")
    sds = jax.ShapeDtypeStruct
    hbm, vmem = pl.BlockSpec(memory_space=pltpu.HBM), pl.BlockSpec(memory_space=pltpu.VMEM)
    resets = resets.reshape(1, T)
    packed = pl.pallas_call(
        pack_kernel,
        out_shape=sds((2 * NX, NZ, MSG, T), BF16),
        in_specs=[hbm] * 5,
        out_specs=hbm,
        scratch_shapes=[
            pltpu.VMEM(x.shape, BF16),
            pltpu.VMEM(b.shape, BF16),
            pltpu.VMEM(c.shape, BF16),
            pltpu.VMEM(dt.shape[::-1], BF16),
            pltpu.VMEM((1, T), I32),
            pltpu.VMEM((2 * NX, NZ, MSG, T), BF16),
            pltpu.SemaphoreType.DMA((2 + 3 * PARTS,)),
            pltpu.SemaphoreType.DMA((PARTS,)),
        ],
        compiler_params=params(56),
        name="pack",
    )(x, b, c, dt.T, resets)
    packed = packed.reshape(2 * NP, MSG, T)
    arrived = lax.all_to_all(packed, ("x", "c", "z"), split_axis=0, concat_axis=0, tiled=True)
    order2 = lax.ppermute(order, "c", [(0, 1), (1, 0)])
    resets2 = lax.ppermute(resets, "c", [(0, 1), (1, 0)])
    perm, cnt = pl.pallas_call(
        plan_kernel,
        out_shape=(sds((2 * T, 2 * T), BF16), sds((T, T), F32)),
        compiler_params=params(16),
        cost_estimate=pl.CostEstimate(flops=1_000_000_000, bytes_accessed=1_000_000, transcendentals=0),
        name="plan",
    )(order, order2, resets, resets2)
    mine = lax.dynamic_slice_in_dim(rate, core * HH, HH)
    rate_row = jnp.concatenate([mine, mine, jnp.zeros((64,), F32)]).reshape(1, T)
    pair = (lax.axis_index("x") * NZ + lax.axis_index("z")) // 2 * 2
    pair_row = jnp.repeat(lax.dynamic_slice_in_dim(rate, core * HH + pair, 2), HP).reshape(1, T)
    skip_row = jnp.repeat(lax.dynamic_slice_in_dim(skip, core * HH, HH), HP).reshape(1, HW)
    xs, bc, cum, step, msg, sums = pl.pallas_call(
        state_kernel,
        out_shape=(
            sds((AWAY, HW), BF16),
            sds((2 * T, 4 * T), BF16),
            sds((T, T), F32),
            sds((T, T), F32),
            sds((NP, 32, T), BF16),
            sds((8, T), F32),
        ),
        out_specs=(hbm,) + (vmem,) * 5,
        scratch_shapes=[pltpu.VMEM((2 * T, HW), BF16), pltpu.SemaphoreType.DMA((4,))],
        compiler_params=params(24),
        name="state",
    )(arrived, rate_row, perm, cnt)
    totals = lax.all_to_all(msg, ("x", "z"), split_axis=0, concat_axis=0, tiled=True)
    partial, factors, swap, decays = pl.pallas_call(
        local_kernel,
        out_shape=(sds((T, HW), F32), sds((T, T), BF16), sds((T, 2 * HW + 3 * T), BF16), sds((NP, T), F32)),
        in_specs=[hbm] + [vmem] * 7,
        scratch_shapes=[
            pltpu.VMEM((2 * T, HW), F32),
            pltpu.VMEM((T, T), F32),
            pltpu.VMEM((2 * T, HW), BF16),
            pltpu.SemaphoreType.DMA,
        ],
        compiler_params=params(20),
        cost_estimate=pl.CostEstimate(flops=2_000_000_000, bytes_accessed=6_000_000, transcendentals=1_100_000),
        name="local",
    )(xs, bc, cum, step, cnt, skip_row, sums, pair_row)
    swap = lax.ppermute(swap, "c", [(0, 1), (1, 0)])
    entering = pl.pallas_call(
        scan_kernel, out_shape=sds((NP, 32, T), BF16), compiler_params=params(16), name="chips"
    )(totals, decays)
    states = lax.all_to_all(entering, ("x", "z"), split_axis=0, concat_axis=0, tiled=True)
    other = lax.ppermute(states, "c", [(0, 1), (1, 0)])
    own = pl.pallas_call(
        mine_kernel, out_shape=sds((T, HW), BF16), compiler_params=params(20), name="mine"
    )(partial, bc, factors, states)
    return pl.pallas_call(
        final_kernel,
        out_shape=sds((T, 2 * HW), BF16),
        in_specs=[pl.BlockSpec(memory_space=pltpu.VMEM)] * 3,
        out_specs=hbm,
        scratch_shapes=[pltpu.VMEM((T, HW), BF16), pltpu.SemaphoreType.DMA((2,))],
        compiler_params=params(20),
        name="final",
    )(own, swap, other)


def solution(mesh):
    fine = Mesh(mesh.devices.reshape(NZ, NX, 2, mesh.shape["seq"]), ("z", "x", "c", "seq"))
    rows = ("seq", "z", "x", "c")
    in_specs = (P(rows, None),) * 5 + (P(rows), P(), P())
    return jax.shard_map(
        per_device, mesh=fine, in_specs=in_specs, out_specs=P(rows, None), check_vma=False
    )
```

time: 94.6 us -> 92.7 us (0.980)
  waiting for transfers between devices: 41.6 us -> 39 us
    all_to_all x1, waiting for transfers between devices: 4.96 us -> 3.19 us  [per_device(): lax.all_to_all(msg, ('x', 'z'), split_axis=0, concat_axis=0, tiled=True)]
    all_to_all x1, waiting for transfers between devices: 35.9 us -> 34.7 us  [per_device(): lax.all_to_all(packed, ('x', 'c', 'z'), split_axis=0, concat_axis=0, tile...]
    pallas_call x2 -> x3, Pallas kernels: 7.66 us -> 8.21 us  [the longest x1 5.45 us: per_device(): pl.pallas_call(local_kernel, out_shape=(sds((T, HW), F32), sds((T, T), BF...]
  transfers between devices with their start and end apart: 4 -> 6, of which waited for: 3 -> 5; matrix products, arithmetic and copies ran while one was open for 1% -> 1% of each run, Pallas kernels for 5% -> 7%
where the time goes in v4:
time: 92.7 us; the launch traced here: 92.4 us
  waiting for transfers between devices  39 us (42%)
  starting transfers between devices  24 us (26%)
  blocking collectives  15.8 us (17%)
  Pallas kernels  12.8 us (14%)
    all_to_all x1, waiting for transfers between devices, per_device(): lax.all_to_all(packed, ('x', 'c', 'z'), split_axis=0, concat_axis=0, tile...  34.7 us
    all_to_all x1, blocking collectives, per_device(): lax.all_to_all(entering, ('x', 'z'), split_axis=0, concat_axis=0, tiled=T...  15.8 us
    all_to_all x1, starting transfers between devices, per_device(): lax.all_to_all(packed, ('x', 'c', 'z'), split_axis=0, concat_axis=0, tile...  13.1 us
    all_to_all x1, starting transfers between devices, per_device(): lax.all_to_all(msg, ('x', 'z'), split_axis=0, concat_axis=0, tiled=True)  5.59 us
    pallas_call x1, Pallas kernels, per_device(): pl.pallas_call(local_kernel, out_shape=(sds((T, HW), F32), sds((T, T), BF...  5.45 us
    ppermute x1, starting transfers between devices, per_device(): other = lax.ppermute(states, 'c', [(0, 1), (1, 0)])  3.6 us
    all_to_all x1, waiting for transfers between devices, per_device(): lax.all_to_all(msg, ('x', 'z'), split_axis=0, concat_axis=0, tiled=True)  3.19 us
    pallas_call x1, Pallas kernels, per_device(): pl.pallas_call(pack_kernel, out_shape=sds((2 * NX, NZ, MSG, T), BF16), in...  2.87 us
  transfers between devices with their start and end apart: 6, of which 5 were waited for; matrix products, arithmetic and copies ran while one was open for 1% of the time, Pallas kernels for 7%

profile of v4, /device:TPU:1, one launch (start us, length us, event | category | flops | bytes accessed | tf_op | source)
XLA Modules:
  0.0 92.4 jit_solution(14563585088631291700)
XLA Ops:
  0.0 2.9 %pack.1 = bf16[8,8,88,128]{3,2,1,0:T(8,128)(2,1)} custom-call(bf16[128,4096]{1,0:T(8,128)(2,1)} %x_hbm.1, bf16[128,512]{1,0:T(8,128)(2,1)} %b_hbm.1, bf16[128,512]{1,0:T(8,128)(2,1)} %c_hbm.1, bf16[64,128]{1,0:T(8,128)(2,1)} %bitcast.9, s32[1,128]{1,0:T(1,128)} %bitcast.5), custom_call_target="tpu_custom_call" | custom-call | tf_op jit(solution)/shard_map/pack/pallas_call | solution.py:360
  2.9 0.0 copy-start
  2.9 0.0 copy-start.1
  2.9 0.0 copy-start.2
  2.9 0.0 copy-start.3
  2.9 13.1 %all-to-all-start = ((bf16[64,88,128]{2,1,0:T(8,128)(2,1)}), bf16[64,88,128]{2,1,0:T(8,128)(2,1)S(1)}, u32[]{:S(2)}, u32[]{:S(2)}) async-start(bf16[64,88,128]{2,1,0:T(8,128)(2,1)} %bitcast.8), calls=%async_computation | async-start | bytes 2883584 | tf_op jit(solution)/shard_map/all_to_all | solution.py:379
  16.1 0.0 copy-done
  16.1 0.5 collective-permute-start.1
  16.6 0.0 copy-done.1
  16.6 0.1 collective-permute-start
  16.7 0.0 copy-done.2
  16.7 0.1 dynamic_slice.9
  16.8 0.1 maximum_bitcast_fusion.rate_ref
  16.9 0.1 dynamic_slice.11
  17.0 0.0 copy-done.3
  17.0 0.1 dynamic_slice.10
  17.0 0.1 broadcast_in_dim.11
  17.1 0.1 reshape_reshape.7.pair_ref
  17.2 0.1 broadcast_in_dim.10
  17.3 0.1 reshape_reshape.6.skip_ref
  17.3 0.1 collective-permute-done.1.reset2_ref
  17.4 0.3 collective-permute-done.order2_ref
  17.7 0.2 plan.1
  18.0 34.7 %all-to-all-done.arrived_ref = bf16[64,88,128]{2,1,0:T(8,128)(2,1)S(1)} async-done(((bf16[64,88,128]{2,1,0:T(8,128)(2,1)}), bf16[64,88,128]{2,1,0:T(8,128)(2,1)S(1)}, u32[]{:S(2)}, u32[]{:S(2)}) %all-to-all-start) | async-done | bytes 1441824 | tf_op jit(solution)/shard_map/all_to_all | solution.py:379
  52.7 2.5 %state.1 = (bf16[12288,2048]{1,0:T(8,128)(2,1)}, bf16[256,512]{1,0:T(8,128)(2,1)S(1)}, f32[128,128]{1,0:T(8,128)S(1)}, f32[128,128]{1,0:T(8,128)S(1)}, bf16[32,3...) custom-call(bf16[64,88,128]{2,1,0:T(8,128)(2,1)S(1)} %all-to-all-done.arrived_ref, f32[1,128]{1,0:T(1,128)S(1)} %maximum_bitcast_fusion.rate_ref, ...), custom_call_target="tpu_custom_call" | custom-call | tf_op jit(solution)/shard_map/state/pallas_call | solution.py:394
  55.2 5.6 %all-to-all-start.1 = ((bf16[32,32,128]{2,1,0:T(8,128)(2,1)}), bf16[32,32,128]{2,1,0:T(8,128)(2,1)S(1)}, u32[]{:S(2)}, u32[]{:S(2)}) async-start(bf16[32,32,128]{2,1,0:T(8,128)(2,1)} %get-tuple-element.26), calls=%async_computation.1 | async-start | bytes 524288 | tf_op jit(solution)/shard_map/all_to_all | solution.py:409
  60.8 5.4 %local.1 = (f32[128,2048]{1,0:T(8,128)S(1)}, bf16[128,128]{1,0:T(8,128)(2,1)S(1)}, bf16[128,4480]{1,0:T(8,128)(2,1)}, f32[32,128]{1,0:T(8,128)S(1)}) custom-call(bf16[12288,2048]{1,0:T(8,128)(2,1)} %get-tuple-element.19.x_hbm, bf16[256,512]{1,0:T(8,128)(2,1)S(1)} %get-tuple-element.20.bc_ref, f32[128,128]{1,0:T(8,128)S(1)} %get-tuple-element.21.cum_ref, ...), custom_call_target="tpu_custom_call" | custom-call | flops 2000000000 | bytes 6000000 | tf_op jit(solution)/shard_map/local/pallas_call | solution.py:410
  66.3 1.0 %collective-permute-start.2 = (bf16[128,4480]{1,0:T(8,128)(2,1)}, bf16[128,4480]{1,0:T(8,128)(2,1)S(1)}, u32[]{:S(2)}, u32[]{:S(2)}) collective-permute-start(bf16[128,4480]{1,0:T(8,128)(2,1)} %get-tuple-element.28), channel_id=1, source_target_pairs={{0,4},{4,0},{1,5},{5,1},{2,6},{6,2},{3,7},{7,3},{8,12},{12,8},{9,1... | collective-permute-start | bytes 3440648 | tf_op jit(solution)/shard_map/ppermute | solution.py:424
  67.3 3.2 %all-to-all-done.1.in_ref = bf16[32,32,128]{2,1,0:T(8,128)(2,1)S(1)} async-done(((bf16[32,32,128]{2,1,0:T(8,128)(2,1)}), bf16[32,32,128]{2,1,0:T(8,128)(2,1)S(1)}, u32[]{:S(2)}, u32[]{:S(2)}) %all-to-all-start.1) | async-done | bytes 262176 | tf_op jit(solution)/shard_map/all_to_all | solution.py:409
  70.5 0.1 chips.1
  70.6 15.8 %all_to_all.15.h_ref = bf16[32,32,128]{2,1,0:T(8,128)(2,1)S(1)} all-to-all(bf16[32,32,128]{2,1,0:T(8,128)(2,1)S(1)} %chips.1), channel_id=1, replica_groups=mesh['z'=8,'x'=4,'c'=2,'seq'=4] {'x','z'}, dimensions={0} | all-to-all | bytes 524288 | tf_op jit(solution)/shard_map/all_to_all | solution.py:428
  86.4 3.6 %collective-permute-start.3 = (bf16[32,32,128]{2,1,0:T(8,128)(2,1)S(1)}, bf16[32,32,128]{2,1,0:T(8,128)(2,1)S(1)}, u32[]{:S(2)}, u32[]{:S(2)}) collective-permute-start(bf16[32,32,128]{2,1,0:T(8,128)(2,1)S(1)} %all_to_all.15.h_ref), channel_id=1, source_target_pairs={{0,4},{4,0},{1,5},{5,1},{2,6},{6,2},{3,7},{7,3},{8,12},{12,8},{9,1... | collective-permute-start | bytes 786440 | tf_op jit(solution)/shard_map/ppermute | solution.py:429
  90.0 0.4 mine.1.mine_ref
  90.4 0.0 collective-permute-done.2.swap_ref
  90.4 0.7 collective-permute-done.3.h_ref
  91.1 1.2 %final.1 = bf16[128,4096]{1,0:T(8,128)(2,1)} custom-call(bf16[128,2048]{1,0:T(8,128)(2,1)S(1)} %mine.1.mine_ref, bf16[128,4480]{1,0:T(8,128)(2,1)S(1)} %collective-permute-done.2.swap_ref, bf16[32,32,128]{2,1,0:T(8,128)(2,1)S(1)} %collective-permute-done.3.h_ref), custom_call_target="tpu_custom_call" | custom-call | tf_op jit(solution)/shard_map/final/pallas_call | solution.py:433
  (1 shorter events, 0.0 us)
Async XLA Ops:
  2.9 13.2 %copy-start = (s32[128]{0:T(128)S(1)}, s32[128]{0:T(128)}, u32[]{:S(2)}) copy-start(s32[128]{0:T(128)} %param.13) | copy-start | bytes 1540
  2.9 13.7 %copy-start.1 = (s32[1,128]{1,0:T(1,128)S(1)}, s32[1,128]{1,0:T(1,128)}, u32[]{:S(2)}) copy-start(s32[1,128]{1,0:T(1,128)} %order_ref.1) | copy-start | bytes 1540
  2.9 13.8 %copy-start.2 = (f32[64]{0:T(128)S(1)}, f32[64]{0:T(128)}, u32[]{:S(2)}) copy-start(f32[64]{0:T(128)} %param.14) | copy-start | bytes 772
  2.9 14.0 %copy-start.3 = (f32[64]{0:T(128)S(1)}, f32[64]{0:T(128)}, u32[]{:S(2)}) copy-start(f32[64]{0:T(128)} %param.15) | copy-start | bytes 772
  2.9 49.8 %all-to-all-start = ((bf16[64,88,128]{2,1,0:T(8,128)(2,1)}), bf16[64,88,128]{2,1,0:T(8,128)(2,1)S(1)}, u32[]{:S(2)}, u32[]{:S(2)}) async-start(bf16[64,88,128]{2,1,0:T(8,128)(2,1)} %bitcast.8), calls=%async_computation | async-start | bytes 2883584 | tf_op jit(solution)/shard_map/all_to_all | solution.py:379
  16.1 1.4 %collective-permute-start.1 = (s32[1,128]{1,0:T(1,128)S(1)}, s32[1,128]{1,0:T(1,128)S(1)}, u32[]{:S(2)}, u32[]{:S(2)}) collective-permute-start(s32[1,128]{1,0:T(1,128)S(1)} %bitcast.6), channel_id=1, source_target_pairs={{0,4},{4,0},{1,5},{5,1},{2,6},{6,2},{3,7},{7,3},{8,12},{12,8},{9,1... | collective-permute-start | bytes 1544 | tf_op jit(solution)/shard_map/ppermute | solution.py:381
  16.6 1.1 %collective-permute-start = (s32[1,128]{1,0:T(1,128)S(1)}, s32[1,128]{1,0:T(1,128)S(1)}, u32[]{:S(2)}, u32[]{:S(2)}) collective-permute-start(s32[1,128]{1,0:T(1,128)S(1)} %copy-done.1), channel_id=1, source_target_pairs={{0,4},{4,0},{1,5},{5,1},{2,6},{6,2},{3,7},{7,3},{8,12},{12,8},{9,1... | collective-permute-start | bytes 1544 | tf_op jit(solution)/shard_map/ppermute | solution.py:380
  55.2 15.3 %all-to-all-start.1 = ((bf16[32,32,128]{2,1,0:T(8,128)(2,1)}), bf16[32,32,128]{2,1,0:T(8,128)(2,1)S(1)}, u32[]{:S(2)}, u32[]{:S(2)}) async-start(bf16[32,32,128]{2,1,0:T(8,128)(2,1)} %get-tuple-element.26), calls=%async_computation.1 | async-start | bytes 524288 | tf_op jit(solution)/shard_map/all_to_all | solution.py:409
  66.3 24.1 %collective-permute-start.2 = (bf16[128,4480]{1,0:T(8,128)(2,1)}, bf16[128,4480]{1,0:T(8,128)(2,1)S(1)}, u32[]{:S(2)}, u32[]{:S(2)}) collective-permute-start(bf16[128,4480]{1,0:T(8,128)(2,1)} %get-tuple-element.28), channel_id=1, source_target_pairs={{0,4},{4,0},{1,5},{5,1},{2,6},{6,2},{3,7},{7,3},{8,12},{12,8},{9,1... | collective-permute-start | bytes 3440648 | tf_op jit(solution)/shard_map/ppermute | solution.py:424
  86.4 4.8 %collective-permute-start.3 = (bf16[32,32,128]{2,1,0:T(8,128)(2,1)S(1)}, bf16[32,32,128]{2,1,0:T(8,128)(2,1)S(1)}, u32[]{:S(2)}, u32[]{:S(2)}) collective-permute-start(bf16[32,32,128]{2,1,0:T(8,128)(2,1)S(1)} %all_to_all.15.h_ref), channel_id=1, source_target_pairs={{0,4},{4,0},{1,5},{5,1},{2,6},{6,2},{3,7},{7,3},{8,12},{12,8},{9,1... | collective-permute-start | bytes 786440 | tf_op jit(solution)/shard_map/ppermute | solution.py:429

commit v5 on v4

--- a/solution.py
+++ b/solution.py
@@ -169,7 +169,7 @@
 
 
 def state_kernel(
-    arrived_ref, rate_ref, perm_ref, cnt_ref, x_hbm, bc_ref, cum_ref, step_ref, msg_ref, sums_ref, x_ref, x_sems
+    arrived_ref, rate_ref, perm_ref, cnt_ref, x_hbm, bc_ref, cum_ref, step_ref, msg_hbm, sums_ref, x_ref, x_sems, msg_ref, msg_sems
 ):
     top = iota((NP, 8, T), 1) < 4
 
@@ -226,6 +226,9 @@
                 for k in range(2):
                     m = (4 * g + pair) * 2 + k
                     msg_ref[m] = h[32 * k : 32 * k + 32, T * pair : T * pair + T]
+            part = pl.ds(8 * g, 8)
+            x_copies.append(pltpu.make_async_copy(msg_ref.at[part], msg_hbm.at[part], msg_sems.at[g]))
+            x_copies[-1].start()
     for copy in x_copies:
         copy.wait()
 
@@ -247,23 +250,29 @@
     factor_ref[...] = of_span(carry, core)
     e = expander()
     entry = dot(of_span(two_parts(entry), 1), e)
+    causal = iota((T, T), 0) >= iota((T, T), 1)
+    keeps, scores = [], []
+    for i in range(2):
+        here = pl.ds(T * i, T)
+        count = jnp.broadcast_to(cnt[:, HH * i : HH * i + 1], (T, T))
+        keeps.append(causal & (count == count.T))
+        for g in range(4):
+            lanes = slice(N * (g % 2), N * (g % 2) + N)
+            b = bc_ref[here, pl.ds(T * (g // 2), T)][:, lanes]
+            c = bc_ref[here, pl.ds(2 * T + T * (g // 2), T)][:, lanes]
+            scores.append(dot_nt(c, b))
     x_copy.wait()
     inner = dot(of_span(inner_weights(cum, step, cnt), 0), e)
     weighted = [
         (x_tile(x_ref, pl.ds(0, T), t).astype(F32) * inner[:, T * t : T * t + T]).astype(BF16) for t in range(16)
     ]
-    causal = iota((T, T), 0) >= iota((T, T), 1)
     left = iota((T, T), 1) < HP
     for i in range(2):
         here = pl.ds(T * i, T)
-        count = jnp.broadcast_to(cnt[:, HH * i : HH * i + 1], (T, T))
-        keep = causal & (count == count.T)
         for g in range(4):
             tile, half = g // 2, g % 2
-            b = bc_ref[here, pl.ds(T * tile, T)][:, N * half : N * half + N]
-            c = bc_ref[here, pl.ds(2 * T + T * tile, T)][:, N * half : N * half + N]
-            scores = dot_nt(c, b)
             if i == 1:
+                c = bc_ref[here, pl.ds(2 * T + T * tile, T)][:, N * half : N * half + N]
                 lanes = slice(GW * g, GW * g + GW)
                 first = bc_ref[pl.ds(0, T), pl.ds(T * tile, T)].astype(F32).T[N * half : N * half + N].astype(BF16)
                 state = dot(first, jnp.concatenate(weighted[4 * g : 4 * g + 4], axis=1)).astype(BF16)
@@ -273,7 +282,7 @@
                 for h in (2 * pair, 2 * pair + 1):
                     col = HH * i + HG * g + h
                     gap = cum_ref[:, col : col + 1] - key_ref[col : col + 1, :]
-                    weights.append((jnp.exp(jnp.where(keep, gap, -jnp.inf)) * scores).astype(BF16))
+                    weights.append((jnp.exp(jnp.where(keeps[i], gap, -jnp.inf)) * scores[4 * i + g]).astype(BF16))
                 lanes = pl.ds(GW * g + T * pair, T)
                 x = x_tile(x_ref, here, 4 * g + pair)
                 zero = jnp.zeros_like(x)
@@ -307,24 +316,30 @@
         h = decay_ref[pl.ds(p, 1), :] * h + in_ref[at].astype(F32)
 
 
-def carried(c, h_ref, g, scale):
-    state = jnp.concatenate(
+def entering(h_ref, g):
+    return jnp.concatenate(
         [jnp.concatenate([h_ref[8 * g + 2 * p], h_ref[8 * g + 2 * p + 1]], axis=0) for p in range(4)], axis=1
     )
-    return dot(c, state) * scale[:, GW * g : GW * g + GW]
-
-
-def mine_kernel(partial_ref, bc_ref, factor_ref, h_ref, out_ref):
+
+
+def mine_kernel(partial_ref, bc_ref, factor_ref, h_ref, swap_ref, out_ref, scale_ref, partial2_ref, c2_ref):
     core = lax.axis_index("c")
-    scale = dot(factor_ref[...], expander())
+    e = expander()
+    scale = dot(factor_ref[...], e)
     cs = bc_ref[pl.ds(pl.multiple_of(T * core, T), T), pl.ds(2 * T, 2 * T)]
     for g in range(4):
         lanes = pl.ds(GW * g, GW)
-        inter = carried(cs[:, N * g : N * g + N], h_ref, g, scale)
+        inter = dot(cs[:, N * g : N * g + N], entering(h_ref, g)) * scale[:, GW * g : GW * g + GW]
         out_ref[:, lanes] = (partial_ref[:, lanes] + inter).astype(BF16)
-
-
-def final_kernel(mine_ref, swap_ref, h_ref, out_hbm, other_ref, sems):
+    c2_ref[...] = swap_ref[:, pl.ds(2 * HW, 2 * T)]
+    scale_ref[...] = dot(swap_ref[:, pl.ds(2 * HW + 2 * T, T)], e)
+    for g in range(4):
+        lanes = pl.ds(GW * g, GW)
+        low = swap_ref[:, pl.ds(HW + GW * g, GW)]
+        partial2_ref[:, lanes] = swap_ref[:, lanes].astype(F32) + low.astype(F32)
+
+
+def final_kernel(mine_ref, scale_ref, partial_ref, c_ref, h_ref, out_hbm, other_ref, sems):
     core = lax.axis_index("c")
 
     def copy(src, n, half):
@@ -336,12 +351,11 @@
         def _():
             copy(mine_ref, 0, k).start()
 
-    scale = dot(swap_ref[:, pl.ds(2 * HW + 2 * T, T)], expander())
-    cs = swap_ref[:, pl.ds(2 * HW, 2 * T)]
+    cs = c_ref[...]
     for g in range(4):
         lanes = pl.ds(GW * g, GW)
-        partial = swap_ref[:, lanes].astype(F32) + swap_ref[:, pl.ds(HW + GW * g, GW)].astype(F32)
-        inter = carried(cs[:, N * g : N * g + N], h_ref, g, scale)
+        inter = dot(cs[:, N * g : N * g + N], entering(h_ref, g)) * scale_ref[:, lanes]
+        partial = partial_ref[:, lanes]
         other_ref[:, lanes] = (partial + inter).astype(BF16)
     for k in range(2):
 
@@ -401,8 +415,13 @@
             sds((NP, 32, T), BF16),
             sds((8, T), F32),
         ),
-        out_specs=(hbm,) + (vmem,) * 5,
-        scratch_shapes=[pltpu.VMEM((2 * T, HW), BF16), pltpu.SemaphoreType.DMA((4,))],
+        out_specs=(hbm,) + (vmem,) * 3 + (hbm, vmem),
+        scratch_shapes=[
+            pltpu.VMEM((2 * T, HW), BF16),
+            pltpu.SemaphoreType.DMA((4,)),
+            pltpu.VMEM((NP, 32, T), BF16),
+            pltpu.SemaphoreType.DMA((4,)),
+        ],
         compiler_params=params(24),
         name="state",
     )(arrived, rate_row, perm, cnt)
@@ -422,23 +441,26 @@
         name="local",
     )(xs, bc, cum, step, cnt, skip_row, sums, pair_row)
     swap = lax.ppermute(swap, "c", [(0, 1), (1, 0)])
-    entering = pl.pallas_call(
+    prefixes = pl.pallas_call(
         scan_kernel, out_shape=sds((NP, 32, T), BF16), compiler_params=params(16), name="chips"
     )(totals, decays)
-    states = lax.all_to_all(entering, ("x", "z"), split_axis=0, concat_axis=0, tiled=True)
+    states = lax.all_to_all(prefixes, ("x", "z"), split_axis=0, concat_axis=0, tiled=True)
     other = lax.ppermute(states, "c", [(0, 1), (1, 0)])
-    own = pl.pallas_call(
-        mine_kernel, out_shape=sds((T, HW), BF16), compiler_params=params(20), name="mine"
-    )(partial, bc, factors, states)
+    own, scale, partial2, c2 = pl.pallas_call(
+        mine_kernel,
+        out_shape=(sds((T, HW), BF16), sds((T, HW), F32), sds((T, HW), F32), sds((T, 2 * T), BF16)),
+        compiler_params=params(20),
+        name="mine",
+    )(partial, bc, factors, states, swap)
     return pl.pallas_call(
         final_kernel,
         out_shape=sds((T, 2 * HW), BF16),
-        in_specs=[pl.BlockSpec(memory_space=pltpu.VMEM)] * 3,
+        in_specs=[vmem] * 5,
         out_specs=hbm,
         scratch_shapes=[pltpu.VMEM((T, HW), BF16), pltpu.SemaphoreType.DMA((2,))],
         compiler_params=params(20),
         name="final",
-    )(own, swap, other)
+    )(own, scale, partial2, c2, other)
 
 
 def solution(mesh):

time: 92.7 us -> 92.3 us (level)
  transfers between devices with their start and end apart: 6 -> 6, of which waited for: 5 -> 5; matrix products, arithmetic and copies ran while one was open for 1% -> 1% of each run, Pallas kernels for 7% -> 6%
where the time goes in v5:
time: 92.3 us; the launch traced here: 92 us
  waiting for transfers between devices  39.3 us (43%)
  starting transfers between devices  24 us (26%)
  blocking collectives  15.8 us (17%)
  Pallas kernels  12.2 us (13%)
    all_to_all x1, waiting for transfers between devices, per_device(): lax.all_to_all(packed, ('x', 'c', 'z'), split_axis=0, concat_axis=0, tile...  34.7 us
    all_to_all x1, blocking collectives, per_device(): lax.all_to_all(prefixes, ('x', 'z'), split_axis=0, concat_axis=0, tiled=T...  15.8 us
    all_to_all x1, starting transfers between devices, per_device(): lax.all_to_all(packed, ('x', 'c', 'z'), split_axis=0, concat_axis=0, tile...  13.1 us
    all_to_all x1, starting transfers between devices, per_device(): lax.all_to_all(msg, ('x', 'z'), split_axis=0, concat_axis=0, tiled=True)  5.59 us
    pallas_call x1, Pallas kernels, per_device(): pl.pallas_call(local_kernel, out_shape=(sds((T, HW), F32), sds((T, T), BF...  4.94 us
    all_to_all x1, waiting for transfers between devices, per_device(): lax.all_to_all(msg, ('x', 'z'), split_axis=0, concat_axis=0, tiled=True)  3.7 us
    ppermute x1, starting transfers between devices, per_device(): other = lax.ppermute(states, 'c', [(0, 1), (1, 0)])  3.6 us
    pallas_call x1, Pallas kernels, per_device(): pl.pallas_call(pack_kernel, out_shape=sds((2 * NX, NZ, MSG, T), BF16), in...  2.85 us
  transfers between devices with their start and end apart: 6, of which 5 were waited for; matrix products, arithmetic and copies ran while one was open for 1% of the time, Pallas kernels for 6%

profile of v5, /device:TPU:1, one launch (start us, length us, event | category | flops | bytes accessed | tf_op | source)
XLA Modules:
  0.0 92.0 jit_solution(1194189462387804163)
XLA Ops:
  0.0 2.8 %pack.1 = bf16[8,8,88,128]{3,2,1,0:T(8,128)(2,1)} custom-call(bf16[128,4096]{1,0:T(8,128)(2,1)} %x_hbm.1, bf16[128,512]{1,0:T(8,128)(2,1)} %b_hbm.1, bf16[128,512]{1,0:T(8,128)(2,1)} %c_hbm.1, bf16[64,128]{1,0:T(8,128)(2,1)} %bitcast.9, s32[1,128]{1,0:T(1,128)} %bitcast.5), custom_call_target="tpu_custom_call" | custom-call | tf_op jit(solution)/shard_map/pack/pallas_call | solution.py:374
  2.9 0.0 copy-start
  2.9 0.0 copy-start.1
  2.9 0.0 copy-start.2
  2.9 0.0 copy-start.3
  2.9 13.1 %all-to-all-start = ((bf16[64,88,128]{2,1,0:T(8,128)(2,1)}), bf16[64,88,128]{2,1,0:T(8,128)(2,1)S(1)}, u32[]{:S(2)}, u32[]{:S(2)}) async-start(bf16[64,88,128]{2,1,0:T(8,128)(2,1)} %bitcast.8), calls=%async_computation | async-start | bytes 2883584 | tf_op jit(solution)/shard_map/all_to_all | solution.py:393
  16.0 0.0 copy-done
  16.1 0.5 collective-permute-start.1
  16.6 0.0 copy-done.1
  16.6 0.1 collective-permute-start
  16.7 0.0 copy-done.2
  16.7 0.1 dynamic_slice.9
  16.8 0.1 maximum_bitcast_fusion.rate_ref
  16.9 0.1 dynamic_slice.11
  16.9 0.0 copy-done.3
  16.9 0.1 dynamic_slice.10
  17.0 0.1 broadcast_in_dim.11
  17.1 0.1 reshape_reshape.7.pair_ref
  17.2 0.1 broadcast_in_dim.10
  17.2 0.1 reshape_reshape.6.skip_ref
  17.3 0.1 collective-permute-done.1.reset2_ref
  17.4 0.3 collective-permute-done.order2_ref
  17.7 0.2 plan.1
  18.0 34.7 %all-to-all-done.arrived_ref = bf16[64,88,128]{2,1,0:T(8,128)(2,1)S(1)} async-done(((bf16[64,88,128]{2,1,0:T(8,128)(2,1)}), bf16[64,88,128]{2,1,0:T(8,128)(2,1)S(1)}, u32[]{:S(2)}, u32[]{:S(2)}) %all-to-all-start) | async-done | bytes 1441824 | tf_op jit(solution)/shard_map/all_to_all | solution.py:393
  52.7 2.3 %state.1 = (bf16[12288,2048]{1,0:T(8,128)(2,1)}, bf16[256,512]{1,0:T(8,128)(2,1)S(1)}, f32[128,128]{1,0:T(8,128)S(1)}, f32[128,128]{1,0:T(8,128)S(1)}, bf16[32,3...) custom-call(bf16[64,88,128]{2,1,0:T(8,128)(2,1)S(1)} %all-to-all-done.arrived_ref, f32[1,128]{1,0:T(1,128)S(1)} %maximum_bitcast_fusion.rate_ref, ...), custom_call_target="tpu_custom_call" | custom-call | tf_op jit(solution)/shard_map/state/pallas_call | solution.py:408
  55.0 5.6 %all-to-all-start.1 = ((bf16[32,32,128]{2,1,0:T(8,128)(2,1)}), bf16[32,32,128]{2,1,0:T(8,128)(2,1)S(1)}, u32[]{:S(2)}, u32[]{:S(2)}) async-start(bf16[32,32,128]{2,1,0:T(8,128)(2,1)} %get-tuple-element.30), calls=%async_computation.1 | async-start | bytes 524288 | tf_op jit(solution)/shard_map/all_to_all | solution.py:428
  60.6 4.9 %local.1 = (f32[128,2048]{1,0:T(8,128)S(1)}, bf16[128,128]{1,0:T(8,128)(2,1)S(1)}, bf16[128,4480]{1,0:T(8,128)(2,1)}, f32[32,128]{1,0:T(8,128)S(1)}) custom-call(bf16[12288,2048]{1,0:T(8,128)(2,1)} %get-tuple-element.23.x_hbm, bf16[256,512]{1,0:T(8,128)(2,1)S(1)} %get-tuple-element.24.bc_ref, f32[128,128]{1,0:T(8,128)S(1)} %get-tuple-element.25.cum_ref, ...), custom_call_target="tpu_custom_call" | custom-call | flops 2000000000 | bytes 6000000 | tf_op jit(solution)/shard_map/local/pallas_call | solution.py:429
  65.5 1.0 %collective-permute-start.2 = (bf16[128,4480]{1,0:T(8,128)(2,1)}, bf16[128,4480]{1,0:T(8,128)(2,1)S(1)}, u32[]{:S(2)}, u32[]{:S(2)}) collective-permute-start(bf16[128,4480]{1,0:T(8,128)(2,1)} %get-tuple-element.32), channel_id=1, source_target_pairs={{0,4},{4,0},{1,5},{5,1},{2,6},{6,2},{3,7},{7,3},{8,12},{12,8},{9,1... | collective-permute-start | bytes 3440648 | tf_op jit(solution)/shard_map/ppermute | solution.py:443
  66.6 3.7 %all-to-all-done.1.in_ref = bf16[32,32,128]{2,1,0:T(8,128)(2,1)S(1)} async-done(((bf16[32,32,128]{2,1,0:T(8,128)(2,1)}), bf16[32,32,128]{2,1,0:T(8,128)(2,1)S(1)}, u32[]{:S(2)}, u32[]{:S(2)}) %all-to-all-start.1) | async-done | bytes 262176 | tf_op jit(solution)/shard_map/all_to_all | solution.py:428
  70.3 0.1 chips.1
  70.4 15.8 %all_to_all.15.h_ref = bf16[32,32,128]{2,1,0:T(8,128)(2,1)S(1)} all-to-all(bf16[32,32,128]{2,1,0:T(8,128)(2,1)S(1)} %chips.1), channel_id=1, replica_groups=mesh['z'=8,'x'=4,'c'=2,'seq'=4] {'x','z'}, dimensions={0} | all-to-all | bytes 524288 | tf_op jit(solution)/shard_map/all_to_all | solution.py:447
  86.1 3.6 %collective-permute-start.3 = (bf16[32,32,128]{2,1,0:T(8,128)(2,1)S(1)}, bf16[32,32,128]{2,1,0:T(8,128)(2,1)S(1)}, u32[]{:S(2)}, u32[]{:S(2)}) collective-permute-start(bf16[32,32,128]{2,1,0:T(8,128)(2,1)S(1)} %all_to_all.15.h_ref), channel_id=1, source_target_pairs={{0,4},{4,0},{1,5},{5,1},{2,6},{6,2},{3,7},{7,3},{8,12},{12,8},{9,1... | collective-permute-start | bytes 786440 | tf_op jit(solution)/shard_map/ppermute | solution.py:448
  89.7 0.0 collective-permute-done.2.swap_ref
  89.7 0.7 mine.1
  90.4 0.5 collective-permute-done.3.h_ref
  90.9 1.1 %final.1 = bf16[128,4096]{1,0:T(8,128)(2,1)} custom-call(bf16[128,2048]{1,0:T(8,128)(2,1)S(1)} %get-tuple-element.33.mine_ref, f32[128,2048]{1,0:T(8,128)S(1)} %get-tuple-element.34.scale_ref, f32[128,2048]{1,0:T(8,128)S(1)} %get-tuple-element.35.partial_ref, bf16[128,256]{1,0:T(8,128)(2,1)S(1)} %get-tuple-element.36.c_ref, ...), custom_call_target="tpu_custom_call" | custom-call | tf_op jit(solution)/shard_map/final/pallas_call | solution.py:455
  (1 shorter events, 0.0 us)
Async XLA Ops:
  2.9 13.2 %copy-start = (s32[128]{0:T(128)S(1)}, s32[128]{0:T(128)}, u32[]{:S(2)}) copy-start(s32[128]{0:T(128)} %param.13) | copy-start | bytes 1540
  2.9 13.7 %copy-start.1 = (s32[1,128]{1,0:T(1,128)S(1)}, s32[1,128]{1,0:T(1,128)}, u32[]{:S(2)}) copy-start(s32[1,128]{1,0:T(1,128)} %order_ref.1) | copy-start | bytes 1540
  2.9 13.8 %copy-start.2 = (f32[64]{0:T(128)S(1)}, f32[64]{0:T(128)}, u32[]{:S(2)}) copy-start(f32[64]{0:T(128)} %param.14) | copy-start | bytes 772
  2.9 14.0 %copy-start.3 = (f32[64]{0:T(128)S(1)}, f32[64]{0:T(128)}, u32[]{:S(2)}) copy-start(f32[64]{0:T(128)} %param.15) | copy-start | bytes 772
  2.9 49.8 %all-to-all-start = ((bf16[64,88,128]{2,1,0:T(8,128)(2,1)}), bf16[64,88,128]{2,1,0:T(8,128)(2,1)S(1)}, u32[]{:S(2)}, u32[]{:S(2)}) async-start(bf16[64,88,128]{2,1,0:T(8,128)(2,1)} %bitcast.8), calls=%async_computation | async-start | bytes 2883584 | tf_op jit(solution)/shard_map/all_to_all | solution.py:393
  16.1 1.4 %collective-permute-start.1 = (s32[1,128]{1,0:T(1,128)S(1)}, s32[1,128]{1,0:T(1,128)S(1)}, u32[]{:S(2)}, u32[]{:S(2)}) collective-permute-start(s32[1,128]{1,0:T(1,128)S(1)} %bitcast.6), channel_id=1, source_target_pairs={{0,4},{4,0},{1,5},{5,1},{2,6},{6,2},{3,7},{7,3},{8,12},{12,8},{9,1... | collective-permute-start | bytes 1544 | tf_op jit(solution)/shard_map/ppermute | solution.py:395
  16.6 1.1 %collective-permute-start = (s32[1,128]{1,0:T(1,128)S(1)}, s32[1,128]{1,0:T(1,128)S(1)}, u32[]{:S(2)}, u32[]{:S(2)}) collective-permute-start(s32[1,128]{1,0:T(1,128)S(1)} %copy-done.1), channel_id=1, source_target_pairs={{0,4},{4,0},{1,5},{5,1},{2,6},{6,2},{3,7},{7,3},{8,12},{12,8},{9,1... | collective-permute-start | bytes 1544 | tf_op jit(solution)/shard_map/ppermute | solution.py:394
  55.0 15.3 %all-to-all-start.1 = ((bf16[32,32,128]{2,1,0:T(8,128)(2,1)}), bf16[32,32,128]{2,1,0:T(8,128)(2,1)S(1)}, u32[]{:S(2)}, u32[]{:S(2)}) async-start(bf16[32,32,128]{2,1,0:T(8,128)(2,1)} %get-tuple-element.30), calls=%async_computation.1 | async-start | bytes 524288 | tf_op jit(solution)/shard_map/all_to_all | solution.py:428
  65.5 24.2 %collective-permute-start.2 = (bf16[128,4480]{1,0:T(8,128)(2,1)}, bf16[128,4480]{1,0:T(8,128)(2,1)S(1)}, u32[]{:S(2)}, u32[]{:S(2)}) collective-permute-start(bf16[128,4480]{1,0:T(8,128)(2,1)} %get-tuple-element.32), channel_id=1, source_target_pairs={{0,4},{4,0},{1,5},{5,1},{2,6},{6,2},{3,7},{7,3},{8,12},{12,8},{9,1... | collective-permute-start | bytes 3440648 | tf_op jit(solution)/shard_map/ppermute | solution.py:443
  86.1 4.8 %collective-permute-start.3 = (bf16[32,32,128]{2,1,0:T(8,128)(2,1)S(1)}, bf16[32,32,128]{2,1,0:T(8,128)(2,1)S(1)}, u32[]{:S(2)}, u32[]{:S(2)}) collective-permute-start(bf16[32,32,128]{2,1,0:T(8,128)(2,1)S(1)} %all_to_all.15.h_ref), channel_id=1, source_target_pairs={{0,4},{4,0},{1,5},{5,1},{2,6},{6,2},{3,7},{7,3},{8,12},{12,8},{9,1... | collective-permute-start | bytes 786440 | tf_op jit(solution)/shard_map/ppermute | solution.py:448

commit v6 on v5

--- a/solution.py
+++ b/solution.py
@@ -106,12 +106,12 @@
                 to = 2 * x + c
                 for q in range(5):
                     lanes = slice(T * (5 * c + q), T * (5 * c + q) + T)
-                    out_ref[to, z, pl.ds(16 * q, 16), :] = got[16 * p : 16 * p + 16, lanes]
+                    out_ref[z, to, pl.ds(16 * q, 16), :] = got[16 * p : 16 * p + 16, lanes]
                 m = 8 * (16 * c + (NZ * x + z) // 2)
                 tail = steps[at : at + 8, T * c : T * c + T] + sums[m : m + 8] + flag
-                out_ref[to, z, pl.ds(80, 8), :] = tail.astype(BF16)
+                out_ref[z, to, pl.ds(80, 8), :] = tail.astype(BF16)
         here = pl.ds(NZ // PARTS * part, NZ // PARTS)
-        sent.append(pltpu.make_async_copy(out_ref.at[:, here], out_hbm.at[:, here], out_sems.at[part]))
+        sent.append(pltpu.make_async_copy(out_ref.at[here], out_hbm.at[here], out_sems.at[part]))
         sent[-1].start()
     for copy in sent:
         copy.wait()
@@ -134,7 +134,6 @@
     cnt_ref[...] = jnp.where(iota((T, T), 1) < HH, counts[0], counts[1])
     order = jnp.concatenate(orders, axis=0).astype(I32)
     source = order >> 1
-    source = ((source & (NZ - 1)) << 3) + (source >> 3)
     target = (source << 2) + ((iota((256, T), 0) >> 7) << 1) + (order & 1)
     for m in range(2):
         perm_ref[:, pl.ds(T * m, T)] = jnp.where(iota((256, T), 1) + T * m == target, 1.0, 0.0).astype(BF16)
@@ -373,7 +372,7 @@
     resets = resets.reshape(1, T)
     packed = pl.pallas_call(
         pack_kernel,
-        out_shape=sds((2 * NX, NZ, MSG, T), BF16),
+        out_shape=sds((NZ, 2 * NX, MSG, T), BF16),
         in_specs=[hbm] * 5,
         out_specs=hbm,
         scratch_shapes=[
@@ -382,7 +381,7 @@
             pltpu.VMEM(c.shape, BF16),
             pltpu.VMEM(dt.shape[::-1], BF16),
             pltpu.VMEM((1, T), I32),
-            pltpu.VMEM((2 * NX, NZ, MSG, T), BF16),
+            pltpu.VMEM((NZ, 2 * NX, MSG, T), BF16),
             pltpu.SemaphoreType.DMA((2 + 3 * PARTS,)),
             pltpu.SemaphoreType.DMA((PARTS,)),
         ],
@@ -390,7 +389,7 @@
         name="pack",
     )(x, b, c, dt.T, resets)
     packed = packed.reshape(2 * NP, MSG, T)
-    arrived = lax.all_to_all(packed, ("x", "c", "z"), split_axis=0, concat_axis=0, tiled=True)
+    arrived = lax.all_to_all(packed, ("z", "x", "c"), split_axis=0, concat_axis=0, tiled=True)
     order2 = lax.ppermute(order, "c", [(0, 1), (1, 0)])
     resets2 = lax.ppermute(resets, "c", [(0, 1), (1, 0)])
     perm, cnt = pl.pallas_call(

time: 92.3 us -> 91.4 us (level)
  transfers between devices with their start and end apart: 6 -> 6, of which waited for: 5 -> 5; matrix products, arithmetic and copies ran while one was open for 1% -> 1% of each run, Pallas kernels for 6% -> 7%
where the time goes in v6:
time: 91.4 us; the launch traced here: 91 us
  waiting for transfers between devices  38.9 us (43%)
  starting transfers between devices  23.7 us (26%)
  blocking collectives  15.5 us (17%)
  Pallas kernels  12.2 us (13%)
    all_to_all x1, waiting for transfers between devices, per_device(): lax.all_to_all(packed, ('z', 'x', 'c'), split_axis=0, concat_axis=0, tile...  34.4 us
    all_to_all x1, blocking collectives, per_device(): lax.all_to_all(prefixes, ('x', 'z'), split_axis=0, concat_axis=0, tiled=T...  15.5 us
    all_to_all x1, starting transfers between devices, per_device(): lax.all_to_all(packed, ('z', 'x', 'c'), split_axis=0, concat_axis=0, tile...  13.1 us
    all_to_all x1, starting transfers between devices, per_device(): lax.all_to_all(msg, ('x', 'z'), split_axis=0, concat_axis=0, tiled=True)  5.06 us
    pallas_call x1, Pallas kernels, per_device(): pl.pallas_call(local_kernel, out_shape=(sds((T, HW), F32), sds((T, T), BF...  4.94 us
    ppermute x1, starting transfers between devices, per_device(): other = lax.ppermute(states, 'c', [(0, 1), (1, 0)])  3.68 us
    all_to_all x1, waiting for transfers between devices, per_device(): lax.all_to_all(msg, ('x', 'z'), split_axis=0, concat_axis=0, tiled=True)  3.57 us
    pallas_call x1, Pallas kernels, per_device(): pl.pallas_call(pack_kernel, out_shape=sds((NZ, 2 * NX, MSG, T), BF16), in...  2.88 us
  transfers between devices with their start and end apart: 6, of which 5 were waited for; matrix products, arithmetic and copies ran while one was open for 1% of the time, Pallas kernels for 7%

profile of v6, /device:TPU:1, one launch (start us, length us, event | category | flops | bytes accessed | tf_op | source)
XLA Modules:
  0.0 91.0 jit_solution(7979438509615086693)
XLA Ops:
  0.0 2.9 %pack.1 = bf16[8,8,88,128]{3,2,1,0:T(8,128)(2,1)} custom-call(bf16[128,4096]{1,0:T(8,128)(2,1)} %x_hbm.1, bf16[128,512]{1,0:T(8,128)(2,1)} %b_hbm.1, bf16[128,512]{1,0:T(8,128)(2,1)} %c_hbm.1, bf16[64,128]{1,0:T(8,128)(2,1)} %bitcast.9, s32[1,128]{1,0:T(1,128)} %bitcast.5), custom_call_target="tpu_custom_call" | custom-call | tf_op jit(solution)/shard_map/pack/pallas_call | solution.py:373
  2.9 0.0 copy-start
  2.9 0.0 copy-start.1
  2.9 0.0 copy-start.2
  2.9 0.0 copy-start.3
  2.9 13.1 %all-to-all-start = ((bf16[64,88,128]{2,1,0:T(8,128)(2,1)}), bf16[64,88,128]{2,1,0:T(8,128)(2,1)S(1)}, u32[]{:S(2)}, u32[]{:S(2)}) async-start(bf16[64,88,128]{2,1,0:T(8,128)(2,1)} %bitcast.8), calls=%async_computation | async-start | bytes 2883584 | tf_op jit(solution)/shard_map/all_to_all | solution.py:392
  16.1 0.0 copy-done
  16.1 0.5 collective-permute-start.1
  16.6 0.0 copy-done.1
  16.6 0.1 collective-permute-start
  16.7 0.0 copy-done.2
  16.7 0.1 dynamic_slice.9
  16.8 0.1 maximum_bitcast_fusion.rate_ref
  16.9 0.1 dynamic_slice.11
  17.0 0.0 copy-done.3
  17.0 0.1 dynamic_slice.10
  17.0 0.1 broadcast_in_dim.11
  17.1 0.1 reshape_reshape.7.pair_ref
  17.2 0.1 broadcast_in_dim.10
  17.3 0.1 reshape_reshape.6.skip_ref
  17.3 0.1 collective-permute-done.1.reset2_ref
  17.4 0.3 collective-permute-done.order2_ref
  17.7 0.2 plan.1
  18.0 34.4 %all-to-all-done.arrived_ref = bf16[64,88,128]{2,1,0:T(8,128)(2,1)S(1)} async-done(((bf16[64,88,128]{2,1,0:T(8,128)(2,1)}), bf16[64,88,128]{2,1,0:T(8,128)(2,1)S(1)}, u32[]{:S(2)}, u32[]{:S(2)}) %all-to-all-start) | async-done | bytes 1441824 | tf_op jit(solution)/shard_map/all_to_all | solution.py:392
  52.4 2.3 %state.1 = (bf16[12288,2048]{1,0:T(8,128)(2,1)}, bf16[256,512]{1,0:T(8,128)(2,1)S(1)}, f32[128,128]{1,0:T(8,128)S(1)}, f32[128,128]{1,0:T(8,128)S(1)}, bf16[32,3...) custom-call(bf16[64,88,128]{2,1,0:T(8,128)(2,1)S(1)} %all-to-all-done.arrived_ref, f32[1,128]{1,0:T(1,128)S(1)} %maximum_bitcast_fusion.rate_ref, ...), custom_call_target="tpu_custom_call" | custom-call | tf_op jit(solution)/shard_map/state/pallas_call | solution.py:407
  54.7 5.1 %all-to-all-start.1 = ((bf16[32,32,128]{2,1,0:T(8,128)(2,1)}), bf16[32,32,128]{2,1,0:T(8,128)(2,1)S(1)}, u32[]{:S(2)}, u32[]{:S(2)}) async-start(bf16[32,32,128]{2,1,0:T(8,128)(2,1)} %get-tuple-element.30), calls=%async_computation.1 | async-start | bytes 524288 | tf_op jit(solution)/shard_map/all_to_all | solution.py:427
  59.8 4.9 %local.1 = (f32[128,2048]{1,0:T(8,128)S(1)}, bf16[128,128]{1,0:T(8,128)(2,1)S(1)}, bf16[128,4480]{1,0:T(8,128)(2,1)}, f32[32,128]{1,0:T(8,128)S(1)}) custom-call(bf16[12288,2048]{1,0:T(8,128)(2,1)} %get-tuple-element.23.x_hbm, bf16[256,512]{1,0:T(8,128)(2,1)S(1)} %get-tuple-element.24.bc_ref, f32[128,128]{1,0:T(8,128)S(1)} %get-tuple-element.25.cum_ref, ...), custom_call_target="tpu_custom_call" | custom-call | flops 2000000000 | bytes 6000000 | tf_op jit(solution)/shard_map/local/pallas_call | solution.py:428
  64.8 1.2 %collective-permute-start.2 = (bf16[128,4480]{1,0:T(8,128)(2,1)}, bf16[128,4480]{1,0:T(8,128)(2,1)S(1)}, u32[]{:S(2)}, u32[]{:S(2)}) collective-permute-start(bf16[128,4480]{1,0:T(8,128)(2,1)} %get-tuple-element.32), channel_id=1, source_target_pairs={{0,4},{4,0},{1,5},{5,1},{2,6},{6,2},{3,7},{7,3},{8,12},{12,8},{9,1... | collective-permute-start | bytes 3440648 | tf_op jit(solution)/shard_map/ppermute | solution.py:442
  65.9 3.6 %all-to-all-done.1.in_ref = bf16[32,32,128]{2,1,0:T(8,128)(2,1)S(1)} async-done(((bf16[32,32,128]{2,1,0:T(8,128)(2,1)}), bf16[32,32,128]{2,1,0:T(8,128)(2,1)S(1)}, u32[]{:S(2)}, u32[]{:S(2)}) %all-to-all-start.1) | async-done | bytes 262176 | tf_op jit(solution)/shard_map/all_to_all | solution.py:427
  69.5 0.1 chips.1
  69.6 15.5 %all_to_all.15.h_ref = bf16[32,32,128]{2,1,0:T(8,128)(2,1)S(1)} all-to-all(bf16[32,32,128]{2,1,0:T(8,128)(2,1)S(1)} %chips.1), channel_id=1, replica_groups=mesh['z'=8,'x'=4,'c'=2,'seq'=4] {'x','z'}, dimensions={0} | all-to-all | bytes 524288 | tf_op jit(solution)/shard_map/all_to_all | solution.py:446
  85.1 3.7 %collective-permute-start.3 = (bf16[32,32,128]{2,1,0:T(8,128)(2,1)S(1)}, bf16[32,32,128]{2,1,0:T(8,128)(2,1)S(1)}, u32[]{:S(2)}, u32[]{:S(2)}) collective-permute-start(bf16[32,32,128]{2,1,0:T(8,128)(2,1)S(1)} %all_to_all.15.h_ref), channel_id=1, source_target_pairs={{0,4},{4,0},{1,5},{5,1},{2,6},{6,2},{3,7},{7,3},{8,12},{12,8},{9,1... | collective-permute-start | bytes 786440 | tf_op jit(solution)/shard_map/ppermute | solution.py:447
  88.8 0.0 collective-permute-done.2.swap_ref
  88.8 0.7 mine.1
  89.5 0.5 collective-permute-done.3.h_ref
  89.9 1.1 %final.1 = bf16[128,4096]{1,0:T(8,128)(2,1)} custom-call(bf16[128,2048]{1,0:T(8,128)(2,1)S(1)} %get-tuple-element.33.mine_ref, f32[128,2048]{1,0:T(8,128)S(1)} %get-tuple-element.34.scale_ref, f32[128,2048]{1,0:T(8,128)S(1)} %get-tuple-element.35.partial_ref, bf16[128,256]{1,0:T(8,128)(2,1)S(1)} %get-tuple-element.36.c_ref, ...), custom_call_target="tpu_custom_call" | custom-call | tf_op jit(solution)/shard_map/final/pallas_call | solution.py:454
  (1 shorter events, 0.0 us)
Async XLA Ops:
  2.9 13.2 %copy-start = (s32[128]{0:T(128)S(1)}, s32[128]{0:T(128)}, u32[]{:S(2)}) copy-start(s32[128]{0:T(128)} %param.13) | copy-start | bytes 1540
  2.9 13.7 %copy-start.1 = (s32[1,128]{1,0:T(1,128)S(1)}, s32[1,128]{1,0:T(1,128)}, u32[]{:S(2)}) copy-start(s32[1,128]{1,0:T(1,128)} %order_ref.1) | copy-start | bytes 1540
  2.9 13.8 %copy-start.2 = (f32[64]{0:T(128)S(1)}, f32[64]{0:T(128)}, u32[]{:S(2)}) copy-start(f32[64]{0:T(128)} %param.14) | copy-start | bytes 772
  2.9 14.0 %copy-start.3 = (f32[64]{0:T(128)S(1)}, f32[64]{0:T(128)}, u32[]{:S(2)}) copy-start(f32[64]{0:T(128)} %param.15) | copy-start | bytes 772
  2.9 49.5 %all-to-all-start = ((bf16[64,88,128]{2,1,0:T(8,128)(2,1)}), bf16[64,88,128]{2,1,0:T(8,128)(2,1)S(1)}, u32[]{:S(2)}, u32[]{:S(2)}) async-start(bf16[64,88,128]{2,1,0:T(8,128)(2,1)} %bitcast.8), calls=%async_computation | async-start | bytes 2883584 | tf_op jit(solution)/shard_map/all_to_all | solution.py:392
  16.1 1.4 %collective-permute-start.1 = (s32[1,128]{1,0:T(1,128)S(1)}, s32[1,128]{1,0:T(1,128)S(1)}, u32[]{:S(2)}, u32[]{:S(2)}) collective-permute-start(s32[1,128]{1,0:T(1,128)S(1)} %bitcast.6), channel_id=1, source_target_pairs={{0,4},{4,0},{1,5},{5,1},{2,6},{6,2},{3,7},{7,3},{8,12},{12,8},{9,1... | collective-permute-start | bytes 1544 | tf_op jit(solution)/shard_map/ppermute | solution.py:394
  16.6 1.1 %collective-permute-start = (s32[1,128]{1,0:T(1,128)S(1)}, s32[1,128]{1,0:T(1,128)S(1)}, u32[]{:S(2)}, u32[]{:S(2)}) collective-permute-start(s32[1,128]{1,0:T(1,128)S(1)} %copy-done.1), channel_id=1, source_target_pairs={{0,4},{4,0},{1,5},{5,1},{2,6},{6,2},{3,7},{7,3},{8,12},{12,8},{9,1... | collective-permute-start | bytes 1544 | tf_op jit(solution)/shard_map/ppermute | solution.py:393
  54.7 14.7 %all-to-all-start.1 = ((bf16[32,32,128]{2,1,0:T(8,128)(2,1)}), bf16[32,32,128]{2,1,0:T(8,128)(2,1)S(1)}, u32[]{:S(2)}, u32[]{:S(2)}) async-start(bf16[32,32,128]{2,1,0:T(8,128)(2,1)} %get-tuple-element.30), calls=%async_computation.1 | async-start | bytes 524288 | tf_op jit(solution)/shard_map/all_to_all | solution.py:427
  64.8 24.0 %collective-permute-start.2 = (bf16[128,4480]{1,0:T(8,128)(2,1)}, bf16[128,4480]{1,0:T(8,128)(2,1)S(1)}, u32[]{:S(2)}, u32[]{:S(2)}) collective-permute-start(bf16[128,4480]{1,0:T(8,128)(2,1)} %get-tuple-element.32), channel_id=1, source_target_pairs={{0,4},{4,0},{1,5},{5,1},{2,6},{6,2},{3,7},{7,3},{8,12},{12,8},{9,1... | collective-permute-start | bytes 3440648 | tf_op jit(solution)/shard_map/ppermute | solution.py:442
  85.1 4.8 %collective-permute-start.3 = (bf16[32,32,128]{2,1,0:T(8,128)(2,1)S(1)}, bf16[32,32,128]{2,1,0:T(8,128)(2,1)S(1)}, u32[]{:S(2)}, u32[]{:S(2)}) collective-permute-start(bf16[32,32,128]{2,1,0:T(8,128)(2,1)S(1)} %all_to_all.15.h_ref), channel_id=1, source_target_pairs={{0,4},{4,0},{1,5},{5,1},{2,6},{6,2},{3,7},{7,3},{8,12},{12,8},{9,1... | collective-permute-start | bytes 786440 | tf_op jit(solution)/shard_map/ppermute | solution.py:447

commit v7 on v6

--- a/solution.py
+++ b/solution.py
@@ -18,7 +18,7 @@
 HH = 32
 HW = HH * HP
 MSG = 88
-PARTS = 2
+PARTS = (64, 48, 16)
 AWAY = 12288
 
 
@@ -54,16 +54,17 @@
     x_ref, b_ref, c_ref, dt_ref, reset_ref, out_ref, sems, out_sems,
 ):
     pairs = [(reset_hbm, reset_ref), (dt_hbm, dt_ref)]
-    span = T // PARTS
-    for part in range(PARTS):
-        rows = pl.ds(span * part, span)
+    for part, span in enumerate(PARTS):
+        rows = pl.ds(sum(PARTS[:part]), span)
         pairs += [(src.at[rows], dst.at[rows]) for src, dst in ((b_hbm, b_ref), (c_hbm, c_ref), (x_hbm, x_ref))]
     copies = [pltpu.make_async_copy(s, d, sems.at[n]) for n, (s, d) in enumerate(pairs)]
     for copy in copies:
         copy.start()
-    row, col = iota((4 * span, 4 * span), 0), iota((4 * span, 4 * span), 1)
-    pick = (col // span == (row % 16) // 4) & (col % span == (row // 16) * 4 + row % 4)
-    pick = pick.astype(BF16)
+    picks = []
+    for span in PARTS:
+        row, col = iota((4 * span, 4 * span), 0), iota((4 * span, 4 * span), 1)
+        pick = (col // span == (row % 16) // 4) & (col % span == (row // 16) * 4 + row % 4)
+        picks.append(pick.astype(BF16))
     lane, head = iota((256, 64), 0), iota((256, 64), 1)
     spread = (lane % T < HH) & (head == (lane // T) * HH + lane % T)
     to, row = iota((256, T), 0), iota((256, T), 1)
@@ -85,10 +86,11 @@
     resets = jnp.sum(reset_ref[...].astype(F32), axis=1, keepdims=True)
     flag = jnp.where(flag, jnp.broadcast_to(resets, (8, T)), 0.0)
     sent = []
-    for part in range(PARTS):
+    for part, span in enumerate(PARTS):
         for copy in copies[2 + 3 * part : 5 + 3 * part]:
             copy.wait()
-        rows = pl.ds(span * part, span)
+        start = sum(PARTS[:part])
+        rows = pl.ds(start, span)
         tiles = []
         for c in range(2):
             for q in range(4):
@@ -98,10 +100,10 @@
                  c_ref[rows, pl.ds(256 * c, T)], c_ref[rows, pl.ds(256 * c + T, T)]]
             )
         right = jnp.concatenate([jnp.concatenate(t, axis=0) for t in tiles], axis=1)
-        got = dot(pick, right).astype(BF16)
-        for p in range(NP // PARTS):
-            z, x = NZ // PARTS * part + p // NX, p % NX
-            at = 8 * (NP // PARTS * part + p)
+        got = dot(picks[part], right).astype(BF16)
+        for p in range(span // 4):
+            z, x = start // 16 + p // NX, p % NX
+            at = 8 * (start // 4 + p)
             for c in range(2):
                 to = 2 * x + c
                 for q in range(5):
@@ -110,7 +112,7 @@
                 m = 8 * (16 * c + (NZ * x + z) // 2)
                 tail = steps[at : at + 8, T * c : T * c + T] + sums[m : m + 8] + flag
                 out_ref[z, to, pl.ds(80, 8), :] = tail.astype(BF16)
-        here = pl.ds(NZ // PARTS * part, NZ // PARTS)
+        here = pl.ds(start // 16, span // 16)
         sent.append(pltpu.make_async_copy(out_ref.at[here], out_hbm.at[here], out_sems.at[part]))
         sent[-1].start()
     for copy in sent:
@@ -382,8 +384,8 @@
             pltpu.VMEM(dt.shape[::-1], BF16),
             pltpu.VMEM((1, T), I32),
             pltpu.VMEM((NZ, 2 * NX, MSG, T), BF16),
-            pltpu.SemaphoreType.DMA((2 + 3 * PARTS,)),
-            pltpu.SemaphoreType.DMA((PARTS,)),
+            pltpu.SemaphoreType.DMA((2 + 3 * len(PARTS),)),
+            pltpu.SemaphoreType.DMA((len(PARTS),)),
         ],
         compiler_params=params(56),
         name="pack",

time: 91.4 us -> 91.4 us (level)
  no operation moved by 1% of the time
where the time goes in v7:
time: 91.4 us; the launch traced here: 91 us
  waiting for transfers between devices  38.9 us (43%)
  starting transfers between devices  23.7 us (26%)
  blocking collectives  15.5 us (17%)
  Pallas kernels  12.2 us (13%)
    all_to_all x1, waiting for transfers between devices, per_device(): lax.all_to_all(packed, ('z', 'x', 'c'), split_axis=0, concat_axis=0, tile...  34.4 us
    all_to_all x1, blocking collectives, per_device(): lax.all_to_all(prefixes, ('x', 'z'), split_axis=0, concat_axis=0, tiled=T...  15.5 us
    all_to_all x1, starting transfers between devices, per_device(): lax.all_to_all(packed, ('z', 'x', 'c'), split_axis=0, concat_axis=0, tile...  13.1 us
    all_to_all x1, starting transfers between devices, per_device(): lax.all_to_all(msg, ('x', 'z'), split_axis=0, concat_axis=0, tiled=True)  5.06 us
    pallas_call x1, Pallas kernels, per_device(): pl.pallas_call(local_kernel, out_shape=(sds((T, HW), F32), sds((T, T), BF...  4.94 us
    ppermute x1, starting transfers between devices, per_device(): other = lax.ppermute(states, 'c', [(0, 1), (1, 0)])  3.68 us
    all_to_all x1, waiting for transfers between devices, per_device(): lax.all_to_all(msg, ('x', 'z'), split_axis=0, concat_axis=0, tiled=True)  3.57 us
    pallas_call x1, Pallas kernels, per_device(): pl.pallas_call(pack_kernel, out_shape=sds((NZ, 2 * NX, MSG, T), BF16), in...  2.86 us
  transfers between devices with their start and end apart: 6, of which 5 were waited for; matrix products, arithmetic and copies ran while one was open for 1% of the time, Pallas kernels for 7%

profile of v7, /device:TPU:1, one launch (start us, length us, event | category | flops | bytes accessed | tf_op | source)
XLA Modules:
  0.0 91.0 jit_solution(5370527562006075493)
XLA Ops:
  0.0 2.9 %pack.1 = bf16[8,8,88,128]{3,2,1,0:T(8,128)(2,1)} custom-call(bf16[128,4096]{1,0:T(8,128)(2,1)} %x_hbm.1, bf16[128,512]{1,0:T(8,128)(2,1)} %b_hbm.1, bf16[128,512]{1,0:T(8,128)(2,1)} %c_hbm.1, bf16[64,128]{1,0:T(8,128)(2,1)} %bitcast.9, s32[1,128]{1,0:T(1,128)} %bitcast.5), custom_call_target="tpu_custom_call" | custom-call | tf_op jit(solution)/shard_map/pack/pallas_call | solution.py:375
  2.9 0.0 copy-start
  2.9 0.0 copy-start.1
  2.9 0.0 copy-start.2
  2.9 0.0 copy-start.3
  2.9 13.1 %all-to-all-start = ((bf16[64,88,128]{2,1,0:T(8,128)(2,1)}), bf16[64,88,128]{2,1,0:T(8,128)(2,1)S(1)}, u32[]{:S(2)}, u32[]{:S(2)}) async-start(bf16[64,88,128]{2,1,0:T(8,128)(2,1)} %bitcast.8), calls=%async_computation | async-start | bytes 2883584 | tf_op jit(solution)/shard_map/all_to_all | solution.py:394
  16.1 0.0 copy-done
  16.1 0.5 collective-permute-start.1
  16.6 0.0 copy-done.1
  16.6 0.1 collective-permute-start
  16.7 0.0 copy-done.2
  16.7 0.1 dynamic_slice.9
  16.8 0.1 maximum_bitcast_fusion.rate_ref
  16.9 0.1 dynamic_slice.11
  16.9 0.0 copy-done.3
  16.9 0.1 dynamic_slice.10
  17.0 0.1 broadcast_in_dim.11
  17.1 0.1 reshape_reshape.7.pair_ref
  17.2 0.1 broadcast_in_dim.10
  17.2 0.1 reshape_reshape.6.skip_ref
  17.3 0.1 collective-permute-done.1.reset2_ref
  17.4 0.3 collective-permute-done.order2_ref
  17.7 0.2 plan.1
  18.0 34.4 %all-to-all-done.arrived_ref = bf16[64,88,128]{2,1,0:T(8,128)(2,1)S(1)} async-done(((bf16[64,88,128]{2,1,0:T(8,128)(2,1)}), bf16[64,88,128]{2,1,0:T(8,128)(2,1)S(1)}, u32[]{:S(2)}, u32[]{:S(2)}) %all-to-all-start) | async-done | bytes 1441824 | tf_op jit(solution)/shard_map/all_to_all | solution.py:394
  52.4 2.3 %state.1 = (bf16[12288,2048]{1,0:T(8,128)(2,1)}, bf16[256,512]{1,0:T(8,128)(2,1)S(1)}, f32[128,128]{1,0:T(8,128)S(1)}, f32[128,128]{1,0:T(8,128)S(1)}, bf16[32,3...) custom-call(bf16[64,88,128]{2,1,0:T(8,128)(2,1)S(1)} %all-to-all-done.arrived_ref, f32[1,128]{1,0:T(1,128)S(1)} %maximum_bitcast_fusion.rate_ref, ...), custom_call_target="tpu_custom_call" | custom-call | tf_op jit(solution)/shard_map/state/pallas_call | solution.py:409
  54.7 5.1 %all-to-all-start.1 = ((bf16[32,32,128]{2,1,0:T(8,128)(2,1)}), bf16[32,32,128]{2,1,0:T(8,128)(2,1)S(1)}, u32[]{:S(2)}, u32[]{:S(2)}) async-start(bf16[32,32,128]{2,1,0:T(8,128)(2,1)} %get-tuple-element.30), calls=%async_computation.1 | async-start | bytes 524288 | tf_op jit(solution)/shard_map/all_to_all | solution.py:429
  59.8 4.9 %local.1 = (f32[128,2048]{1,0:T(8,128)S(1)}, bf16[128,128]{1,0:T(8,128)(2,1)S(1)}, bf16[128,4480]{1,0:T(8,128)(2,1)}, f32[32,128]{1,0:T(8,128)S(1)}) custom-call(bf16[12288,2048]{1,0:T(8,128)(2,1)} %get-tuple-element.23.x_hbm, bf16[256,512]{1,0:T(8,128)(2,1)S(1)} %get-tuple-element.24.bc_ref, f32[128,128]{1,0:T(8,128)S(1)} %get-tuple-element.25.cum_ref, ...), custom_call_target="tpu_custom_call" | custom-call | flops 2000000000 | bytes 6000000 | tf_op jit(solution)/shard_map/local/pallas_call | solution.py:430
  64.8 1.2 %collective-permute-start.2 = (bf16[128,4480]{1,0:T(8,128)(2,1)}, bf16[128,4480]{1,0:T(8,128)(2,1)S(1)}, u32[]{:S(2)}, u32[]{:S(2)}) collective-permute-start(bf16[128,4480]{1,0:T(8,128)(2,1)} %get-tuple-element.32), channel_id=1, source_target_pairs={{0,4},{4,0},{1,5},{5,1},{2,6},{6,2},{3,7},{7,3},{8,12},{12,8},{9,1... | collective-permute-start | bytes 3440648 | tf_op jit(solution)/shard_map/ppermute | solution.py:444
  65.9 3.6 %all-to-all-done.1.in_ref = bf16[32,32,128]{2,1,0:T(8,128)(2,1)S(1)} async-done(((bf16[32,32,128]{2,1,0:T(8,128)(2,1)}), bf16[32,32,128]{2,1,0:T(8,128)(2,1)S(1)}, u32[]{:S(2)}, u32[]{:S(2)}) %all-to-all-start.1) | async-done | bytes 262176 | tf_op jit(solution)/shard_map/all_to_all | solution.py:429
  69.5 0.1 chips.1
  69.5 15.5 %all_to_all.15.h_ref = bf16[32,32,128]{2,1,0:T(8,128)(2,1)S(1)} all-to-all(bf16[32,32,128]{2,1,0:T(8,128)(2,1)S(1)} %chips.1), channel_id=1, replica_groups=mesh['z'=8,'x'=4,'c'=2,'seq'=4] {'x','z'}, dimensions={0} | all-to-all | bytes 524288 | tf_op jit(solution)/shard_map/all_to_all | solution.py:448
  85.1 3.7 %collective-permute-start.3 = (bf16[32,32,128]{2,1,0:T(8,128)(2,1)S(1)}, bf16[32,32,128]{2,1,0:T(8,128)(2,1)S(1)}, u32[]{:S(2)}, u32[]{:S(2)}) collective-permute-start(bf16[32,32,128]{2,1,0:T(8,128)(2,1)S(1)} %all_to_all.15.h_ref), channel_id=1, source_target_pairs={{0,4},{4,0},{1,5},{5,1},{2,6},{6,2},{3,7},{7,3},{8,12},{12,8},{9,1... | collective-permute-start | bytes 786440 | tf_op jit(solution)/shard_map/ppermute | solution.py:449
  88.8 0.0 collective-permute-done.2.swap_ref
  88.8 0.7 mine.1
  89.4 0.5 collective-permute-done.3.h_ref
  89.9 1.1 %final.1 = bf16[128,4096]{1,0:T(8,128)(2,1)} custom-call(bf16[128,2048]{1,0:T(8,128)(2,1)S(1)} %get-tuple-element.33.mine_ref, f32[128,2048]{1,0:T(8,128)S(1)} %get-tuple-element.34.scale_ref, f32[128,2048]{1,0:T(8,128)S(1)} %get-tuple-element.35.partial_ref, bf16[128,256]{1,0:T(8,128)(2,1)S(1)} %get-tuple-element.36.c_ref, ...), custom_call_target="tpu_custom_call" | custom-call | tf_op jit(solution)/shard_map/final/pallas_call | solution.py:456
  (1 shorter events, 0.0 us)
Async XLA Ops:
  2.9 13.2 %copy-start = (s32[128]{0:T(128)S(1)}, s32[128]{0:T(128)}, u32[]{:S(2)}) copy-start(s32[128]{0:T(128)} %param.13) | copy-start | bytes 1540
  2.9 13.7 %copy-start.1 = (s32[1,128]{1,0:T(1,128)S(1)}, s32[1,128]{1,0:T(1,128)}, u32[]{:S(2)}) copy-start(s32[1,128]{1,0:T(1,128)} %order_ref.1) | copy-start | bytes 1540
  2.9 13.8 %copy-start.2 = (f32[64]{0:T(128)S(1)}, f32[64]{0:T(128)}, u32[]{:S(2)}) copy-start(f32[64]{0:T(128)} %param.14) | copy-start | bytes 772
  2.9 14.0 %copy-start.3 = (f32[64]{0:T(128)S(1)}, f32[64]{0:T(128)}, u32[]{:S(2)}) copy-start(f32[64]{0:T(128)} %param.15) | copy-start | bytes 772
  2.9 49.5 %all-to-all-start = ((bf16[64,88,128]{2,1,0:T(8,128)(2,1)}), bf16[64,88,128]{2,1,0:T(8,128)(2,1)S(1)}, u32[]{:S(2)}, u32[]{:S(2)}) async-start(bf16[64,88,128]{2,1,0:T(8,128)(2,1)} %bitcast.8), calls=%async_computation | async-start | bytes 2883584 | tf_op jit(solution)/shard_map/all_to_all | solution.py:394
  16.1 1.4 %collective-permute-start.1 = (s32[1,128]{1,0:T(1,128)S(1)}, s32[1,128]{1,0:T(1,128)S(1)}, u32[]{:S(2)}, u32[]{:S(2)}) collective-permute-start(s32[1,128]{1,0:T(1,128)S(1)} %bitcast.6), channel_id=1, source_target_pairs={{0,4},{4,0},{1,5},{5,1},{2,6},{6,2},{3,7},{7,3},{8,12},{12,8},{9,1... | collective-permute-start | bytes 1544 | tf_op jit(solution)/shard_map/ppermute | solution.py:396
  16.6 1.1 %collective-permute-start = (s32[1,128]{1,0:T(1,128)S(1)}, s32[1,128]{1,0:T(1,128)S(1)}, u32[]{:S(2)}, u32[]{:S(2)}) collective-permute-start(s32[1,128]{1,0:T(1,128)S(1)} %copy-done.1), channel_id=1, source_target_pairs={{0,4},{4,0},{1,5},{5,1},{2,6},{6,2},{3,7},{7,3},{8,12},{12,8},{9,1... | collective-permute-start | bytes 1544 | tf_op jit(solution)/shard_map/ppermute | solution.py:395
  54.7 14.7 %all-to-all-start.1 = ((bf16[32,32,128]{2,1,0:T(8,128)(2,1)}), bf16[32,32,128]{2,1,0:T(8,128)(2,1)S(1)}, u32[]{:S(2)}, u32[]{:S(2)}) async-start(bf16[32,32,128]{2,1,0:T(8,128)(2,1)} %get-tuple-element.30), calls=%async_computation.1 | async-start | bytes 524288 | tf_op jit(solution)/shard_map/all_to_all | solution.py:429
  64.8 24.0 %collective-permute-start.2 = (bf16[128,4480]{1,0:T(8,128)(2,1)}, bf16[128,4480]{1,0:T(8,128)(2,1)S(1)}, u32[]{:S(2)}, u32[]{:S(2)}) collective-permute-start(bf16[128,4480]{1,0:T(8,128)(2,1)} %get-tuple-element.32), channel_id=1, source_target_pairs={{0,4},{4,0},{1,5},{5,1},{2,6},{6,2},{3,7},{7,3},{8,12},{12,8},{9,1... | collective-permute-start | bytes 3440648 | tf_op jit(solution)/shard_map/ppermute | solution.py:444
  85.1 4.8 %collective-permute-start.3 = (bf16[32,32,128]{2,1,0:T(8,128)(2,1)S(1)}, bf16[32,32,128]{2,1,0:T(8,128)(2,1)S(1)}, u32[]{:S(2)}, u32[]{:S(2)}) collective-permute-start(bf16[32,32,128]{2,1,0:T(8,128)(2,1)S(1)} %all_to_all.15.h_ref), channel_id=1, source_target_pairs={{0,4},{4,0},{1,5},{5,1},{2,6},{6,2},{3,7},{7,3},{8,12},{12,8},{9,1... | collective-permute-start | bytes 786440 | tf_op jit(solution)/shard_map/ppermute | solution.py:449

commit v8 on v7

--- a/solution.py
+++ b/solution.py
@@ -18,7 +18,7 @@
 HH = 32
 HW = HH * HP
 MSG = 88
-PARTS = (64, 48, 16)
+PARTS = (48, 64, 16)
 AWAY = 12288
 
 

time: 91.4 us -> 91.4 us (level)
  transfers between devices with their start and end apart: 6 -> 6, of which waited for: 5 -> 5; matrix products, arithmetic and copies ran while one was open for 1% -> 1% of each run, Pallas kernels for 7% -> 6%
where the time goes in v8:
time: 91.4 us; the launch traced here: 91.1 us
  waiting for transfers between devices  38.9 us (43%)
  starting transfers between devices  23.7 us (26%)
  blocking collectives  15.5 us (17%)
  Pallas kernels  12.2 us (13%)
    all_to_all x1, waiting for transfers between devices, per_device(): lax.all_to_all(packed, ('z', 'x', 'c'), split_axis=0, concat_axis=0, tile...  34.4 us
    all_to_all x1, blocking collectives, per_device(): lax.all_to_all(prefixes, ('x', 'z'), split_axis=0, concat_axis=0, tiled=T...  15.5 us
    all_to_all x1, starting transfers between devices, per_device(): lax.all_to_all(packed, ('z', 'x', 'c'), split_axis=0, concat_axis=0, tile...  13.1 us
    all_to_all x1, starting transfers between devices, per_device(): lax.all_to_all(msg, ('x', 'z'), split_axis=0, concat_axis=0, tiled=True)  5.06 us
    pallas_call x1, Pallas kernels, per_device(): pl.pallas_call(local_kernel, out_shape=(sds((T, HW), F32), sds((T, T), BF...  4.94 us
    ppermute x1, starting transfers between devices, per_device(): other = lax.ppermute(states, 'c', [(0, 1), (1, 0)])  3.68 us
    all_to_all x1, waiting for transfers between devices, per_device(): lax.all_to_all(msg, ('x', 'z'), split_axis=0, concat_axis=0, tiled=True)  3.57 us
    pallas_call x1, Pallas kernels, per_device(): pl.pallas_call(pack_kernel, out_shape=sds((NZ, 2 * NX, MSG, T), BF16), in...  2.91 us
  transfers between devices with their start and end apart: 6, of which 5 were waited for; matrix products, arithmetic and copies ran while one was open for 1% of the time, Pallas kernels for 6%

profile of v8, /device:TPU:1, one launch (start us, length us, event | category | flops | bytes accessed | tf_op | source)
XLA Modules:
  0.0 91.1 jit_solution(12073837734467378589)
XLA Ops:
  0.0 2.9 %pack.1 = bf16[8,8,88,128]{3,2,1,0:T(8,128)(2,1)} custom-call(bf16[128,4096]{1,0:T(8,128)(2,1)} %x_hbm.1, bf16[128,512]{1,0:T(8,128)(2,1)} %b_hbm.1, bf16[128,512]{1,0:T(8,128)(2,1)} %c_hbm.1, bf16[64,128]{1,0:T(8,128)(2,1)} %bitcast.9, s32[1,128]{1,0:T(1,128)} %bitcast.5), custom_call_target="tpu_custom_call" | custom-call | tf_op jit(solution)/shard_map/pack/pallas_call | solution.py:375
  2.9 0.0 copy-start
  2.9 0.0 copy-start.1
  2.9 0.0 copy-start.2
  3.0 0.0 copy-start.3
  3.0 13.1 %all-to-all-start = ((bf16[64,88,128]{2,1,0:T(8,128)(2,1)}), bf16[64,88,128]{2,1,0:T(8,128)(2,1)S(1)}, u32[]{:S(2)}, u32[]{:S(2)}) async-start(bf16[64,88,128]{2,1,0:T(8,128)(2,1)} %bitcast.8), calls=%async_computation | async-start | bytes 2883584 | tf_op jit(solution)/shard_map/all_to_all | solution.py:394
  16.1 0.0 copy-done
  16.1 0.5 collective-permute-start.1
  16.7 0.0 copy-done.1
  16.7 0.1 collective-permute-start
  16.8 0.0 copy-done.2
  16.8 0.1 dynamic_slice.9
  16.9 0.1 maximum_bitcast_fusion.rate_ref
  16.9 0.1 dynamic_slice.11
  17.0 0.0 copy-done.3
  17.0 0.1 dynamic_slice.10
  17.1 0.1 broadcast_in_dim.11
  17.2 0.1 reshape_reshape.7.pair_ref
  17.2 0.1 broadcast_in_dim.10
  17.3 0.1 reshape_reshape.6.skip_ref
  17.4 0.1 collective-permute-done.1.reset2_ref
  17.5 0.3 collective-permute-done.order2_ref
  17.8 0.2 plan.1
  18.0 34.4 %all-to-all-done.arrived_ref = bf16[64,88,128]{2,1,0:T(8,128)(2,1)S(1)} async-done(((bf16[64,88,128]{2,1,0:T(8,128)(2,1)}), bf16[64,88,128]{2,1,0:T(8,128)(2,1)S(1)}, u32[]{:S(2)}, u32[]{:S(2)}) %all-to-all-start) | async-done | bytes 1441824 | tf_op jit(solution)/shard_map/all_to_all | solution.py:394
  52.5 2.3 %state.1 = (bf16[12288,2048]{1,0:T(8,128)(2,1)}, bf16[256,512]{1,0:T(8,128)(2,1)S(1)}, f32[128,128]{1,0:T(8,128)S(1)}, f32[128,128]{1,0:T(8,128)S(1)}, bf16[32,3...) custom-call(bf16[64,88,128]{2,1,0:T(8,128)(2,1)S(1)} %all-to-all-done.arrived_ref, f32[1,128]{1,0:T(1,128)S(1)} %maximum_bitcast_fusion.rate_ref, ...), custom_call_target="tpu_custom_call" | custom-call | tf_op jit(solution)/shard_map/state/pallas_call | solution.py:409
  54.8 5.1 %all-to-all-start.1 = ((bf16[32,32,128]{2,1,0:T(8,128)(2,1)}), bf16[32,32,128]{2,1,0:T(8,128)(2,1)S(1)}, u32[]{:S(2)}, u32[]{:S(2)}) async-start(bf16[32,32,128]{2,1,0:T(8,128)(2,1)} %get-tuple-element.30), calls=%async_computation.1 | async-start | bytes 524288 | tf_op jit(solution)/shard_map/all_to_all | solution.py:429
  59.9 4.9 %local.1 = (f32[128,2048]{1,0:T(8,128)S(1)}, bf16[128,128]{1,0:T(8,128)(2,1)S(1)}, bf16[128,4480]{1,0:T(8,128)(2,1)}, f32[32,128]{1,0:T(8,128)S(1)}) custom-call(bf16[12288,2048]{1,0:T(8,128)(2,1)} %get-tuple-element.23.x_hbm, bf16[256,512]{1,0:T(8,128)(2,1)S(1)} %get-tuple-element.24.bc_ref, f32[128,128]{1,0:T(8,128)S(1)} %get-tuple-element.25.cum_ref, ...), custom_call_target="tpu_custom_call" | custom-call | flops 2000000000 | bytes 6000000 | tf_op jit(solution)/shard_map/local/pallas_call | solution.py:430
  64.8 1.2 %collective-permute-start.2 = (bf16[128,4480]{1,0:T(8,128)(2,1)}, bf16[128,4480]{1,0:T(8,128)(2,1)S(1)}, u32[]{:S(2)}, u32[]{:S(2)}) collective-permute-start(bf16[128,4480]{1,0:T(8,128)(2,1)} %get-tuple-element.32), channel_id=1, source_target_pairs={{0,4},{4,0},{1,5},{5,1},{2,6},{6,2},{3,7},{7,3},{8,12},{12,8},{9,1... | collective-permute-start | bytes 3440648 | tf_op jit(solution)/shard_map/ppermute | solution.py:444
  66.0 3.6 %all-to-all-done.1.in_ref = bf16[32,32,128]{2,1,0:T(8,128)(2,1)S(1)} async-done(((bf16[32,32,128]{2,1,0:T(8,128)(2,1)}), bf16[32,32,128]{2,1,0:T(8,128)(2,1)S(1)}, u32[]{:S(2)}, u32[]{:S(2)}) %all-to-all-start.1) | async-done | bytes 262176 | tf_op jit(solution)/shard_map/all_to_all | solution.py:429
  69.5 0.1 chips.1
  69.6 15.5 %all_to_all.15.h_ref = bf16[32,32,128]{2,1,0:T(8,128)(2,1)S(1)} all-to-all(bf16[32,32,128]{2,1,0:T(8,128)(2,1)S(1)} %chips.1), channel_id=1, replica_groups=mesh['z'=8,'x'=4,'c'=2,'seq'=4] {'x','z'}, dimensions={0} | all-to-all | bytes 524288 | tf_op jit(solution)/shard_map/all_to_all | solution.py:448
  85.1 3.7 %collective-permute-start.3 = (bf16[32,32,128]{2,1,0:T(8,128)(2,1)S(1)}, bf16[32,32,128]{2,1,0:T(8,128)(2,1)S(1)}, u32[]{:S(2)}, u32[]{:S(2)}) collective-permute-start(bf16[32,32,128]{2,1,0:T(8,128)(2,1)S(1)} %all_to_all.15.h_ref), channel_id=1, source_target_pairs={{0,4},{4,0},{1,5},{5,1},{2,6},{6,2},{3,7},{7,3},{8,12},{12,8},{9,1... | collective-permute-start | bytes 786440 | tf_op jit(solution)/shard_map/ppermute | solution.py:449
  88.8 0.0 collective-permute-done.2.swap_ref
  88.8 0.7 mine.1
  89.5 0.5 collective-permute-done.3.h_ref
  90.0 1.1 %final.1 = bf16[128,4096]{1,0:T(8,128)(2,1)} custom-call(bf16[128,2048]{1,0:T(8,128)(2,1)S(1)} %get-tuple-element.33.mine_ref, f32[128,2048]{1,0:T(8,128)S(1)} %get-tuple-element.34.scale_ref, f32[128,2048]{1,0:T(8,128)S(1)} %get-tuple-element.35.partial_ref, bf16[128,256]{1,0:T(8,128)(2,1)S(1)} %get-tuple-element.36.c_ref, ...), custom_call_target="tpu_custom_call" | custom-call | tf_op jit(solution)/shard_map/final/pallas_call | solution.py:456
  (1 shorter events, 0.0 us)
Async XLA Ops:
  2.9 13.2 %copy-start = (s32[128]{0:T(128)S(1)}, s32[128]{0:T(128)}, u32[]{:S(2)}) copy-start(s32[128]{0:T(128)} %param.13) | copy-start | bytes 1540
  2.9 13.7 %copy-start.1 = (s32[1,128]{1,0:T(1,128)S(1)}, s32[1,128]{1,0:T(1,128)}, u32[]{:S(2)}) copy-start(s32[1,128]{1,0:T(1,128)} %order_ref.1) | copy-start | bytes 1540
  2.9 13.8 %copy-start.2 = (f32[64]{0:T(128)S(1)}, f32[64]{0:T(128)}, u32[]{:S(2)}) copy-start(f32[64]{0:T(128)} %param.14) | copy-start | bytes 772
  3.0 14.1 %copy-start.3 = (f32[64]{0:T(128)S(1)}, f32[64]{0:T(128)}, u32[]{:S(2)}) copy-start(f32[64]{0:T(128)} %param.15) | copy-start | bytes 772
  3.0 49.5 %all-to-all-start = ((bf16[64,88,128]{2,1,0:T(8,128)(2,1)}), bf16[64,88,128]{2,1,0:T(8,128)(2,1)S(1)}, u32[]{:S(2)}, u32[]{:S(2)}) async-start(bf16[64,88,128]{2,1,0:T(8,128)(2,1)} %bitcast.8), calls=%async_computation | async-start | bytes 2883584 | tf_op jit(solution)/shard_map/all_to_all | solution.py:394
  16.1 1.4 %collective-permute-start.1 = (s32[1,128]{1,0:T(1,128)S(1)}, s32[1,128]{1,0:T(1,128)S(1)}, u32[]{:S(2)}, u32[]{:S(2)}) collective-permute-start(s32[1,128]{1,0:T(1,128)S(1)} %bitcast.6), channel_id=1, source_target_pairs={{0,4},{4,0},{1,5},{5,1},{2,6},{6,2},{3,7},{7,3},{8,12},{12,8},{9,1... | collective-permute-start | bytes 1544 | tf_op jit(solution)/shard_map/ppermute | solution.py:396
  16.7 1.1 %collective-permute-start = (s32[1,128]{1,0:T(1,128)S(1)}, s32[1,128]{1,0:T(1,128)S(1)}, u32[]{:S(2)}, u32[]{:S(2)}) collective-permute-start(s32[1,128]{1,0:T(1,128)S(1)} %copy-done.1), channel_id=1, source_target_pairs={{0,4},{4,0},{1,5},{5,1},{2,6},{6,2},{3,7},{7,3},{8,12},{12,8},{9,1... | collective-permute-start | bytes 1544 | tf_op jit(solution)/shard_map/ppermute | solution.py:395
  54.8 14.7 %all-to-all-start.1 = ((bf16[32,32,128]{2,1,0:T(8,128)(2,1)}), bf16[32,32,128]{2,1,0:T(8,128)(2,1)S(1)}, u32[]{:S(2)}, u32[]{:S(2)}) async-start(bf16[32,32,128]{2,1,0:T(8,128)(2,1)} %get-tuple-element.30), calls=%async_computation.1 | async-start | bytes 524288 | tf_op jit(solution)/shard_map/all_to_all | solution.py:429
  64.8 24.0 %collective-permute-start.2 = (bf16[128,4480]{1,0:T(8,128)(2,1)}, bf16[128,4480]{1,0:T(8,128)(2,1)S(1)}, u32[]{:S(2)}, u32[]{:S(2)}) collective-permute-start(bf16[128,4480]{1,0:T(8,128)(2,1)} %get-tuple-element.32), channel_id=1, source_target_pairs={{0,4},{4,0},{1,5},{5,1},{2,6},{6,2},{3,7},{7,3},{8,12},{12,8},{9,1... | collective-permute-start | bytes 3440648 | tf_op jit(solution)/shard_map/ppermute | solution.py:444
  85.1 4.8 %collective-permute-start.3 = (bf16[32,32,128]{2,1,0:T(8,128)(2,1)S(1)}, bf16[32,32,128]{2,1,0:T(8,128)(2,1)S(1)}, u32[]{:S(2)}, u32[]{:S(2)}) collective-permute-start(bf16[32,32,128]{2,1,0:T(8,128)(2,1)S(1)} %all_to_all.15.h_ref), channel_id=1, source_target_pairs={{0,4},{4,0},{1,5},{5,1},{2,6},{6,2},{3,7},{7,3},{8,12},{12,8},{9,1... | collective-permute-start | bytes 786440 | tf_op jit(solution)/shard_map/ppermute | solution.py:449
